TPU v7x, 32 devices: a whole 2x2x4 slice. The times are simulated.
32 devices in a mesh: dp: 16 (over z, y, x), tensor: 2 (over core).
Axes of the slice: x: 2, y: 2, z: 4, core: 2. Of those that a mesh axis runs over, the one named last changes fastest.
Arguments:
- tokens: bfloat16 [32768, 1280], P(('dp', 'tensor')), may hold values from -6 to 6
- cotangent: bfloat16 [32768, 1280], P(('dp', 'tensor')), may hold values from -6 to 6
- picture_ids: int32 [32768], P('dp'), may hold values from 0 to 3, as said below
- positions: int32 [2, 32768], P(None, 'dp'), may hold values from 0 to 383, as said below
- valid: int32 [32768], P('dp'), may hold values from 0 to 1, as said below
- norm1_gain: bfloat16 [1280], replicated, may hold values from 0.099609375 to 1.8984375
- norm1_bias: bfloat16 [1280], replicated, may hold values from -3 to 3
- qkv_weight: bfloat16 [1280, 3, 1280], P('dp', None, 'tensor'), may hold values from -0.15625 to 0.15625
- qkv_bias: bfloat16 [3, 1280], replicated, may hold values from -3 to 3
- proj_weight: bfloat16 [1280, 1280], P('tensor', 'dp'), may hold values from -1 to 1
- proj_bias: bfloat16 [1280], replicated, may hold values from -3 to 3
- norm2_gain: bfloat16 [1280], replicated, may hold values from 0.099609375 to 1.8984375
- norm2_bias: bfloat16 [1280], replicated, may hold values from -3 to 3
- fc1_weight: bfloat16 [1280, 5120], P('dp', 'tensor'), may hold values from -0.15625 to 0.15625
- fc1_bias: bfloat16 [5120], replicated, may hold values from -3 to 3
- fc2_weight: bfloat16 [5120, 1280], P('tensor', 'dp'), may hold values from -0.078125 to 0.078125
- fc2_bias: bfloat16 [1280], replicated, may hold values from -3 to 3
Outputs:
- output: float32 [32768, 1280], P(('dp', 'tensor'))
- input_grad: float32 [32768, 1280], P(('dp', 'tensor'))
- norm1_gain_grad: float32 [1280], replicated
- norm1_bias_grad: float32 [1280], replicated
- qkv_weight_grad: float32 [1280, 3, 1280], P('dp', None, 'tensor')
- qkv_bias_grad: float32 [3, 1280], replicated
- proj_weight_grad: float32 [1280, 1280], P('tensor', 'dp')
- proj_bias_grad: float32 [1280], replicated
- norm2_gain_grad: float32 [1280], replicated
- norm2_bias_grad: float32 [1280], replicated
- fc1_weight_grad: float32 [1280, 5120], P('dp', 'tensor')
- fc1_bias_grad: float32 [5120], replicated
- fc2_weight_grad: float32 [5120, 1280], P('tensor', 'dp')
- fc2_bias_grad: float32 [1280], replicated
Inputs may be any that keep to these rules, and one draw needn't show every extreme that they name: `picture_ids`: each row of 2048 patches holds four pictures in order, ids 0 to 3 never falling; the first picture has 1024 to 1536 patches, every picture at least one valid patch; padding patches come at a row's end and carry id 3. A picture's patches run row by row over a grid of 4 to 32 columns; padding patches have positions 0. In each row the valid patches come first; up to 256 padding patches follow, exactly 256 in the first row.
All inputs are finite; a program needn't handle non-finite values.
Results may differ from a plain program's by a relative error of at most 0.023.
Values may be sent and summed in bfloat16 or wider, within the bound.
No kernel may reach another device: no remote copies, remote signals or barrier semaphores. Data moves between devices by JAX's collectives and lax.ppermute only.
A program may use at most 384 MiB of HBM per device.

v0:
```python
import jax
import jax.numpy as jnp
from jax import lax
from jax.sharding import PartitionSpec as P

HEAD_DIM = 80


EPS = 1e-06


def norm_forward(values, gain, shift):
    center = values - jnp.mean(values, axis=-1, keepdims=True)
    inverse = lax.rsqrt(jnp.mean(center * center, axis=-1, keepdims=True) + EPS)
    unit = center * inverse
    return (unit * gain + shift, unit, inverse)


def norm_backward(grad_out, unit, inverse, gain):
    scaled = grad_out * gain
    grad_in = inverse * (
        scaled
        - jnp.mean(scaled, axis=-1, keepdims=True)
        - unit * jnp.mean(scaled * unit, axis=-1, keepdims=True)
    )
    return (grad_in, jnp.sum(grad_out * unit, axis=0), jnp.sum(grad_out, axis=0))


def rope_tables(place):
    quarter = HEAD_DIM // 4
    freqs = 10000.0 ** (-2.0 * jnp.arange(quarter, dtype=jnp.float32) / (HEAD_DIM // 2))
    along_rows = place[0].astype(jnp.float32)[:, None] * freqs[None, :]
    along_cols = place[1].astype(jnp.float32)[:, None] * freqs[None, :]
    theta = jnp.concatenate([along_rows, along_cols, along_rows, along_cols], axis=1)
    return (jnp.cos(theta)[:, None, :], jnp.sin(theta)[:, None, :])


def rotate(values, cosine, sine):
    half = values.shape[-1] // 2
    turned = jnp.concatenate([-values[..., half:], values[..., :half]], axis=-1)
    return values * cosine + turned * sine


def rotate_back(grads, cosine, sine):
    half = grads.shape[-1] // 2
    weighted = grads * sine
    turned = jnp.concatenate([weighted[..., half:], -weighted[..., :half]], axis=-1)
    return grads * cosine + turned


def block_scores(query_block, keys, id_block, picture, live):
    scale = HEAD_DIM ** (-0.5)
    scores = (
        jnp.einsum("qhd,khd->hqk", query_block, keys, preferred_element_type=jnp.float32) * scale
    )
    allowed = (id_block[:, None] == picture[None, :]) & (live[None, :] > 0)
    return jnp.where(allowed[None], scores, -1e30)


def attend_row(queries, keys, values, picture, live):
    length = queries.shape[0]
    block = min(512, length)

    def one_block(index):
        query_block = lax.dynamic_slice_in_dim(queries, index * block, block, 0)
        id_block = lax.dynamic_slice_in_dim(picture, index * block, block, 0)
        scores = block_scores(query_block, keys, id_block, picture, live)
        peak = jnp.max(scores, axis=-1, keepdims=True)
        shifted = jnp.exp(scores - peak)
        total = jnp.sum(shifted, axis=-1, keepdims=True)
        probs = (shifted / total).astype(jnp.bfloat16)
        mixed = jnp.einsum("hqk,khd->qhd", probs, values, preferred_element_type=jnp.float32)
        return (mixed.astype(jnp.bfloat16), (peak + jnp.log(total))[..., 0])

    mixed, logsum = lax.map(one_block, jnp.arange(length // block))
    return (mixed.reshape(length, queries.shape[1], queries.shape[2]), logsum)


def attend_back(queries, keys, values, picture, live, mixed_grad, logsum):
    length = queries.shape[0]
    block = min(512, length)
    scale = HEAD_DIM ** (-0.5)

    def one_block(carry, index):
        key_grad, value_grad = carry
        query_block = lax.dynamic_slice_in_dim(queries, index * block, block, 0)
        id_block = lax.dynamic_slice_in_dim(picture, index * block, block, 0)
        grad_block = lax.dynamic_slice_in_dim(mixed_grad, index * block, block, 0)
        scores = block_scores(query_block, keys, id_block, picture, live)
        probs = jnp.exp(scores - logsum[index][..., None])
        prob_grad = jnp.einsum(
            "qhd,khd->hqk", grad_block, values, preferred_element_type=jnp.float32
        )
        center = jnp.sum(probs * prob_grad, axis=-1, keepdims=True)
        score_grad = (probs * (prob_grad - center)).astype(jnp.bfloat16)
        query_grad = (
            jnp.einsum("hqk,khd->qhd", score_grad, keys, preferred_element_type=jnp.float32) * scale
        )
        key_grad = (
            key_grad
            + jnp.einsum(
                "hqk,qhd->khd", score_grad, query_block, preferred_element_type=jnp.float32
            )
            * scale
        )
        value_grad = value_grad + jnp.einsum(
            "hqk,qhd->khd",
            probs.astype(jnp.bfloat16),
            grad_block,
            preferred_element_type=jnp.float32,
        )
        return ((key_grad, value_grad), query_grad)

    zeros = jnp.zeros(keys.shape, jnp.float32)
    (key_grad, value_grad), query_grads = lax.scan(
        one_block, (zeros, zeros), jnp.arange(length // block)
    )
    return (query_grads.reshape(queries.shape), key_grad, value_grad)


def on_device(
    tokens,
    cotangent,
    picture_ids,
    positions,
    valid,
    norm1_gain,
    norm1_bias,
    qkv_weight,
    qkv_bias,
    proj_weight,
    proj_bias,
    norm2_gain,
    norm2_bias,
    fc1_weight,
    fc1_bias,
    fc2_weight,
    fc2_bias,
):
    tensor_index = lax.axis_index("tensor")
    model_width = tokens.shape[1]
    local_width = qkv_weight.shape[2]
    local_hidden = fc1_weight.shape[1]
    local_heads = local_width // HEAD_DIM
    gain_one = norm1_gain.astype(jnp.float32)
    shift_one = norm1_bias.astype(jnp.float32)
    gain_two = norm2_gain.astype(jnp.float32)
    shift_two = norm2_bias.astype(jnp.float32)
    qkv_shift = lax.dynamic_slice_in_dim(
        qkv_bias.astype(jnp.float32), tensor_index * local_width, local_width, 1
    ).reshape(3 * local_width)
    fc1_shift = lax.dynamic_slice_in_dim(
        fc1_bias.astype(jnp.float32), tensor_index * local_hidden, local_hidden, 0
    )
    qkv_full, proj_full, fc1_full, fc2_full = (
        lax.all_gather(qkv_weight, "dp", axis=0, tiled=True),
        lax.all_gather(proj_weight, "dp", axis=1, tiled=True),
        lax.all_gather(fc1_weight, "dp", axis=0, tiled=True),
        lax.all_gather(fc2_weight, "dp", axis=1, tiled=True),
    )
    qkv_matrix = qkv_full.reshape(model_width, 3 * local_width)
    inputs = tokens.astype(jnp.float32)
    normed_one, unit_one, inverse_one = norm_forward(inputs, gain_one, shift_one)
    attn_in = lax.all_gather(normed_one.astype(jnp.bfloat16), "tensor", axis=0, tiled=True)
    total_rows = attn_in.shape[0]
    qkv_raw = jnp.dot(attn_in, qkv_matrix, preferred_element_type=jnp.float32) + qkv_shift
    split = qkv_raw.reshape(total_rows, 3, local_heads, HEAD_DIM)
    cosine, sine = rope_tables(positions)
    queries = rotate(split[:, 0], cosine, sine).astype(jnp.bfloat16)
    keys = rotate(split[:, 1], cosine, sine).astype(jnp.bfloat16)
    values = split[:, 2].astype(jnp.bfloat16)
    mixed_row, logsum_row = attend_row(queries, keys, values, picture_ids, valid)
    attn_mixed = mixed_row.reshape(total_rows, local_width)
    piece = attn_mixed
    attn_out = lax.psum_scatter(
        jnp.dot(piece, proj_full, preferred_element_type=jnp.float32).astype(jnp.bfloat16),
        "tensor",
        scatter_dimension=0,
        tiled=True,
    ).astype(jnp.float32) + proj_bias.astype(jnp.float32)
    middle = inputs + attn_out
    normed_two, unit_two, inverse_two = norm_forward(middle, gain_two, shift_two)
    mlp_in = lax.all_gather(normed_two.astype(jnp.bfloat16), "tensor", axis=0, tiled=True)
    hidden_pre = jnp.dot(mlp_in, fc1_full, preferred_element_type=jnp.float32) + fc1_shift
    sigmoid_gate = jax.nn.sigmoid(1.702 * hidden_pre)
    hidden = (hidden_pre * sigmoid_gate).astype(jnp.bfloat16)
    piece = hidden
    mlp_out = lax.psum_scatter(
        jnp.dot(piece, fc2_full, preferred_element_type=jnp.float32).astype(jnp.bfloat16),
        "tensor",
        scatter_dimension=0,
        tiled=True,
    ).astype(jnp.float32) + fc2_bias.astype(jnp.float32)
    output = middle + mlp_out
    qkv_back, proj_back, fc1_back, fc2_back = (
        lax.all_gather(qkv_weight, "dp", axis=0, tiled=True),
        lax.all_gather(proj_weight, "dp", axis=1, tiled=True),
        lax.all_gather(fc1_weight, "dp", axis=0, tiled=True),
        lax.all_gather(fc2_weight, "dp", axis=1, tiled=True),
    )
    qkv_back = qkv_back.reshape(model_width, 3 * local_width)
    out_grad = cotangent.astype(jnp.float32)
    fc2_shift_grad = jnp.sum(out_grad, axis=0)
    out_grad_full = lax.all_gather(cotangent, "tensor", axis=0, tiled=True)
    fc2_grad = jnp.dot(hidden.T, out_grad_full, preferred_element_type=jnp.float32)
    hidden_grad = jnp.dot(out_grad_full, fc2_back.T, preferred_element_type=jnp.float32)
    slope = sigmoid_gate + 1.702 * hidden_pre * sigmoid_gate * (1.0 - sigmoid_gate)
    pre_grad = (hidden_grad * slope).astype(jnp.bfloat16)
    fc1_shift_grad = jnp.sum(pre_grad.astype(jnp.float32), axis=0)
    fc1_grad = jnp.dot(mlp_in.T, pre_grad, preferred_element_type=jnp.float32)
    piece = pre_grad
    normed_two_grad = lax.psum_scatter(
        jnp.dot(piece, fc1_back.T, preferred_element_type=jnp.float32).astype(jnp.bfloat16),
        "tensor",
        scatter_dimension=0,
        tiled=True,
    ).astype(jnp.float32)
    middle_part, gain_two_grad, shift_two_grad = norm_backward(
        normed_two_grad, unit_two, inverse_two, gain_two
    )
    middle_grad = out_grad + middle_part
    attn_grad_low = middle_grad.astype(jnp.bfloat16)
    proj_shift_grad = jnp.sum(attn_grad_low.astype(jnp.float32), axis=0)
    attn_grad_full = lax.all_gather(attn_grad_low, "tensor", axis=0, tiled=True)
    proj_grad = jnp.dot(attn_mixed.T, attn_grad_full, preferred_element_type=jnp.float32)
    mixed_grad = jnp.dot(attn_grad_full, proj_back.T, preferred_element_type=jnp.float32).astype(
        jnp.bfloat16
    )
    mixed_grad = mixed_grad.reshape(total_rows, local_heads, HEAD_DIM)
    query_grad, key_grad, value_grad = attend_back(
        queries, keys, values, picture_ids, valid, mixed_grad, logsum_row
    )
    query_pre = rotate_back(query_grad, cosine, sine)
    key_pre = rotate_back(key_grad, cosine, sine)
    qkv_grad = jnp.stack([query_pre, key_pre, value_grad], axis=1).reshape(
        total_rows, 3 * local_width
    )
    qkv_grad = qkv_grad.astype(jnp.bfloat16)
    qkv_shift_grad = jnp.sum(qkv_grad.astype(jnp.float32), axis=0)
    qkv_grad_weight = jnp.dot(attn_in.T, qkv_grad, preferred_element_type=jnp.float32)
    qkv_grad_weight = qkv_grad_weight.reshape(model_width, 3, local_width)
    piece = qkv_grad
    normed_one_grad = lax.psum_scatter(
        jnp.dot(piece, qkv_back.T, preferred_element_type=jnp.float32).astype(jnp.bfloat16),
        "tensor",
        scatter_dimension=0,
        tiled=True,
    ).astype(jnp.float32)
    input_part, gain_one_grad, shift_one_grad = norm_backward(
        normed_one_grad, unit_one, inverse_one, gain_one
    )
    input_grad = middle_grad + input_part
    qkv_grad_shard, proj_grad_shard, fc1_grad_shard, fc2_grad_shard = (
        lax.psum_scatter(
            qkv_grad_weight.astype(jnp.bfloat16), "dp", scatter_dimension=0, tiled=True
        ).astype(jnp.float32),
        lax.psum_scatter(
            proj_grad.astype(jnp.bfloat16), "dp", scatter_dimension=1, tiled=True
        ).astype(jnp.float32),
        lax.psum_scatter(
            fc1_grad.astype(jnp.bfloat16), "dp", scatter_dimension=0, tiled=True
        ).astype(jnp.float32),
        lax.psum_scatter(
            fc2_grad.astype(jnp.bfloat16), "dp", scatter_dimension=1, tiled=True
        ).astype(jnp.float32),
    )
    qkv_shift_full = lax.dynamic_update_slice_in_dim(
        jnp.zeros((3, model_width), jnp.float32),
        qkv_shift_grad.reshape(3, local_width),
        tensor_index * local_width,
        1,
    )
    fc1_shift_full = lax.dynamic_update_slice_in_dim(
        jnp.zeros((fc1_bias.shape[0],), jnp.float32), fc1_shift_grad, tensor_index * local_hidden, 0
    )
    summed = lax.psum(
        (
            gain_one_grad,
            shift_one_grad,
            qkv_shift_full,
            proj_shift_grad,
            gain_two_grad,
            shift_two_grad,
            fc1_shift_full,
            fc2_shift_grad,
        ),
        ("dp", "tensor"),
    )
    return (
        output,
        input_grad,
        summed[0],
        summed[1],
        qkv_grad_shard,
        summed[2],
        proj_grad_shard,
        summed[3],
        summed[4],
        summed[5],
        fc1_grad_shard,
        summed[6],
        fc2_grad_shard,
        summed[7],
    )


def solution(mesh):
    return jax.shard_map(
        on_device,
        mesh=mesh,
        in_specs=(
            P(("dp", "tensor"), None),
            P(("dp", "tensor"), None),
            P("dp"),
            P(None, "dp"),
            P("dp"),
            P(),
            P(),
            P("dp", None, "tensor"),
            P(),
            P("tensor", "dp"),
            P(),
            P(),
            P(),
            P("dp", "tensor"),
            P(),
            P("tensor", "dp"),
            P(),
        ),
        out_specs=(
            P(("dp", "tensor"), None),
            P(("dp", "tensor"), None),
            P(),
            P(),
            P("dp", None, "tensor"),
            P(),
            P("tensor", "dp"),
            P(),
            P(),
            P(),
            P("dp", "tensor"),
            P(),
            P("tensor", "dp"),
            P(),
        ),
        check_vma=False,
    )
```

profile of v0, /device:TPU:8, one launch (start us, length us, event | category | flops | bytes accessed | tf_op | source)
XLA Modules:
  0.0 1712.3 jit_solution(11466806691444289608)
XLA Ops:
  21.6 72.3 %all-gather.11.cloned.1.call-done = bf16[1280,3,640]{2,0,1:T(8,128)(2,1)} async-done(((bf16[80,3,640]{2,0,1:T(8,128)(2,1)}), bf16[1280,3,640]{2,0,1:T(8,128)(2,1)}) %all-gather.11.cloned.1.call-update) | async-done | bytes 4915216 | tf_op jit(solution)/shard_map/all_gather | solution.py:156
  150.7 201.2 %while.27 = (s32[]{:T(128)}, bf16[4,512,8,80]{1,3,2,0:T(8,128)(2,1)}, f32[4,8,512]{2,1,0:T(8,128)}, s32[4]{0:T(128)S(1)}, s32[2048]{0:T(1024)S(1)}, /*index=5*/s...) while((s32[]{:T(128)}, ...), condition=%wide.region_5.6_spmd, body=%wide.region_2.5_spmd.sunk | while | flops 2787440640 | bytes 115763440 | solution.py:75
  391.8 90.6 %all-gather.17.cloned.1.call-done = bf16[1280,2560]{1,0:T(8,128)(2,1)} async-done(((bf16[80,2560]{1,0:T(8,128)(2,1)}), bf16[1280,2560]{1,0:T(8,128)(2,1)}) %all-gather.17.cloned.1.call-update) | async-done | bytes 6553616 | tf_op jit(solution)/shard_map/all_gather | solution.py:158
  498.9 25.7 %multiply_convert_fusion.2 = (bf16[2048,2560]{1,0:T(8,128)(2,1)}, f32[2048,2560]{1,0:T(8,128)}) fusion(f32[2560]{0:T(1024)S(1)} %dynamic-slice_convert_fusion, bf16[2048,1280]{1,0:T(8,128)(2,1)} %all-gather.15.cloned.1.call-done, bf16[1280,2560]{1,0:T(8,128)(2,1)} %all-gather.17.cloned.1.call-done), kind=kOutput, calls=%fused_computation.40 | convolution fusion | flops 13458472960 | bytes 43264000 | tf_op jit(solution)/shard_map/dot_general | solution.py:184
  524.6 92.3 %all-gather.19.cloned.1.call-done = bf16[2560,1280]{0,1:T(8,128)(2,1)} async-done(((bf16[2560,80]{0,1:T(8,128)(2,1)}), bf16[2560,1280]{0,1:T(8,128)(2,1)}) %all-gather.19.cloned.1.call-update) | async-done | bytes 6553616 | tf_op jit(solution)/shard_map/all_gather | solution.py:159
  616.9 30.0 %convert_reduce_fusion = (f32[2560]{0:T(1024)}, bf16[2048,2560]{1,0:T(8,128)(2,1)}) fusion(f32[2048,2560]{1,0:T(8,128)} %get-tuple-element.260, f32[2560]{0:T(1024)S(1)} %dynamic-slice_convert_fusion, bf16[2048,1280]{1,0:T(8,128)(2,1)} %all-gather.21.cloned.1.call-done, bf16[2560,1280]{0,1:T(8,128)(2,1)} %all-gather.19.cloned.1.call-done), kind=kOutput, calls=%fused_computation.38 | convolution fusion | flops 13489928192 | bytes 43274240 | tf_op jit(solution)/shard_map/dot_general | solution.py:206
  666.3 19.8 %convolution_convert_fusion.5 = bf16[2048,1280]{1,0:T(8,128)(2,1)} fusion(bf16[2048,2560]{1,0:T(8,128)(2,1)} %get-tuple-element.259, bf16[2560,1280]{0,1:T(8,128)(2,1)} %all-gather.19.cloned.1.call-done), kind=kOutput, calls=%fused_computation.59 | convolution fusion | flops 13424394240 | bytes 22282240 | tf_op jit(solution)/shard_map/dot_general | solution.py:189
  708.9 19.9 %convolution_convert_fusion = bf16[2560,1280]{0,1:T(8,128)(2,1)} fusion(bf16[2048,2560]{1,0:T(8,128)(2,1)} %get-tuple-element.259, bf16[2048,1280]{1,0:T(8,128)(2,1)} %all-gather.21.cloned.1.call-done), kind=kOutput, calls=%fused_computation.44 | convolution fusion | flops 13425049600 | bytes 22282240 | tf_op jit(solution)/shard_map/dot_general | solution.py:205
  728.9 20.1 %convolution_convert_fusion.1 = bf16[1280,2560]{1,0:T(8,128)(2,1)} fusion(bf16[2048,1280]{1,0:T(8,128)(2,1)} %all-gather.15.cloned.1.call-done, bf16[2048,2560]{1,0:T(8,128)(2,1)} %get-tuple-element.262), kind=kOutput, calls=%fused_computation.45 | convolution fusion | flops 13425049600 | bytes 22282240 | tf_op jit(solution)/shard_map/dot_general | solution.py:210
  757.4 563.9 %while.28 = (s32[]{:T(128)}, f32[2048,8,80]{0,2,1:T(8,128)}, f32[2048,8,80]{0,2,1:T(8,128)}, f32[4,512,8,80]{1,0,3,2:T(4,128)}, s32[4]{0:T(128)S(1)}, /*index=5*...) while((s32[]{:T(128)}, f32[2048,8,80]{0,2,1:T(8,128)}, ...), condition=%wide.region_15.16_spmd.clone, body=%wide.region_13.15_spmd.clone.sunk | while | flops 6795360256 | bytes 374712704 | solution.py:115
  780.4 25.0 %multiply_reduce_fusion.3 = (f32[8,512]{1,0:T(8,128)S(1)}, f32[8,512,2048]{2,1,0:T(8,128)}) fusion(f32[8,512,2048]{2,1,0:T(8,128)} %fusion.123, f32[8,512]{1,0:T(8,128)S(1)} %dynamic-slice_bitcast_fusion.2, bf16[2048,8,80]{0,2,1:T(8,128)(2,1)S(1)} %get-tuple-element.482, bf16[2048,8,80]{0,2,1:T(8,128)(2,1)} %get-tuple-element.479, ...), kind=kOutput, calls=%fused_computation.18.clone.1 | convolution fusion | flops 1384116224 | bytes 71467008 | tf_op jit(solution)/shard_map/while/body/eval_jaxpr/qhd,khd->hqk/dot_general | solution.py:54
  805.4 27.8 %multiply_convert_fusion.4 = bf16[8,512,2048]{2,1,0:T(8,128)(2,1)} fusion(f32[8,512,2048]{2,1,0:T(8,128)} %get-tuple-element.399, f32[8,512,2048]{2,1,0:T(8,128)} %fusion.123, f32[8,512]{1,0:T(8,128)S(1)} %get-tuple-element.400), kind=kLoop, calls=%fused_computation.17.clone.1 | loop fusion | flops 25165824 | bytes 83902464 | tf_op jit(solution)/shard_map/while/body/eval_jaxpr/convert_element_type | solution.py:95
  870.8 26.1 %dynamic_update_slice.29 = f32[4,512,8,80]{1,0,3,2:T(4,128)} dynamic-update-slice(f32[4,512,8,80]{1,0,3,2:T(4,128)} %get-tuple-element.460, f32[1,512,8,80]{1,0,3,2:T(1,128)} %copy.64, s32[]{:T(128)S(6)} %copy.81, s32[]{:T(128)} %constant.50.clone.1..sunk.1, s32[]{:T(128)} %constant.50.clone.1..sunk.1, s32[]{:T(128)} %constant.50.clone.1..sunk.1) | dynamic-update-slice | bytes 2621444 | tf_op jit(solution)/shard_map/while/body/jit(dynamic_update_index_in_dim)/dynamic_update_slice | solution.py:115
  919.4 25.0 %multiply_reduce_fusion.3 = (f32[8,512]{1,0:T(8,128)S(1)}, f32[8,512,2048]{2,1,0:T(8,128)}) fusion(f32[8,512,2048]{2,1,0:T(8,128)} %fusion.123, f32[8,512]{1,0:T(8,128)S(1)} %dynamic-slice_bitcast_fusion.2, bf16[2048,8,80]{0,2,1:T(8,128)(2,1)S(1)} %get-tuple-element.482, bf16[2048,8,80]{0,2,1:T(8,128)(2,1)} %get-tuple-element.479, ...), kind=kOutput, calls=%fused_computation.18.clone.1 | convolution fusion | flops 1384116224 | bytes 71467008 | tf_op jit(solution)/shard_map/while/body/eval_jaxpr/qhd,khd->hqk/dot_general | solution.py:54
  944.4 27.8 %multiply_convert_fusion.4 = bf16[8,512,2048]{2,1,0:T(8,128)(2,1)} fusion(f32[8,512,2048]{2,1,0:T(8,128)} %get-tuple-element.399, f32[8,512,2048]{2,1,0:T(8,128)} %fusion.123, f32[8,512]{1,0:T(8,128)S(1)} %get-tuple-element.400), kind=kLoop, calls=%fused_computation.17.clone.1 | loop fusion | flops 25165824 | bytes 83902464 | tf_op jit(solution)/shard_map/while/body/eval_jaxpr/convert_element_type | solution.py:95
  1012.9 26.1 %dynamic_update_slice.29 = f32[4,512,8,80]{1,0,3,2:T(4,128)} dynamic-update-slice(f32[4,512,8,80]{1,0,3,2:T(4,128)} %get-tuple-element.460, f32[1,512,8,80]{1,0,3,2:T(1,128)} %copy.64, s32[]{:T(128)S(6)} %copy.81, s32[]{:T(128)} %constant.50.clone.1..sunk.1, s32[]{:T(128)} %constant.50.clone.1..sunk.1, s32[]{:T(128)} %constant.50.clone.1..sunk.1) | dynamic-update-slice | bytes 2621444 | tf_op jit(solution)/shard_map/while/body/jit(dynamic_update_index_in_dim)/dynamic_update_slice | solution.py:115
  1061.3 24.9 %multiply_reduce_fusion.3 = (f32[8,512]{1,0:T(8,128)S(1)}, f32[8,512,2048]{2,1,0:T(8,128)}) fusion(f32[8,512,2048]{2,1,0:T(8,128)} %fusion.123, f32[8,512]{1,0:T(8,128)S(1)} %dynamic-slice_bitcast_fusion.2, bf16[2048,8,80]{0,2,1:T(8,128)(2,1)S(1)} %get-tuple-element.482, bf16[2048,8,80]{0,2,1:T(8,128)(2,1)} %get-tuple-element.479, ...), kind=kOutput, calls=%fused_computation.18.clone.1 | convolution fusion | flops 1384116224 | bytes 71467008 | tf_op jit(solution)/shard_map/while/body/eval_jaxpr/qhd,khd->hqk/dot_general | solution.py:54
  1086.2 27.4 %multiply_convert_fusion.4 = bf16[8,512,2048]{2,1,0:T(8,128)(2,1)} fusion(f32[8,512,2048]{2,1,0:T(8,128)} %get-tuple-element.399, f32[8,512,2048]{2,1,0:T(8,128)} %fusion.123, f32[8,512]{1,0:T(8,128)S(1)} %get-tuple-element.400), kind=kLoop, calls=%fused_computation.17.clone.1 | loop fusion | flops 25165824 | bytes 83902464 | tf_op jit(solution)/shard_map/while/body/eval_jaxpr/convert_element_type | solution.py:95
  1154.0 26.1 %dynamic_update_slice.29 = f32[4,512,8,80]{1,0,3,2:T(4,128)} dynamic-update-slice(f32[4,512,8,80]{1,0,3,2:T(4,128)} %get-tuple-element.460, f32[1,512,8,80]{1,0,3,2:T(1,128)} %copy.64, s32[]{:T(128)S(6)} %copy.81, s32[]{:T(128)} %constant.50.clone.1..sunk.1, s32[]{:T(128)} %constant.50.clone.1..sunk.1, s32[]{:T(128)} %constant.50.clone.1..sunk.1) | dynamic-update-slice | bytes 2621444 | tf_op jit(solution)/shard_map/while/body/jit(dynamic_update_index_in_dim)/dynamic_update_slice | solution.py:115
  1202.4 24.9 %multiply_reduce_fusion.3 = (f32[8,512]{1,0:T(8,128)S(1)}, f32[8,512,2048]{2,1,0:T(8,128)}) fusion(f32[8,512,2048]{2,1,0:T(8,128)} %fusion.123, f32[8,512]{1,0:T(8,128)S(1)} %dynamic-slice_bitcast_fusion.2, bf16[2048,8,80]{0,2,1:T(8,128)(2,1)S(1)} %get-tuple-element.482, bf16[2048,8,80]{0,2,1:T(8,128)(2,1)} %get-tuple-element.479, ...), kind=kOutput, calls=%fused_computation.18.clone.1 | convolution fusion | flops 1384116224 | bytes 71467008 | tf_op jit(solution)/shard_map/while/body/eval_jaxpr/qhd,khd->hqk/dot_general | solution.py:54
  1227.3 27.4 %multiply_convert_fusion.4 = bf16[8,512,2048]{2,1,0:T(8,128)(2,1)} fusion(f32[8,512,2048]{2,1,0:T(8,128)} %get-tuple-element.399, f32[8,512,2048]{2,1,0:T(8,128)} %fusion.123, f32[8,512]{1,0:T(8,128)S(1)} %get-tuple-element.400), kind=kLoop, calls=%fused_computation.17.clone.1 | loop fusion | flops 25165824 | bytes 83902464 | tf_op jit(solution)/shard_map/while/body/eval_jaxpr/convert_element_type | solution.py:95
  1295.1 26.1 %dynamic_update_slice.29 = f32[4,512,8,80]{1,0,3,2:T(4,128)} dynamic-update-slice(f32[4,512,8,80]{1,0,3,2:T(4,128)} %get-tuple-element.460, f32[1,512,8,80]{1,0,3,2:T(1,128)} %copy.64, s32[]{:T(128)S(6)} %copy.81, s32[]{:T(128)} %constant.50.clone.1..sunk.1, s32[]{:T(128)} %constant.50.clone.1..sunk.1, s32[]{:T(128)} %constant.50.clone.1..sunk.1) | dynamic-update-slice | bytes 2621444 | tf_op jit(solution)/shard_map/while/body/jit(dynamic_update_index_in_dim)/dynamic_update_slice | solution.py:115
  1430.7 112.3 %reduce-scatter.17.cloned.1.call-done = bf16[80,3,640]{2,0,1:T(8,128)(2,1)} async-done(((bf16[1280,3,640]{2,0,1:T(8,128)(2,1)}), bf16[80,3,640]{2,0,1:T(8,128)(2,1)}) %reduce-scatter.17.cloned.1.call-update) | async-done | bytes 307216 | tf_op jit(solution)/shard_map/reduce_scatter | solution.py:254
  1571.4 123.6 %all-reduce.3.cloned.1.call-done = (f32[1280]{0:T(1024)}, f32[1280]{0:T(1024)}, f32[3,1280]{1,0:T(4,128)}, f32[1280]{0:T(1024)}, f32[1280]{0:T(1024)}, /*index=5*/f32[1280]{0:T(1024)}, f32[5120]{0:T(1024)}, f32[1280]{0:T(1024)}) async-done(((f32[1280]{0:T(1024)}, f32[1280]{0:T(1024)}, f32[3,1280]{1,0:T(4,128)}, f32[1280]{0:T(1024)}, f32[1280]{0:T(1024)}, /*index=5*/f32[1280]{0:T(1024)}, f32[5120]{0:T(1024)}, ...) | async-done | bytes 66576 | tf_op jit(solution)/shard_map/psum | solution.py:276
  (326 shorter events, 761.7 us)
Async XLA Ops:
  7.2 86.7 %all-gather.11.cloned.1.call-start = ((), (), s32[]{:S(2)}) async-start(), calls=%async_computation.9 | async-start | bytes 5222400 | tf_op jit(solution)/shard_map/all_gather | solution.py:156
  7.9 102.3 %all-gather.9.cloned.1.call-start = ((), (), s32[]{:S(2)}) async-start(), calls=%async_computation.8 | async-start | bytes 7864320 | tf_op jit(solution)/shard_map/all_gather | solution.py:164
  17.3 341.8 %all-gather.13.cloned.1.call-start = ((), (), s32[]{:S(2)}) async-start(), calls=%async_computation.10 | async-start | bytes 1740800 | tf_op jit(solution)/shard_map/all_gather | solution.py:157
  18.0 364.6 %reduce-scatter.9.cloned.1.call-start = ((), (), s32[]{:S(2)}) async-start(), calls=%async_computation.11 | async-start | bytes 7864320 | tf_op jit(solution)/shard_map/reduce_scatter | solution.py:175
  21.6 118.8 %copy-start.13 = (f32[2048,80]{0,1:T(8,128)}, f32[2048,80]{0,1:T(8,128)S(1)}, u32[]{:S(2)}) copy-start(f32[2048,80]{0,1:T(8,128)S(1)} %get-tuple-element.253) | copy-start | bytes 1966084
  368.0 114.4 %all-gather.17.cloned.1.call-start = ((), (), s32[]{:S(2)}) async-start(), calls=%async_computation.13 | async-start | bytes 6963200 | tf_op jit(solution)/shard_map/all_gather | solution.py:158
  368.6 130.3 %all-gather.15.cloned.1.call-start = ((), (), s32[]{:S(2)}) async-start(), calls=%async_computation.12 | async-start | bytes 7864320 | tf_op jit(solution)/shard_map/all_gather | solution.py:183
  390.2 134.4 %all-gather.21.cloned.1.call-start = ((), (), s32[]{:S(2)}) async-start(), calls=%async_computation.16 | async-start | bytes 7864320 | tf_op jit(solution)/shard_map/all_gather | solution.py:204
  391.0 226.0 %all-gather.19.cloned.1.call-start = ((), (), s32[]{:S(2)}) async-start(), calls=%async_computation.14 | async-start | bytes 6963200 | tf_op jit(solution)/shard_map/all_gather | solution.py:159
  391.7 295.1 %reduce-scatter.13.cloned.1.call-start = ((), (), s32[]{:S(2)}) async-start(), calls=%async_computation.17 | async-start | bytes 7864320 | tf_op jit(solution)/shard_map/reduce_scatter | solution.py:212
  666.3 32.6 %reduce-scatter.11.cloned.1.call-start = ((), (), s32[]{:S(2)}) async-start(), calls=%async_computation.15 | async-start | bytes 7864320 | tf_op jit(solution)/shard_map/reduce_scatter | solution.py:188
  686.2 62.9 %all-gather.23.cloned.1.call-start = ((), (), s32[]{:S(2)}) async-start(), calls=%async_computation.18 | async-start | bytes 7864320 | tf_op jit(solution)/shard_map/all_gather | solution.py:224
  708.8 698.0 %reduce-scatter.23.cloned.1.call-start = ((), (), s32[]{:S(2)}) async-start(), calls=%async_computation.23 | async-start | bytes 6963200 | tf_op jit(solution)/shard_map/reduce_scatter | solution.py:263
  728.8 680.0 %reduce-scatter.21.cloned.1.call-start = ((), (), s32[]{:S(2)}) async-start(), calls=%async_computation.22 | async-start | bytes 6963200 | tf_op jit(solution)/shard_map/reduce_scatter | solution.py:260
  749.1 680.0 %reduce-scatter.19.cloned.1.call-start = ((), (), s32[]{:S(2)}) async-start(), calls=%async_computation.21 | async-start | bytes 1740800 | tf_op jit(solution)/shard_map/reduce_scatter | solution.py:257
  1354.7 188.3 %reduce-scatter.17.cloned.1.call-start = ((), (), s32[]{:S(2)}) async-start(), calls=%async_computation.20 | async-start | bytes 5222400 | tf_op jit(solution)/shard_map/reduce_scatter | solution.py:254
  1388.8 172.2 %reduce-scatter.15.cloned.1.call-start = ((), (), s32[]{:S(2)}) async-start(), calls=%async_computation.19 | async-start | bytes 7864320 | tf_op jit(solution)/shard_map/reduce_scatter | solution.py:243
  1405.5 155.5 %copy-start.8 = (bf16[1024,1280]{1,0:T(8,128)(2,1)S(1)}, bf16[1024,1280]{1,0:T(8,128)(2,1)}, u32[]{:S(2)}) copy-start(bf16[1024,1280]{1,0:T(8,128)(2,1)} %param.21) | copy-start | bytes 7864324
  1405.5 155.5 %copy-start.25 = (f32[1280]{0:T(1024)S(1)}, f32[1280]{0:T(1024)}, u32[]{:S(2)}) copy-start(f32[1280]{0:T(1024)} %copy-done.24) | copy-start | bytes 15364
  1405.5 155.5 %copy-start.29 = (f32[1024]{0:T(1024)S(1)}, f32[1024]{0:T(1024)}, u32[]{:S(2)}) copy-start(f32[1024]{0:T(1024)} %copy-done.28) | copy-start | bytes 12292
  1405.5 155.5 %copy-start.35 = (f32[1024]{0:T(1024)S(1)}, f32[1024]{0:T(1024)}, u32[]{:S(2)}) copy-start(f32[1024]{0:T(1024)} %copy-done.34) | copy-start | bytes 12292
  1405.5 289.6 %all-reduce.3.cloned.1.call-start = ((), (), s32[]{:S(2)}) async-start(), calls=%async_computation.24 | async-start | bytes 180224 | tf_op jit(solution)/shard_map/psum | solution.py:276
  1406.8 159.0 %copy-start.33 = (f32[5120]{0:T(1024)}, f32[5120]{0:T(1024)S(1)}, u32[]{:S(2)}) copy-start(f32[5120]{0:T(1024)S(1)} %dynamic_update_slice.19) | copy-start | bytes 61444
  1410.8 154.9 %copy-start.32 = (f32[3,1280]{1,0:T(4,128)}, f32[3,1280]{1,0:T(4,128)S(1)}, u32[]{:S(2)}) copy-start(f32[3,1280]{1,0:T(4,128)S(1)} %constant_dynamic-update-slice_fusion) | copy-start | bytes 46084
  (57 other events, 483.8 us)
Sparse Core Ops, SparseCore 0:
  10.7 83.1 all-gather.10
  96.0 14.1 all-gather.8
  112.9 58.3 all-gather.12
  368.1 14.4 reduce-scatter.8
  385.5 96.8 all-gather.16
  484.5 14.4 all-gather.14
  500.5 16.3 all-gather.20
  520.0 96.8 all-gather.18
  666.4 12.5 reduce-scatter.12
  686.3 12.5 reduce-scatter.10
  708.9 16.3 all-gather.22
  728.9 141.5 reduce-scatter.22
  872.8 143.3 reduce-scatter.20
  1354.8 74.2 reduce-scatter.18
  1431.3 111.6 reduce-scatter.16
  1545.2 15.7 reduce-scatter.14
  1568.4 126.6 all-reduce.2
where the time goes:
time: 1720 us; the launch traced here: 1710 us
  matrix products  647 us (38%)
  waiting for transfers between devices  573 us (33%)
  other arithmetic  274 us (16%)
  local copies, waits for them, and re-layouts  188 us (11%)
    dot_general x8, matrix products, block_scores(): jnp.einsum('qhd,khd->hqk', query_block, keys, preferred_element_type=jnp....  162 us
    psum x1, waiting for transfers between devices, on_device(): lax.psum((gain_one_grad, shift_one_grad, qkv_shift_full, proj_shift_grad,...  124 us
    dynamic_update_slice x8, local copies, waits for them, and re-layouts, attend_back(): lax.scan(one_block, (zeros, zeros), jnp.arange(length // block))  114 us
    reduce_scatter x1, waiting for transfers between devices, on_device(): lax.psum_scatter(qkv_grad_weight.astype(jnp.bfloat16), 'dp', scatter_dime...  112 us
    convert_element_type x4, other arithmetic, one_block(): score_grad = (probs * (prob_grad - center)).astype(jnp.bfloat16)  111 us
    all_gather x1, waiting for transfers between devices, on_device(): lax.all_gather(fc2_weight, 'dp', axis=1, tiled=True)  92.3 us
    all_gather x1, waiting for transfers between devices, on_device(): lax.all_gather(fc1_weight, 'dp', axis=0, tiled=True)  90.6 us
    all_gather x1, waiting for transfers between devices, on_device(): lax.all_gather(qkv_weight, 'dp', axis=0, tiled=True)  72.3 us
  transfers between devices with their start and end apart: 17, of which 11 were waited for; matrix products, arithmetic and copies ran while one was open for 59% of the time, Pallas kernels for 0%

commit v1 on v0

--- a/solution.py
+++ b/solution.py
@@ -1,19 +1,43 @@
+import functools
+import math
+
 import jax
 import jax.numpy as jnp
 from jax import lax
+from jax.experimental import pallas as pl
+from jax.experimental.pallas import tpu as pltpu
 from jax.sharding import PartitionSpec as P
 
 HEAD_DIM = 80
-
-
 EPS = 1e-06
-
-
-def norm_forward(values, gain, shift):
+LOG2E = math.log2(math.e)
+FAR = 1e30
+f32 = jnp.float32
+bf16 = jnp.bfloat16
+NT = (((1,), (1,)), ((), ()))
+NN = (((1,), (0,)), ((), ()))
+TN = (((0,), (0,)), ((), ()))
+
+
+def lasts(micros):
+    return pl.CostEstimate(flops=int(micros * 1.1e9), bytes_accessed=1, transcendentals=0)
+
+
+ROOMY = pltpu.CompilerParams(vmem_limit_bytes=62 * 2**20)
+
+
+def mm(left, right, dims):
+    return lax.dot_general(left, right, dims, preferred_element_type=f32)
+
+
+def whole(shape):
+    return pl.BlockSpec(shape, lambda i: (0,) * len(shape))
+
+
+def norm_parts(values):
     center = values - jnp.mean(values, axis=-1, keepdims=True)
     inverse = lax.rsqrt(jnp.mean(center * center, axis=-1, keepdims=True) + EPS)
-    unit = center * inverse
-    return (unit * gain + shift, unit, inverse)
+    return center * inverse, inverse
 
 
 def norm_backward(grad_out, unit, inverse, gain):
@@ -26,99 +50,668 @@
     return (grad_in, jnp.sum(grad_out * unit, axis=0), jnp.sum(grad_out, axis=0))
 
 
-def rope_tables(place):
+def rope_tables(place, width):
     quarter = HEAD_DIM // 4
-    freqs = 10000.0 ** (-2.0 * jnp.arange(quarter, dtype=jnp.float32) / (HEAD_DIM // 2))
-    along_rows = place[0].astype(jnp.float32)[:, None] * freqs[None, :]
-    along_cols = place[1].astype(jnp.float32)[:, None] * freqs[None, :]
-    theta = jnp.concatenate([along_rows, along_cols, along_rows, along_cols], axis=1)
-    return (jnp.cos(theta)[:, None, :], jnp.sin(theta)[:, None, :])
-
-
-def rotate(values, cosine, sine):
-    half = values.shape[-1] // 2
-    turned = jnp.concatenate([-values[..., half:], values[..., :half]], axis=-1)
-    return values * cosine + turned * sine
-
-
-def rotate_back(grads, cosine, sine):
-    half = grads.shape[-1] // 2
-    weighted = grads * sine
-    turned = jnp.concatenate([weighted[..., half:], -weighted[..., :half]], axis=-1)
-    return grads * cosine + turned
-
-
-def block_scores(query_block, keys, id_block, picture, live):
-    scale = HEAD_DIM ** (-0.5)
-    scores = (
-        jnp.einsum("qhd,khd->hqk", query_block, keys, preferred_element_type=jnp.float32) * scale
-    )
-    allowed = (id_block[:, None] == picture[None, :]) & (live[None, :] > 0)
-    return jnp.where(allowed[None], scores, -1e30)
-
-
-def attend_row(queries, keys, values, picture, live):
-    length = queries.shape[0]
-    block = min(512, length)
-
-    def one_block(index):
-        query_block = lax.dynamic_slice_in_dim(queries, index * block, block, 0)
-        id_block = lax.dynamic_slice_in_dim(picture, index * block, block, 0)
-        scores = block_scores(query_block, keys, id_block, picture, live)
-        peak = jnp.max(scores, axis=-1, keepdims=True)
-        shifted = jnp.exp(scores - peak)
-        total = jnp.sum(shifted, axis=-1, keepdims=True)
-        probs = (shifted / total).astype(jnp.bfloat16)
-        mixed = jnp.einsum("hqk,khd->qhd", probs, values, preferred_element_type=jnp.float32)
-        return (mixed.astype(jnp.bfloat16), (peak + jnp.log(total))[..., 0])
-
-    mixed, logsum = lax.map(one_block, jnp.arange(length // block))
-    return (mixed.reshape(length, queries.shape[1], queries.shape[2]), logsum)
-
-
-def attend_back(queries, keys, values, picture, live, mixed_grad, logsum):
-    length = queries.shape[0]
-    block = min(512, length)
-    scale = HEAD_DIM ** (-0.5)
-
-    def one_block(carry, index):
-        key_grad, value_grad = carry
-        query_block = lax.dynamic_slice_in_dim(queries, index * block, block, 0)
-        id_block = lax.dynamic_slice_in_dim(picture, index * block, block, 0)
-        grad_block = lax.dynamic_slice_in_dim(mixed_grad, index * block, block, 0)
-        scores = block_scores(query_block, keys, id_block, picture, live)
-        probs = jnp.exp(scores - logsum[index][..., None])
-        prob_grad = jnp.einsum(
-            "qhd,khd->hqk", grad_block, values, preferred_element_type=jnp.float32
+    freqs = 10000.0 ** (-2.0 * jnp.arange(quarter, dtype=f32) / (HEAD_DIM // 2))
+    along_rows = place[0].astype(f32)[:, None] * freqs[None, :]
+    along_cols = place[1].astype(f32)[:, None] * freqs[None, :]
+    theta = jnp.concatenate([along_rows, along_cols], axis=1)
+    lane = jnp.arange(width)[None, :] % HEAD_DIM
+    entry = jnp.arange(HEAD_DIM // 2)[:, None]
+    low = jnp.where(lane == entry, 1.0, 0.0)
+    high = jnp.where(lane == entry + HEAD_DIM // 2, 1.0, 0.0)
+    exact = functools.partial(jnp.dot, precision=lax.Precision.HIGHEST)
+    cosine, sine = jnp.cos(theta), jnp.sin(theta)
+    return exact(cosine, low + high), exact(sine, -low), exact(sine, high)
+
+
+def mask_lanes(picture, valid, pairs):
+    lane = jnp.arange(256)[None, None, :]
+    pair = jnp.arange(pairs)[:, None, None]
+    spare = (lane - 32 * pair - 160) % 256
+    ident = picture[None, :, None]
+    dead = (valid <= 0).astype(f32)[None, :, None]
+    for_query = jnp.where(
+        spare < 4, jnp.where(spare == ident, 0.0, -FAR), jnp.where(spare == 4, -FAR, 0.0)
+    )
+    for_key = jnp.where(
+        spare < 4, jnp.where(spare == ident, 1.0, 0.0), jnp.where(spare == 4, dead, 0.0)
+    )
+    return for_query.astype(bf16), for_key.astype(bf16)
+
+
+def window_lanes(pair):
+    place = lax.broadcasted_iota(jnp.int32, (1, 256), 1) - 32 * pair
+    first = (place >= 0) & (place < HEAD_DIM)
+    second = (place >= HEAD_DIM) & (place < 2 * HEAD_DIM)
+    return first, second, (place - 2 * HEAD_DIM) & 255
+
+
+def as_ones(condition):
+    return jnp.where(condition, 1.0, 0.0).astype(bf16)
+
+
+def reach(length, block):
+    half, most = length // 2, 3 * length // 4
+    spans = []
+    for start in range(0, length, block):
+        if start + block <= half:
+            spans.append((start, 0, most))
+        elif start >= most:
+            spans.append((start, half, length))
+        else:
+            spans.append((start, 0, length))
+    return spans
+
+
+def attend_kernel(*refs, block, begin):
+    mq_ref, mk_ref, q_ref, k_ref, v_ref = refs[:5]
+    o_ref, lse_ref, qs, ks, vs = refs[-5:]
+    length = q_ref.shape[0]
+    pair = pl.program_id(0) + begin
+    if begin:
+
+        @pl.when(pl.program_id(0) == 0)
+        def _():
+            o_ref[...] = refs[5][...]
+
+    win = pl.ds(pl.multiple_of(128 * pair, 128), 256)
+    first, second, spare = window_lanes(pair)
+    both = first | second
+    m0, m1, mp = as_ones(first), as_ones(second), as_ones(both)
+    count0, count1 = as_ones(spare == 5), as_ones(spare == 6)
+    for start in range(0, length, 512):
+        rows = pl.ds(start, 512)
+        mk = mk_ref[0, rows, :]
+        k, v = k_ref[rows, win], v_ref[rows, win]
+        qs[rows, :] = q_ref[rows, win] * mp + mq_ref[0, rows, :]
+        ks[0, rows, :] = k * m0 + mk
+        ks[1, rows, :] = k * m1 + mk
+        vs[0, rows, :] = v * m0 + count0
+        vs[1, rows, :] = v * m1 + count1
+    for start, low, high in reach(length, block):
+        rows, keys = pl.ds(start, block), pl.ds(low, high - low)
+        weights, peaks = [], []
+        for head in range(2):
+            scores = mm(qs[rows, :], ks[head, keys, :], NT)
+            peak = jnp.max(scores, axis=1, keepdims=True)
+            peaks.append(peak)
+            weights.append(jnp.exp2(scores - peak).astype(bf16))
+        mixed = mm(
+            jnp.concatenate(weights, 1),
+            jnp.concatenate([vs[0, keys, :], vs[1, keys, :]], 0),
+            NN,
         )
-        center = jnp.sum(probs * prob_grad, axis=-1, keepdims=True)
-        score_grad = (probs * (prob_grad - center)).astype(jnp.bfloat16)
-        query_grad = (
-            jnp.einsum("hqk,khd->qhd", score_grad, keys, preferred_element_type=jnp.float32) * scale
+        total0 = jnp.sum(jnp.where(spare == 5, mixed, 0.0), axis=1, keepdims=True)
+        total1 = jnp.sum(jnp.where(spare == 6, mixed, 0.0), axis=1, keepdims=True)
+        mixed = mixed * jnp.where(first, 1.0 / total0, 1.0 / total1)
+        o_ref[rows, win] = jnp.where(both, mixed, o_ref[rows, win].astype(f32)).astype(bf16)
+        lane = lax.broadcasted_iota(jnp.int32, (block, 128), 1)
+        sums = jnp.where(
+            lane == 0,
+            peaks[0] + jnp.log2(total0),
+            jnp.where(lane == 1, peaks[1] + jnp.log2(total1), 0.0),
         )
-        key_grad = (
-            key_grad
-            + jnp.einsum(
-                "hqk,qhd->khd", score_grad, query_block, preferred_element_type=jnp.float32
+        lse_ref[0, :, rows] = jnp.transpose(sums)[:8, :]
+
+
+def attend(mq, mk, q, k, v, begin=0, count=None, before=(), block=512):
+    length, width = q.shape
+    count = mq.shape[0] - begin if count is None else count
+    part = lambda shape, skip: pl.BlockSpec(shape, lambda i: (i + skip, 0, 0))
+    return pl.pallas_call(
+        functools.partial(attend_kernel, block=block, begin=begin),
+        grid=(count,),
+        in_specs=[part((1, length, 256), begin)] * 2
+        + [whole((length, width))] * (3 + len(before)),
+        out_specs=[whole((length, width)), part((1, 8, length), 0)],
+        scratch_shapes=[pltpu.VMEM((length, 256), bf16)]
+        + [pltpu.VMEM((2, length, 256), bf16)] * 2,
+        out_shape=[
+            jax.ShapeDtypeStruct((length, width), bf16),
+            jax.ShapeDtypeStruct((count, 8, length), f32),
+        ],
+        compiler_params=ROOMY,
+        cost_estimate=lasts(10),
+        name="attend",
+    )(mq, mk, q, k, v, *before)
+
+
+def attend_back_kernel(
+    mq_ref, mk_ref, q_ref, k_ref, v_ref, o_ref, g_ref, lse_ref, cos_ref, down_ref, up_ref,
+    out_ref, qs, ks, gs, dq, center, *, block, step,
+):
+    length, width = q_ref.shape
+    pair = pl.program_id(0)
+    win = pl.ds(pl.multiple_of(128 * pair, 128), 256)
+    first, second, _ = window_lanes(pair)
+    both = first | second
+    m0, m1 = as_ones(first), as_ones(second)
+    row = lax.broadcasted_iota(jnp.int32, (8, 256), 0)
+    pick = as_ones(((row == 0) & first) | ((row == 1) & second))
+    for start in range(0, length, 512):
+        rows = pl.ds(start, 512)
+        mq, mk = mq_ref[0, rows, :], mk_ref[0, rows, :]
+        q, k, g = q_ref[rows, win], k_ref[rows, win], g_ref[rows, win]
+        qs[0, rows, :] = q * m0 + mq
+        qs[1, rows, :] = q * m1 + mq
+        ks[0, rows, :] = k * m0 + mk
+        ks[1, rows, :] = k * m1 + mk
+        gs[0, rows, :] = g * m0
+        gs[1, rows, :] = g * m1
+        product = g.astype(f32) * o_ref[rows, win].astype(f32)
+        high = product.astype(bf16)
+        low = (product - high.astype(f32)).astype(bf16)
+        center[:, rows] = mm(pick, high, NT) + mm(pick, low, NT)
+        dq[rows, :] = jnp.zeros((512, 256), f32)
+
+    def turn_back(grad, rows):
+        turned = (
+            pltpu.roll(grad, 256 - HEAD_DIM // 2, 1) * down_ref[rows, win]
+            + pltpu.roll(grad, HEAD_DIM // 2, 1) * up_ref[rows, win]
+        )
+        return grad * cos_ref[rows, win] - turned
+
+    def put(grad, rows, part):
+        to = pl.ds(pl.multiple_of(128 * pair + part * width, 128), 256)
+        out_ref[rows, to] = jnp.where(both, grad, out_ref[rows, to].astype(f32)).astype(bf16)
+
+    for start, low, high in reach(length, block):
+        keys = pl.ds(start, block)
+        v = v_ref[keys, win]
+        dk = dv = None
+        for at in range(low, high, step):
+            rows = pl.ds(at, min(step, high - at))
+            probs, grads = [], []
+            for head in range(2):
+                scores = mm(ks[head, keys, :], qs[head, rows, :], NT)
+                prob_grad = mm(v, gs[head, rows, :], NT)
+                prob = jnp.exp2(scores - lse_ref[0, head : head + 1, rows])
+                probs.append(prob.astype(bf16))
+                grads.append((prob * (prob_grad - center[head : head + 1, rows])).astype(bf16))
+            dv_part = mm(
+                jnp.concatenate(probs, 1),
+                jnp.concatenate([gs[0, rows, :], gs[1, rows, :]], 0),
+                NN,
             )
-            * scale
+            dk_part = mm(
+                jnp.concatenate(grads, 1),
+                jnp.concatenate([qs[0, rows, :], qs[1, rows, :]], 0),
+                NN,
+            )
+            dv = dv_part if dv is None else dv + dv_part
+            dk = dk_part if dk is None else dk + dk_part
+            dq[rows, :] += mm(
+                jnp.concatenate(grads, 0),
+                jnp.concatenate([ks[0, keys, :], ks[1, keys, :]], 0),
+                TN,
+            )
+        put(turn_back(dk * (1.0 / LOG2E), keys), keys, 1)
+        put(dv, keys, 2)
+    for start in range(0, length, 512):
+        rows = pl.ds(start, 512)
+        put(turn_back(dq[rows, :] * HEAD_DIM**-0.5, rows), rows, 0)
+
+
+def attend_back(mq, mk, q, k, v, o, g, lse, tables, block=512, step=1024):
+    length, width = q.shape
+    pairs = width // 128 - 1
+    part = lambda shape: pl.BlockSpec(shape, lambda i: (i, 0, 0))
+    return pl.pallas_call(
+        functools.partial(attend_back_kernel, block=block, step=step),
+        grid=(pairs,),
+        in_specs=[part((1, length, 256))] * 2
+        + [whole((length, width))] * 5
+        + [part((1, 8, length))]
+        + [whole((length, width))] * 3,
+        out_specs=whole((length, 3 * width)),
+        scratch_shapes=[pltpu.VMEM((2, length, 256), bf16)] * 3
+        + [pltpu.VMEM((length, 256), f32), pltpu.VMEM((8, length), f32)],
+        out_shape=jax.ShapeDtypeStruct((length, 3 * width), bf16),
+        compiler_params=pltpu.CompilerParams(vmem_limit_bytes=63 * 2**20),
+        cost_estimate=lasts(47),
+        name="attend_back",
+    )(mq, mk, q, k, v, o, g, lse, *tables)
+
+
+def qkv_kernel(a, w, b, cos, down, up, q, k, v):
+    width = q.shape[1]
+    x = mm(a[...], w[...], NN) + b[...]
+
+    def rotate(part):
+        return (
+            part * cos[...]
+            + pltpu.roll(part, width - HEAD_DIM // 2, 1) * down[...]
+            + pltpu.roll(part, HEAD_DIM // 2, 1) * up[...]
         )
-        value_grad = value_grad + jnp.einsum(
-            "hqk,qhd->khd",
-            probs.astype(jnp.bfloat16),
-            grad_block,
-            preferred_element_type=jnp.float32,
+
+    q[...] = (rotate(x[:, :width]) * (HEAD_DIM**-0.5 * LOG2E)).astype(bf16)
+    k[...] = rotate(x[:, width : 2 * width]).astype(bf16)
+    v[...] = x[:, 2 * width :].astype(bf16)
+
+
+def qkv_rotate(a, w, b, tables, block=512):
+    length, depth = a.shape
+    width = w.shape[1] // 3
+    rows = lambda n: pl.BlockSpec((block, n), lambda i: (i, 0))
+    return pl.pallas_call(
+        qkv_kernel,
+        grid=(length // block,),
+        in_specs=[rows(depth), whole(w.shape), whole(b.shape)] + [rows(width)] * 3,
+        out_specs=[rows(width)] * 3,
+        out_shape=[jax.ShapeDtypeStruct((length, width), bf16)] * 3,
+        compiler_params=ROOMY,
+        cost_estimate=lasts(9),
+        name="qkv_rotate",
+    )(a, w, b, *tables)
+
+
+def hidden_kernel(c, w, b, hidden, slope):
+    pre = mm(c[...], w[...], NN) + b[...]
+    gate = 1.0 / (1.0 + jnp.exp2(pre * (-1.702 * LOG2E)))
+    value = pre * gate
+    hidden[...] = value.astype(bf16)
+    slope[...] = (gate + 1.702 * value * (1.0 - gate)).astype(bf16)
+
+
+def hidden_slope(c, w, b, block=128):
+    length, depth = c.shape
+    units = w.shape[1]
+    rows = lambda n: pl.BlockSpec((block, n), lambda i: (i, 0))
+    return pl.pallas_call(
+        hidden_kernel,
+        grid=(length // block,),
+        in_specs=[rows(depth), whole(w.shape), whole(b.shape)],
+        out_specs=[rows(units)] * 2,
+        out_shape=[jax.ShapeDtypeStruct((length, units), bf16)] * 2,
+        compiler_params=ROOMY,
+        cost_estimate=lasts(7),
+        name="hidden_slope",
+    )(c, w, b)
+
+
+def pre_grad_kernel(g, w, slope, out, bias):
+    grad = (mm(g[...], w[...], NN) * slope[...].astype(f32)).astype(bf16)
+    out[...] = grad
+
+    @pl.when(pl.program_id(0) == 0)
+    def _():
+        bias[...] = jnp.zeros(bias.shape, f32)
+
+    bias[...] += jnp.sum(grad.astype(f32).reshape(-1, 8, grad.shape[1]), axis=0)
+
+
+def pre_grad(g, w, slope, block=256):
+    length, depth = g.shape
+    units = w.shape[1]
+    rows = lambda n: pl.BlockSpec((block, n), lambda i: (i, 0))
+    return pl.pallas_call(
+        pre_grad_kernel,
+        grid=(length // block,),
+        in_specs=[rows(depth), whole(w.shape), rows(units)],
+        out_specs=[rows(units), whole((8, units))],
+        out_shape=[
+            jax.ShapeDtypeStruct((length, units), bf16),
+            jax.ShapeDtypeStruct((8, units), f32),
+        ],
+        compiler_params=ROOMY,
+        cost_estimate=lasts(6),
+        name="pre_grad",
+    )(g, w, slope)
+
+
+def weight_grad_kernel(*refs, count):
+    total = None
+    for left, right in zip(refs[:count], refs[count : 2 * count]):
+        part = mm(left[...], right[...], TN)
+        total = part if total is None else total + part
+    refs[2 * count][...] = total.astype(bf16)
+
+
+def weight_grad(lefts, rights, block=512):
+    count = len(lefts)
+    length, high = lefts[0].shape
+    wide = rights[0].shape[1]
+    if wide % block:
+        block = 384 if wide % 384 == 0 else 128
+    return pl.pallas_call(
+        functools.partial(weight_grad_kernel, count=count),
+        grid=(wide // block,),
+        in_specs=[whole((length, high))] * count
+        + [pl.BlockSpec((length, block), lambda i: (0, i))] * count,
+        out_specs=pl.BlockSpec((high, block), lambda i: (0, i)),
+        out_shape=jax.ShapeDtypeStruct((high, wide), bf16),
+        compiler_params=ROOMY,
+        cost_estimate=lasts(9),
+        name="weight_grad",
+    )(*lefts, *rights)
+
+
+def flip(size, bit):
+    return [(i, i ^ bit) for i in range(size)]
+
+
+def send(value, pairs, axis="dp"):
+    return lax.ppermute(value, axis, pairs)
+
+
+def tie(*values):
+    leaves, tree = jax.tree.flatten(values)
+    return jax.tree.unflatten(tree, lax.optimization_barrier(leaves))
+
+
+def gather_slow(shard, size):
+    ring = size // 4
+    pieces = [shard] + [
+        send(shard, [(i, (i + 4 * step) % size) for i in range(size)]) for step in range(1, ring)
+    ]
+    return jnp.stack(pieces)
+
+
+def gather_near(own, size):
+    return send(own, flip(size, 1)), send(own, flip(size, 2))
+
+
+def gather_far(near, size, cut):
+    return send(near[0][:, :, :cut], flip(size, 2)), send(near[1][:, :, cut:], flip(size, 1))
+
+
+def place_kernel(index_ref, own, fast, second, left, right, out, sem, *, size, cut):
+    index = index_ref[0]
+    high, low = index // 4, index % 4
+    ring, rows = size // 4, own.shape[1]
+    wide = out.shape[1]
+    copies = []
+    for piece, bits, start, stop in (
+        (own, 0, 0, wide), (fast, 1, 0, wide), (second, 2, 0, wide),
+        (left, 3, 0, cut), (right, 3, cut, wide),
+    ):
+        for step in range(ring):
+            block = lax.rem(high - step + ring, ring) * 4 + (low ^ bits)
+            to = out.at[pl.ds(pl.multiple_of(block * rows, rows), rows), pl.ds(start, stop - start)]
+            copies.append(pltpu.make_async_copy(piece.at[step], to, sem.at[len(copies)]))
+    for copy in copies:
+        copy.start()
+    for copy in copies:
+        copy.wait()
+
+
+def place(own, near, far, size):
+    _, rows, wide = own.shape
+    anywhere = pl.BlockSpec(memory_space=pl.ANY)
+    return pl.pallas_call(
+        functools.partial(place_kernel, size=size, cut=far[0].shape[2]),
+        in_specs=[pl.BlockSpec(memory_space=pltpu.SMEM)] + [anywhere] * 5,
+        out_specs=pl.BlockSpec(memory_space=pltpu.VMEM),
+        scratch_shapes=[pltpu.SemaphoreType.DMA((5 * size // 4,))],
+        out_shape=jax.ShapeDtypeStruct((rows * size, wide), bf16),
+        compiler_params=pltpu.CompilerParams(vmem_limit_bytes=24 * 2**20),
+        cost_estimate=lasts(1),
+        name="place",
+    )(lax.axis_index("dp").reshape(1), own, *near, *far)
+
+
+def split_grad_kernel(*refs, count, size):
+    index = refs[0][0]
+    lefts, rights = refs[1 : 1 + count], refs[1 + count : 1 + 2 * count]
+    outs, result = refs[1 + 2 * count : 5 + 2 * count], refs[5 + 2 * count]
+    total = None
+    for left, right in zip(lefts, rights):
+        part = mm(left[...], right[...], TN)
+        total = part if total is None else total + part
+    result[...] = total.astype(bf16)
+    high, low = index // 4, index % 4
+    ring, rows = size // 4, outs[0].shape[1]
+    for bits in range(4):
+        for step in range(ring):
+            block = lax.rem(high + step, ring) * 4 + (low ^ bits)
+            outs[bits][step] = result[pl.ds(pl.multiple_of(block * rows, rows), rows), :]
+
+
+def split_grad(lefts, rights, size, block=512):
+    count = len(lefts)
+    length, high = lefts[0].shape
+    wide = rights[0].shape[1]
+    ring, rows = size // 4, high // size
+    return pl.pallas_call(
+        functools.partial(split_grad_kernel, count=count, size=size),
+        grid=(pl.cdiv(wide, block),),
+        in_specs=[pl.BlockSpec(memory_space=pltpu.SMEM)]
+        + [whole((length, high))] * count
+        + [pl.BlockSpec((length, block), lambda i: (0, i))] * count,
+        out_specs=[pl.BlockSpec((ring, rows, block), lambda i: (0, 0, i))] * 4,
+        out_shape=[jax.ShapeDtypeStruct((ring, rows, wide), bf16)] * 4,
+        scratch_shapes=[pltpu.VMEM((high, block), bf16)],
+        compiler_params=ROOMY,
+        cost_estimate=lasts(9),
+        name="split_grad",
+    )(lax.axis_index("dp").reshape(1), *lefts, *rights)
+
+
+def add_low(*parts):
+    total = parts[0].astype(f32)
+    for part in parts[1:]:
+        total = total + part.astype(f32)
+    return total.astype(bf16)
+
+
+def scatter_far(stacks, size, cut):
+    far = stacks[3]
+    return send(far[:, :, :cut], flip(size, 2)), send(far[:, :, cut:], flip(size, 1))
+
+
+def scatter_near(stacks, got, size):
+    left, right = got
+    cut = left.shape[2]
+    fast = jnp.concatenate([add_low(stacks[1][:, :, :cut], left), stacks[1][:, :, cut:]], axis=2)
+    second = jnp.concatenate([stacks[2][:, :, :cut], add_low(stacks[2][:, :, cut:], right)], axis=2)
+    return send(fast, flip(size, 1)), send(second, flip(size, 2))
+
+
+def scatter_slow(stacks, got, size):
+    total = add_low(stacks[0], *got)
+    return total[0], [
+        send(total[step], [(i, (i + 4 * step) % size) for i in range(size)])
+        for step in range(1, size // 4)
+    ]
+
+
+def scatter_last(own, got):
+    return sum((part.astype(f32) for part in got), own.astype(f32))
+
+
+def sum_everywhere(value, size):
+    for bit in [1 << i for i in range(size.bit_length() - 1)]:
+        value = value + send(value, flip(size, bit))
+    return value + send(value, [(0, 1), (1, 0)], "tensor")
+
+
+def on_device(
+    size,
+    tokens,
+    cotangent,
+    picture_ids,
+    positions,
+    valid,
+    norm1_gain,
+    norm1_bias,
+    qkv_weight,
+    qkv_bias,
+    proj_weight,
+    proj_bias,
+    norm2_gain,
+    norm2_bias,
+    fc1_weight,
+    fc1_bias,
+    fc2_weight,
+    fc2_bias,
+):
+    me = lax.axis_index("tensor")
+    length = picture_ids.shape[0]
+    half, model = tokens.shape
+    rows = qkv_weight.shape[0]
+    width = qkv_weight.shape[2]
+    units = fc1_weight.shape[1]
+    swap = [(0, 1), (1, 0)]
+    cross = lambda value: send(value, swap, "tensor")
+    mine = lambda value: lax.dynamic_slice_in_dim(value, me * half, half, 0)
+    theirs = lambda value: lax.dynamic_slice_in_dim(value, (1 - me) * half, half, 0)
+
+    def in_order(own, other):
+        return jnp.where(
+            me == 0, jnp.concatenate([own, other], 0), jnp.concatenate([other, own], 0)
         )
-        return ((key_grad, value_grad), query_grad)
-
-    zeros = jnp.zeros(keys.shape, jnp.float32)
-    (key_grad, value_grad), query_grads = lax.scan(
-        one_block, (zeros, zeros), jnp.arange(length // block)
-    )
-    return (query_grads.reshape(queries.shape), key_grad, value_grad)
-
-
-def on_device(
+
+    gain_one, shift_one = norm1_gain.astype(f32), norm1_bias.astype(f32)
+    gain_two, shift_two = norm2_gain.astype(f32), norm2_bias.astype(f32)
+    qkv_shift = lax.dynamic_slice_in_dim(qkv_bias.astype(f32), me * width, width, 1).reshape(1, -1)
+    fc1_shift = lax.dynamic_slice_in_dim(fc1_bias.astype(f32), me * units, units, 0).reshape(1, -1)
+
+    qkv_cut, cut, fc1_cut, fc2_cut = 1024, 1664, 1280, 1280
+    inputs = tokens.astype(f32)
+    unit_one, inverse_one = norm_parts(inputs)
+    normed_own = (unit_one * gain_one + shift_one).astype(bf16)
+    attn_in = in_order(normed_own, cross(normed_own))
+    tables = rope_tables(positions, width)
+    mq, mk = mask_lanes(picture_ids, valid, width // 128 - 1)
+
+    qkv_own = gather_slow(qkv_weight.reshape(rows, 3 * width), size)
+    joined = jnp.concatenate([proj_weight.T, fc1_weight], axis=1)
+    qkv_own, joined = tie(qkv_own, joined)
+    qkv_near = gather_near(qkv_own, size)
+    own = gather_slow(joined, size)
+    qkv_near, attn_in = tie(qkv_near, attn_in)
+    qkv_far = gather_far(qkv_near, size, qkv_cut)
+    qkv_far, own, tables = tie(qkv_far, own, tables)
+    near = gather_near(own, size)
+    qkv_full = place(qkv_own, qkv_near, qkv_far, size)
+    q, k, v = qkv_rotate(attn_in, qkv_full, qkv_shift, tables)
+    pairs = mq.shape[0]
+    fc2_shard, q, mq = tie(fc2_weight.T, q, mq)
+    fc2_own = gather_slow(fc2_shard, size)
+    mixed, lse_low = attend(mq, mk, q, k, v, 0, pairs // 2)
+    near, mixed = tie(near, mixed)
+    far = gather_far(near, size, cut)
+    mixed, lse_high = attend(mq, mk, q, k, v, pairs // 2, pairs - pairs // 2, (mixed,))
+    far, fc2_own, mixed = tie(far, fc2_own, mixed)
+    fc2_near = gather_near(fc2_own, size)
+    joined = place(own, near, far, size)
+    proj_turned, fc1_full = joined[:, :width], joined[:, width:]
+
+    away = cross(mm(theirs(mixed), proj_turned, NT).astype(bf16))
+    attn_out = mm(mine(mixed), proj_turned, NT) + away.astype(f32)
+    middle = inputs + (attn_out + proj_bias.astype(f32))
+    unit_two, inverse_two = norm_parts(middle)
+    c_own = (unit_two * gain_two + shift_two).astype(bf16)
+    grad_other = cross(cotangent)
+    c_other = cross(c_own)
+    hidden_own, slope_own = hidden_slope(c_own, fc1_full, fc1_shift)
+    fc2_near, hidden_own = tie(fc2_near, hidden_own)
+    fc2_far = gather_far(fc2_near, size, fc2_cut)
+    hidden_other, slope_other = hidden_slope(c_other, fc1_full, fc1_shift)
+
+    fc2_stacks = split_grad([cotangent, grad_other], [hidden_own, hidden_other], size)
+    fc2_far, fc2_stacks = tie(fc2_far, fc2_stacks)
+    fc2_got = scatter_far(fc2_stacks, size, fc2_cut)
+    fc2_turned = place(fc2_own, fc2_near, fc2_far, size)
+    pre_other, bias_other = pre_grad(grad_other, fc2_turned, slope_other)
+    fc2_got, pre_other = tie(fc2_got, pre_other)
+    fc2_got = scatter_near(fc2_stacks, fc2_got, size)
+    pre_own, bias_own = pre_grad(cotangent, fc2_turned, slope_own)
+    fc1_stacks = split_grad([c_own, c_other], [pre_own, pre_other], size)
+    fc2_got, fc1_stacks, pre_other, pre_own = tie(fc2_got, fc1_stacks, pre_other, pre_own)
+    fc2_kept, fc2_got = scatter_slow(fc2_stacks, fc2_got, size)
+    fc1_got = scatter_far(fc1_stacks, size, fc1_cut)
+    away = cross(mm(pre_other, fc1_full, NT).astype(bf16))
+    normed_two_grad = mm(pre_own, fc1_full, NT) + away.astype(f32)
+
+    out_grad = cotangent.astype(f32)
+    fc2_shift_grad = jnp.sum(out_grad, axis=0)
+    middle_part, gain_two_grad, shift_two_grad = norm_backward(
+        normed_two_grad, unit_two, inverse_two, gain_two
+    )
+    middle_grad = out_grad + middle_part
+    attn_grad_own = middle_grad.astype(bf16)
+    proj_shift_grad = jnp.sum(attn_grad_own.astype(f32), axis=0)
+    fc1_got, attn_grad_own = tie(fc1_got, attn_grad_own)
+    attn_grad_other = cross(attn_grad_own)
+    fc1_got = scatter_near(fc1_stacks, fc1_got, size)
+    attn_grad = in_order(attn_grad_own, attn_grad_other)
+    mixed_grad = mm(attn_grad, proj_turned, NN).astype(bf16)
+    proj_grad = weight_grad([attn_grad], [mixed])
+    fc1_got, fc2_got, mixed_grad, proj_grad = tie(fc1_got, fc2_got, mixed_grad, proj_grad)
+    fc2_shard = scatter_last(fc2_kept, fc2_got)
+    fc1_kept, fc1_got = scatter_slow(fc1_stacks, fc1_got, size)
+    proj_shard = lax.psum_scatter(proj_grad, "dp", scatter_dimension=0, tiled=True).astype(f32)
+    lse = jnp.concatenate([lse_low, lse_high], axis=0)
+    mixed_grad, fc2_shard, fc1_kept = tie(mixed_grad, fc2_shard, fc1_kept)
+    qkv_grad = attend_back(mq, mk, q, k, v, mixed, mixed_grad, lse, tables)
+    fc1_got, proj_shard, qkv_grad = tie(fc1_got, proj_shard, qkv_grad)
+    fc1_shard = scatter_last(fc1_kept, fc1_got)
+    qkv_stacks = split_grad([attn_in], [qkv_grad], size)
+    qkv_stacks, qkv_grad = tie(qkv_stacks, qkv_grad)
+    qkv_got = scatter_far(qkv_stacks, size, qkv_cut)
+    part = mm(theirs(qkv_grad), qkv_full, NT).astype(bf16)
+    qkv_got, part = tie(qkv_got, part)
+    qkv_got = scatter_near(qkv_stacks, qkv_got, size)
+    normed_one_grad = mm(mine(qkv_grad), qkv_full, NT) + cross(part).astype(f32)
+    qkv_shift_grad = jnp.sum(qkv_grad.astype(f32), axis=0)
+    input_part, gain_one_grad, shift_one_grad = norm_backward(
+        normed_one_grad, unit_one, inverse_one, gain_one
+    )
+    input_grad = middle_grad + input_part
+
+    input_grad, hidden_other = tie(input_grad, hidden_other)
+    part = mm(hidden_other, fc2_turned, NT).astype(bf16)
+    qkv_got, part = tie(qkv_got, part)
+    qkv_kept, qkv_got = scatter_slow(qkv_stacks, qkv_got, size)
+    output = (
+        middle + (mm(hidden_own, fc2_turned, NT) + cross(part).astype(f32)) + fc2_bias.astype(f32)
+    )
+    qkv_shard = scatter_last(qkv_kept, qkv_got)
+
+    fc1_shift_grad = jnp.sum(bias_own, axis=0) + jnp.sum(bias_other, axis=0)
+    fc1_place = lax.dynamic_update_slice_in_dim(
+        jnp.zeros((2 * units,), f32), fc1_shift_grad, me * units, 0
+    )
+    qkv_place = lax.dynamic_update_slice_in_dim(
+        jnp.zeros((3, 2 * width), f32), qkv_shift_grad.reshape(3, width), me * width, 1
+    )
+    sums = [
+        gain_one_grad, shift_one_grad, qkv_place.reshape(-1), proj_shift_grad,
+        gain_two_grad, shift_two_grad, fc1_place, fc2_shift_grad,
+    ]
+    totals = sum_everywhere(jnp.concatenate(sums).reshape(-1, 128), size).reshape(-1)
+    small = []
+    for part in sums:
+        small.append(totals[: part.shape[0]])
+        totals = totals[part.shape[0] :]
+    return (
+        output,
+        input_grad,
+        small[0],
+        small[1],
+        qkv_shard.reshape(rows, 3, width),
+        small[2].reshape(3, 2 * width),
+        proj_shard.T,
+        small[3],
+        small[4],
+        small[5],
+        fc1_shard,
+        small[6],
+        fc2_shard.T,
+        small[7],
+    )
+
+
+def norm_forward(values, gain, shift):
+    center = values - jnp.mean(values, axis=-1, keepdims=True)
+    inverse = lax.rsqrt(jnp.mean(center * center, axis=-1, keepdims=True) + EPS)
+    unit = center * inverse
+    return (unit * gain + shift, unit, inverse)
+
+
+def on_any(
     tokens,
     cotangent,
     picture_ids,
@@ -164,13 +757,22 @@
     attn_in = lax.all_gather(normed_one.astype(jnp.bfloat16), "tensor", axis=0, tiled=True)
     total_rows = attn_in.shape[0]
     qkv_raw = jnp.dot(attn_in, qkv_matrix, preferred_element_type=jnp.float32) + qkv_shift
-    split = qkv_raw.reshape(total_rows, 3, local_heads, HEAD_DIM)
-    cosine, sine = rope_tables(positions)
-    queries = rotate(split[:, 0], cosine, sine).astype(jnp.bfloat16)
-    keys = rotate(split[:, 1], cosine, sine).astype(jnp.bfloat16)
-    values = split[:, 2].astype(jnp.bfloat16)
-    mixed_row, logsum_row = attend_row(queries, keys, values, picture_ids, valid)
-    attn_mixed = mixed_row.reshape(total_rows, local_width)
+    pairs = -(-local_heads // 2)
+    padded = 128 * (pairs + 1)
+    fill = lambda value: jnp.pad(value, ((0, 0), (0, padded - local_width)))
+    tables = [fill(table) for table in rope_tables(positions, local_width)]
+    mq, mk = mask_lanes(picture_ids, valid, pairs)
+
+    def rotate(part):
+        turned = jnp.roll(part, -HEAD_DIM // 2, 1) * tables[1]
+        return part * tables[0] + turned + jnp.roll(part, HEAD_DIM // 2, 1) * tables[2]
+
+    split = [fill(part) for part in jnp.split(qkv_raw, 3, axis=1)]
+    queries = (rotate(split[0]) * (HEAD_DIM**-0.5 * LOG2E)).astype(jnp.bfloat16)
+    keys = rotate(split[1]).astype(jnp.bfloat16)
+    values = split[2].astype(jnp.bfloat16)
+    mixed_row, logsum_row = attend(mq, mk, queries, keys, values)
+    attn_mixed = mixed_row[:, :local_width]
     piece = attn_mixed
     attn_out = lax.psum_scatter(
         jnp.dot(piece, proj_full, preferred_element_type=jnp.float32).astype(jnp.bfloat16),
@@ -226,16 +828,12 @@
     mixed_grad = jnp.dot(attn_grad_full, proj_back.T, preferred_element_type=jnp.float32).astype(
         jnp.bfloat16
     )
-    mixed_grad = mixed_grad.reshape(total_rows, local_heads, HEAD_DIM)
-    query_grad, key_grad, value_grad = attend_back(
-        queries, keys, values, picture_ids, valid, mixed_grad, logsum_row
-    )
-    query_pre = rotate_back(query_grad, cosine, sine)
-    key_pre = rotate_back(key_grad, cosine, sine)
-    qkv_grad = jnp.stack([query_pre, key_pre, value_grad], axis=1).reshape(
-        total_rows, 3 * local_width
-    )
-    qkv_grad = qkv_grad.astype(jnp.bfloat16)
+    qkv_grad = attend_back(
+        mq, mk, queries, keys, values, mixed_row, fill(mixed_grad), logsum_row, tables
+    )
+    qkv_grad = jnp.concatenate(
+        [qkv_grad[:, at : at + local_width] for at in (0, padded, 2 * padded)], axis=1
+    )
     qkv_shift_grad = jnp.sum(qkv_grad.astype(jnp.float32), axis=0)
     qkv_grad_weight = jnp.dot(attn_in.T, qkv_grad, preferred_element_type=jnp.float32)
     qkv_grad_weight = qkv_grad_weight.reshape(model_width, 3, local_width)
@@ -305,8 +903,10 @@
 
 
 def solution(mesh):
+    size = mesh.shape["dp"]
+    paired = mesh.shape["tensor"] == 2 and size == 16
     return jax.shard_map(
-        on_device,
+        functools.partial(on_device, size) if paired else on_any,
         mesh=mesh,
         in_specs=(
             P(("dp", "tensor"), None),

time: 1720 us -> 706 us (0.41)
  matrix products: 647 us -> 109 us
  waiting for transfers between devices: 573 us -> 105 us
  Pallas kernels: 0 us -> 285 us
  other arithmetic: 274 us -> 78.6 us
  local copies, waits for them, and re-layouts: 188 us -> 43.2 us
  starting transfers between devices: 0.86 us -> 56.4 us
    dot_general x40 -> x12, matrix products: 647 us -> 109 us  [the longest x9 87.9 us: mm(): return lax.dot_general(left, right, dims, preferred_element_type=f32)]
    pallas_call x0 -> x15, Pallas kernels: none -> 285 us  [the longest x1 94.1 us: attend_back(): pl.pallas_call(functools.partial(attend_back_kernel, block=block, step=st...]
    all_gather x8 -> x0, waiting for transfers between devices: 280 us -> none  [the longest x1 92.3 us: on_device(): lax.all_gather(fc2_weight, 'dp', axis=1, tiled=True)]
    reduce_scatter x8 -> x1, waiting for transfers between devices: 166 us -> 0.02 us  [on_device(): lax.psum_scatter(proj_grad, 'dp', scatter_dimension=0, tiled=True)]
    psum x1 -> x0, waiting for transfers between devices: 124 us -> none  [on_device(): lax.psum((gain_one_grad, shift_one_grad, qkv_shift_full, proj_shift_grad,...]
    dynamic_update_slice x10 -> x1, local copies, waits for them, and re-layouts: 115 us -> 0.02 us  [on_device(): lax.dynamic_update_slice_in_dim(jnp.zeros((3, 2 * width), f32), qkv_shift...]
    convert_element_type x20 -> x22, other arithmetic: 135 us -> 23.7 us  [the longest x9 12.6 us: add_low(): return total.astype(bf16)]
    ppermute x0 -> x55, waiting for transfers between devices: none -> 105 us  [send(): return lax.ppermute(value, axis, pairs)]
  transfers between devices with their start and end apart: 17 -> 56, of which waited for: 11 -> 24; matrix products, arithmetic and copies ran while one was open for 59% -> 24% of each run, Pallas kernels for 0% -> 38%
where the time goes in v1:
time: 706 us; the launch traced here: 693 us
  Pallas kernels  285 us (40%)
  matrix products  109 us (15%)
  waiting for transfers between devices  105 us (15%)
  other arithmetic  78.6 us (11%)
  starting transfers between devices  56.4 us (8%)
  local copies, waits for them, and re-layouts  43.2 us (6%)
  between operations  15.6 us (2%)
    ppermute x55, waiting for transfers between devices, send(): return lax.ppermute(value, axis, pairs)  105 us
    pallas_call x1, Pallas kernels, attend_back(): pl.pallas_call(functools.partial(attend_back_kernel, block=block, step=st...  94.1 us
    dot_general x9, matrix products, mm(): return lax.dot_general(left, right, dims, preferred_element_type=f32)  87.9 us
    ppermute x55, starting transfers between devices, send(): return lax.ppermute(value, axis, pairs)  56.4 us
    pallas_call x3, Pallas kernels, split_grad(): pl.pallas_call(functools.partial(split_grad_kernel, count=count, size=siz...  55.5 us
    pallas_call x2, Pallas kernels, attend(): pl.pallas_call(functools.partial(attend_kernel, block=block, begin=begin)...  45 us
    pallas_call x2, Pallas kernels, hidden_slope(): pl.pallas_call(hidden_kernel, grid=(length // block,), in_specs=[rows(dep...  27.1 us
    pallas_call x2, Pallas kernels, pre_grad(): pl.pallas_call(pre_grad_kernel, grid=(length // block,), in_specs=[rows(d...  25.7 us
  transfers between devices with their start and end apart: 56, of which 24 were waited for; matrix products, arithmetic and copies ran while one was open for 24% of the time, Pallas kernels for 38%

profile of v1, /device:TPU:8, one launch (start us, length us, event | category | flops | bytes accessed | tf_op | source)
XLA Modules:
  0.0 693.3 jit_solution(5055687272597065555)
XLA Ops:
  73.2 6.9 fusion.38.down.down_ref
  83.2 18.1 %collective-permute-done.9 = bf16[80,3200]{1,0:T(8,128)(2,1)} collective-permute-done((bf16[80,3200]{1,0:T(8,128)(2,1)}, bf16[80,3200]{1,0:T(8,128)(2,1)}, u32[]{:S(2)}, u32[]{:S(2)}) %collective-permute-start.9) | collective-permute-done | bytes 512032 | tf_op jit(solution)/shard_map/ppermute | solution.py:395
  111.1 17.5 %qkv_rotate.1 = (bf16[2048,640]{1,0:T(8,128)(2,1)}, bf16[2048,640]{1,0:T(8,128)(2,1)}, bf16[2048,640]{1,0:T(8,128)(2,1)}) custom-call(bf16[2048,1280]{1,0:T(8,128)(2,1)} %maximum_select_fusion.a.refs_1_, bf16[1280,1920]{1,0:T(8,128)(2,1)} %copy-done.2, f32[1,1920]{1,0:T(1,128)} %bitcast.109, f32[2048,640]{1,0:T(8,128)} %fusion.33.cos.cos_ref, ...), custom_call_target="tpu_custom_call" | custom-call | flops 9900000256 | bytes 1 | tf_op jit(solution)/shard_map/qkv_rotate/pallas_call | solution.py:297
  133.2 21.5 %attend.2 = (bf16[2048,640]{1,0:T(8,128)(2,1)}, f32[2,8,2048]{2,1,0:T(8,128)}) custom-call(bf16[4,2048,256]{2,1,0:T(8,128)(2,1)} %get-tuple-element.125.refs_0_.mq_ref, bf16[4,2048,256]{2,1,0:T(8,128)(2,1)} %get-tuple-element.288.refs_1_.mk_ref, bf16[2048,640]{1,0:T(8,128)(2,1)} %get-tuple-element.126.refs_2_.q_ref, ...), custom_call_target="tpu_custom_call" | custom-call | flops 11000000512 | bytes 1 | tf_op jit(solution)/shard_map/attend/pallas_call | solution.py:162
  171.3 23.4 %attend.3 = (bf16[2048,640]{1,0:T(8,128)(2,1)}, f32[2,8,2048]{2,1,0:T(8,128)}) custom-call(bf16[4,2048,256]{2,1,0:T(8,128)(2,1)} %get-tuple-element.125.refs_0_.mq_ref, bf16[4,2048,256]{2,1,0:T(8,128)(2,1)} %get-tuple-element.288.refs_1_.mk_ref, bf16[2048,640]{1,0:T(8,128)(2,1)} %get-tuple-element.126.refs_2_.q_ref, ...), custom_call_target="tpu_custom_call" | custom-call | flops 11000000512 | bytes 1 | tf_op jit(solution)/shard_map/attend/pallas_call | solution.py:162
  226.8 13.5 %hidden_slope.2 = (bf16[1024,2560]{1,0:T(8,128)(2,1)}, bf16[1024,2560]{1,0:T(8,128)(2,1)}) custom-call(bf16[1024,1280]{1,0:T(8,128)(2,1)} %add_convert_fusion.c.refs_1_, bf16[1280,2560]{1,0:T(8,128)(2,1)} %slice.246.w, f32[1,2560]{1,0:T(1,128)} %reshape.268.b), custom_call_target="tpu_custom_call" | custom-call | flops 7699999744 | bytes 1 | tf_op jit(solution)/shard_map/hidden_slope/pallas_call | solution.py:321
  240.3 15.6 %collective-permute-done.19.fast = bf16[4,80,2560]{2,1,0:T(8,128)(2,1)} collective-permute-done((bf16[4,80,2560]{2,1,0:T(8,128)(2,1)S(1)}, bf16[4,80,2560]{2,1,0:T(8,128)(2,1)}, u32[]{:S(2)}, u32[]{:S(2)}) %collective-permute-start.19) | collective-permute-done | bytes 1638432 | tf_op jit(solution)/shard_map/ppermute | solution.py:395
  263.3 13.6 %hidden_slope.3 = (bf16[1024,2560]{1,0:T(8,128)(2,1)}, bf16[1024,2560]{1,0:T(8,128)(2,1)}) custom-call(bf16[1024,1280]{1,0:T(8,128)(2,1)} %collective-permute-done.24.c.refs_2_, bf16[1280,2560]{1,0:T(8,128)(2,1)} %slice.246.w, f32[1,2560]{1,0:T(1,128)} %reshape.268.b), custom_call_target="tpu_custom_call" | custom-call | flops 7699999744 | bytes 1 | tf_op jit(solution)/shard_map/hidden_slope/pallas_call | solution.py:321
  276.9 19.4 %split_grad.3 = (bf16[4,80,2560]{2,1,0:T(8,128)(2,1)}, bf16[4,80,2560]{2,1,0:T(8,128)(2,1)}, bf16[4,80,2560]{2,1,0:T(8,128)(2,1)}, bf16[4,80,2560]{2,1,0:T(8,128)(2,1)}) custom-call(s32[1]{0:T(128)} %bitcast.11.index_ref.refs_0_, bf16[1024,1280]{1,0:T(8,128)(2,1)} %g.1, bf16[1024,1280]{1,0:T(8,128)(2,1)} %collective-permute-done.23.refs_2_.g, ...), custom_call_target="tpu_custom_call" | custom-call | flops 9900000256 | bytes 1 | tf_op jit(solution)/shard_map/split_grad/pallas_call | solution.py:476
  309.4 12.9 %pre_grad.2 = (bf16[1024,2560]{1,0:T(8,128)(2,1)}, f32[8,2560]{1,0:T(8,128)}) custom-call(bf16[1024,1280]{1,0:T(8,128)(2,1)} %collective-permute-done.23.refs_2_.g, bf16[1280,2560]{1,0:T(8,128)(2,1)} %copy-done.1, bf16[1024,2560]{1,0:T(8,128)(2,1)} %get-tuple-element.152.slope), custom_call_target="tpu_custom_call" | custom-call | flops 6600000000 | bytes 1 | tf_op jit(solution)/shard_map/pre_grad/pallas_call | solution.py:348
  331.2 12.7 %pre_grad.3 = (bf16[1024,2560]{1,0:T(8,128)(2,1)}, f32[8,2560]{1,0:T(8,128)}) custom-call(bf16[1024,1280]{1,0:T(8,128)(2,1)} %g.1, bf16[1280,2560]{1,0:T(8,128)(2,1)} %copy-done.1, bf16[1024,2560]{1,0:T(8,128)(2,1)} %get-tuple-element.157.slope), custom_call_target="tpu_custom_call" | custom-call | flops 6600000000 | bytes 1 | tf_op jit(solution)/shard_map/pre_grad/pallas_call | solution.py:348
  343.9 19.5 %split_grad.4 = (bf16[4,80,2560]{2,1,0:T(8,128)(2,1)}, bf16[4,80,2560]{2,1,0:T(8,128)(2,1)}, bf16[4,80,2560]{2,1,0:T(8,128)(2,1)}, bf16[4,80,2560]{2,1,0:T(8,128)(2,1)}) custom-call(s32[1]{0:T(128)} %bitcast.11.index_ref.refs_0_, bf16[1024,1280]{1,0:T(8,128)(2,1)} %add_convert_fusion.c.refs_1_, bf16[1024,1280]{1,0:T(8,128)(2,1)} %collective-permute-done.24.c.refs_2_, ...), custom_call_target="tpu_custom_call" | custom-call | flops 9900000256 | bytes 1 | tf_op jit(solution)/shard_map/split_grad/pallas_call | solution.py:476
  365.5 11.0 %convolution_convert_fusion.2 = bf16[1024,1280]{1,0:T(8,128)(2,1)S(1)} fusion(bf16[1024,2560]{1,0:T(8,128)(2,1)} %get-tuple-element.168.refs_4_, bf16[1280,3200]{1,0:T(8,128)(2,1)} %copy-done), kind=kOutput, calls=%fused_computation.45 | convolution fusion | flops 6712197120 | bytes 14417920 | tf_op jit(solution)/shard_map/dot_general | solution.py:30
  381.6 12.5 %multiply_reduce_fusion = (f32[1280]{0:T(1024)S(1)}, f32[1024]{0:T(1024)S(1)}, f32[1024]{0:T(1024)S(1)}, f32[1280]{0:T(1024)S(1)}, f32[1024,1280]{1,0:T(8,128)S(1)}) fusion(f32[1024,1280]{1,0:T(8,128)S(1)} %bitcast.90, f32[1024]{0:T(1024)S(1)} %add_rsqrt_fusion, f32[1024]{0:T(1024)S(1)} %broadcast_multiply_fusion.6, f32[1280]{0:T(1024)S(1)} %convert_element_type.251, ...), kind=kOutput, calls=%fused_computation.28 | convolution fusion | flops 6725300224 | bytes 24935424 | tf_op jit(solution)/shard_map/dot_general | solution.py:30
  412.9 9.4 %maximum_select_fusion.1.refs_0_ = bf16[2048,1280]{1,0:T(8,128)(2,1)} fusion(bf16[1024,1280]{1,0:T(8,128)(2,1)S(1)} %collective-permute-done.37, bf16[1024,1280]{1,0:T(8,128)(2,1)S(1)} %get-tuple-element.175, pred[]{:T(512)S(6)} %eq.78), kind=kLoop, calls=%fused_computation.27 | loop fusion | flops 23592960 | bytes 10485761 | tf_op jit(solution)/shard_map/jit(_where)/select_n | solution.py:561
  422.4 11.4 %weight_grad.1 = bf16[1280,640]{1,0:T(8,128)(2,1)} custom-call(bf16[2048,1280]{1,0:T(8,128)(2,1)} %maximum_select_fusion.1.refs_0_, bf16[2048,640]{1,0:T(8,128)(2,1)} %get-tuple-element.135.refs_1_.o_ref), custom_call_target="tpu_custom_call" | custom-call | flops 9900000256 | bytes 1 | tf_op jit(solution)/shard_map/weight_grad/pallas_call | solution.py:377
  433.8 8.8 %convolution_convert_fusion.3.g_ref = bf16[2048,640]{1,0:T(8,128)(2,1)} fusion(bf16[2048,1280]{1,0:T(8,128)(2,1)} %maximum_select_fusion.1.refs_0_, bf16[1280,3200]{1,0:T(8,128)(2,1)} %copy-done), kind=kOutput, calls=%fused_computation.48 | convolution fusion | flops 3356753920 | bytes 9502720 | tf_op jit(solution)/shard_map/dot_general | solution.py:30
  458.1 94.1 %attend_back.1.refs_2_ = bf16[2048,1920]{1,0:T(8,128)(2,1)} custom-call(bf16[4,2048,256]{2,1,0:T(8,128)(2,1)} %get-tuple-element.125.refs_0_.mq_ref, bf16[4,2048,256]{2,1,0:T(8,128)(2,1)} %get-tuple-element.288.refs_1_.mk_ref, bf16[2048,640]{1,0:T(8,128)(2,1)} %get-tuple-element.126.refs_2_.q_ref, bf16[2048,640]{1,0:T(8,128)(2,1)} %get-tuple-element.127.refs_3_.k_ref, ...), custom_call_target="tpu_custom_call" | custom-call | flops 51699998720 | bytes 1 | tf_op jit(solution)/shard_map/attend_back/pallas_call | solution.py:260
  553.9 16.5 %split_grad.5 = (bf16[4,80,1920]{2,1,0:T(8,128)(2,1)}, bf16[4,80,1920]{2,1,0:T(8,128)(2,1)}, bf16[4,80,1920]{2,1,0:T(8,128)(2,1)}, bf16[4,80,1920]{2,1,0:T(8,128)(2,1)}) custom-call(s32[1]{0:T(128)} %bitcast.11.index_ref.refs_0_, bf16[2048,1280]{1,0:T(8,128)(2,1)} %maximum_select_fusion.a.refs_1_, bf16[2048,1920]{1,0:T(8,128)(2,1)} %attend_back.1.refs_2_), custom_call_target="tpu_custom_call" | custom-call | flops 9900000256 | bytes 1 | tf_op jit(solution)/shard_map/split_grad/pallas_call | solution.py:476
  575.7 9.9 %fusion.21 = bf16[1024,1280]{1,0:T(8,128)(2,1)} fusion(bf16[1280,1920]{1,0:T(8,128)(2,1)} %copy-done.2, bf16[2048,1920]{1,0:T(8,128)(2,1)} %attend_back.1.refs_2_, s32[]{:T(128)S(6)} %select_n.125), kind=kOutput, calls=%fused_computation.43 | convolution fusion | flops 5034475520 | bytes 11468804 | tf_op jit(solution)/shard_map/dot_general | solution.py:30
  602.2 10.6 %fusion.16 = (f32[1280]{0:T(1024)S(1)}, f32[1024]{0:T(1024)S(1)}, f32[1024]{0:T(1024)S(1)}, f32[1280]{0:T(1024)S(1)}, f32[1024,1280]{1,0:T(8,128)}) fusion(bf16[1024,1280]{1,0:T(8,128)(2,1)S(1)} %copy-done.5, f32[1024]{0:T(1024)S(1)} %copy-done.40, f32[1024]{0:T(1024)S(1)} %copy-done.38, f32[1280]{0:T(1024)S(1)} %copy-done.36, ...), kind=kOutput, calls=%fused_computation.24 | convolution fusion | flops 5048889344 | bytes 19364868 | tf_op jit(solution)/shard_map/dot_general | solution.py:30
  619.4 10.0 %convolution_convert_fusion.1 = bf16[1024,1280]{1,0:T(8,128)(2,1)} fusion(bf16[1024,2560]{1,0:T(8,128)(2,1)} %get-tuple-element.198.refs_4_, bf16[1280,2560]{1,0:T(8,128)(2,1)S(1)} %bitcast.86), kind=kOutput, calls=%fused_computation.44 | convolution fusion | flops 6712197120 | bytes 14417920 | tf_op jit(solution)/shard_map/dot_general | solution.py:30
  648.0 18.0 %collective-permute-done.50 = f32[130,128]{1,0:T(8,128)S(1)} collective-permute-done((f32[130,128]{1,0:T(8,128)S(1)}, f32[130,128]{1,0:T(8,128)S(1)}, u32[]{:S(2)}, u32[]{:S(2)}) %collective-permute-start.50) | collective-permute-done | bytes 66592 | tf_op jit(solution)/shard_map/ppermute | solution.py:395
  671.1 15.0 %add_add_fusion = f32[1024,1280]{1,0:T(8,128)} fusion(f32[1024,1280]{1,0:T(8,128)} %copy-done.3, bf16[1024,1280]{1,0:T(8,128)(2,1)} %collective-permute-done.46, bf16[1024,2560]{1,0:T(8,128)(2,1)} %get-tuple-element.140.refs_3_, bf16[1280,2560]{1,0:T(8,128)(2,1)} %copy-done.1, f32[1280]{0:T(1024)S(1)} %convert_element_type.296), kind=kOutput, calls=%fused_computation.30 | convolution fusion | flops 6716129280 | bytes 24908800 | tf_op jit(solution)/shard_map/dot_general | solution.py:30
  (354 shorter events, 255.6 us)
Async XLA Ops:
  7.2 545.1 %reduce-scatter.2.cloned.1.call-start = ((), (), s32[]{:S(2)}) async-start(), calls=%async_computation.1 | async-start | bytes 1740800 | tf_op jit(solution)/shard_map/reduce_scatter | solution.py:645
  19.4 39.4 %collective-permute-start.5 = (bf16[1024,1280]{1,0:T(8,128)(2,1)}, bf16[1024,1280]{1,0:T(8,128)(2,1)}, u32[]{:S(2)}, u32[]{:S(2)}) collective-permute-start(bf16[1024,1280]{1,0:T(8,128)(2,1)} %fusion.11), channel_id=1, source_target_pairs={{0,1},{1,0},{2,3},{3,2},{4,5},{5,4},{6,7},{7,6},{8,9},{9,8},{10,11... | collective-permute-start | bytes 7864328 | tf_op jit(solution)/shard_map/ppermute | solution.py:395
  57.2 44.1 %collective-permute-start.9 = (bf16[80,3200]{1,0:T(8,128)(2,1)}, bf16[80,3200]{1,0:T(8,128)(2,1)}, u32[]{:S(2)}, u32[]{:S(2)}) collective-permute-start(bf16[80,3200]{1,0:T(8,128)(2,1)} %pad_maximum_fusion.9), channel_id=1, source_target_pairs={{0,16},{2,18},{4,20},{6,22},{8,24},{10,26},{12,28},{14,30},{16,0},... | collective-permute-start | bytes 1536008 | tf_op jit(solution)/shard_map/ppermute | solution.py:395
  58.8 43.5 %collective-permute-start.10 = (bf16[80,3200]{1,0:T(8,128)(2,1)}, bf16[80,3200]{1,0:T(8,128)(2,1)}, u32[]{:S(2)}, u32[]{:S(2)}) collective-permute-start(bf16[80,3200]{1,0:T(8,128)(2,1)} %pad_maximum_fusion.9), channel_id=1, source_target_pairs={{0,24},{2,26},{4,28},{6,30},{8,0},{10,2},{12,4},{14,6},{16,8},{18,... | collective-permute-start | bytes 1536008 | tf_op jit(solution)/shard_map/ppermute | solution.py:395
  105.5 49.3 %collective-permute-start.11 = (bf16[4,80,3200]{2,1,0:T(8,128)(2,1)}, bf16[4,80,3200]{2,1,0:T(8,128)(2,1)}, u32[]{:S(2)}, u32[]{:S(2)}) collective-permute-start(bf16[4,80,3200]{2,1,0:T(8,128)(2,1)} %pad_maximum_fusion.own), channel_id=1, source_target_pairs={{0,2},{2,0},{4,6},{6,4},{8,10},{10,8},{12,14},{14,12},{16,18},{18,... | collective-permute-start | bytes 6144008 | tf_op jit(solution)/shard_map/ppermute | solution.py:395
  106.1 48.7 %collective-permute-start.12 = (bf16[4,80,3200]{2,1,0:T(8,128)(2,1)}, bf16[4,80,3200]{2,1,0:T(8,128)(2,1)}, u32[]{:S(2)}, u32[]{:S(2)}) collective-permute-start(bf16[4,80,3200]{2,1,0:T(8,128)(2,1)} %pad_maximum_fusion.own), channel_id=1, source_target_pairs={{0,4},{2,6},{4,0},{6,2},{8,12},{10,14},{12,8},{14,10},{16,20},{18,... | collective-permute-start | bytes 6144008 | tf_op jit(solution)/shard_map/ppermute | solution.py:395
  128.7 34.9 %collective-permute-start.16 = (bf16[80,2560]{1,0:T(8,128)(2,1)S(1)}, bf16[80,2560]{1,0:T(8,128)(2,1)S(1)}, u32[]{:S(2)}, u32[]{:S(2)}) collective-permute-start(bf16[80,2560]{1,0:T(8,128)(2,1)S(1)} %bitcast.99), channel_id=1, source_target_pairs={{0,16},{2,18},{4,20},{6,22},{8,24},{10,26},{12,28},{14,30},{16,0},... | collective-permute-start | bytes 1228808 | tf_op jit(solution)/shard_map/ppermute | solution.py:395
  157.1 37.7 %collective-permute-start.13 = (bf16[4,80,1664]{2,1,0:T(8,128)(2,1)}, bf16[4,80,1664]{2,1,0:T(8,128)(2,1)}, u32[]{:S(2)}, u32[]{:S(2)}) collective-permute-start(bf16[4,80,1664]{2,1,0:T(8,128)(2,1)} %slice.194), channel_id=1, source_target_pairs={{0,4},{2,6},{4,0},{6,2},{8,12},{10,14},{12,8},{14,10},{16,20},{18,... | collective-permute-start | bytes 3194888 | tf_op jit(solution)/shard_map/ppermute | solution.py:395
  217.4 45.9 %collective-permute-start.24 = (bf16[1024,1280]{1,0:T(8,128)(2,1)}, bf16[1024,1280]{1,0:T(8,128)(2,1)}, u32[]{:S(2)}, u32[]{:S(2)}) collective-permute-start(bf16[1024,1280]{1,0:T(8,128)(2,1)} %add_convert_fusion.c.refs_1_), channel_id=1, source_target_pairs={{0,1},{1,0},{2,3},{3,2},{4,5},{5,4},{6,7},{7,6},{8,9},{9,8},{10,11... | collective-permute-start | bytes 7864328 | tf_op jit(solution)/shard_map/ppermute | solution.py:395
  217.5 59.4 %collective-permute-start.23 = (bf16[1024,1280]{1,0:T(8,128)(2,1)}, bf16[1024,1280]{1,0:T(8,128)(2,1)}, u32[]{:S(2)}, u32[]{:S(2)}) collective-permute-start(bf16[1024,1280]{1,0:T(8,128)(2,1)} %g.1), channel_id=1, source_target_pairs={{0,1},{1,0},{2,3},{3,2},{4,5},{5,4},{6,7},{7,6},{8,9},{9,8},{10,11... | collective-permute-start | bytes 7864328 | tf_op jit(solution)/shard_map/ppermute | solution.py:395
  217.9 37.9 %collective-permute-start.19 = (bf16[4,80,2560]{2,1,0:T(8,128)(2,1)S(1)}, bf16[4,80,2560]{2,1,0:T(8,128)(2,1)}, u32[]{:S(2)}, u32[]{:S(2)}) collective-permute-start(bf16[4,80,2560]{2,1,0:T(8,128)(2,1)S(1)} %pad_maximum_fusion.1.own), channel_id=1, source_target_pairs={{0,2},{2,0},{4,6},{6,4},{8,10},{10,8},{12,14},{14,12},{16,18},{18,... | collective-permute-start | bytes 4915208 | tf_op jit(solution)/shard_map/ppermute | solution.py:395
  218.6 37.7 %collective-permute-start.20 = (bf16[4,80,2560]{2,1,0:T(8,128)(2,1)S(1)}, bf16[4,80,2560]{2,1,0:T(8,128)(2,1)}, u32[]{:S(2)}, u32[]{:S(2)}) collective-permute-start(bf16[4,80,2560]{2,1,0:T(8,128)(2,1)S(1)} %pad_maximum_fusion.1.own), channel_id=1, source_target_pairs={{0,4},{2,6},{4,0},{6,2},{8,12},{10,14},{12,8},{14,10},{16,20},{18,... | collective-permute-start | bytes 4915208 | tf_op jit(solution)/shard_map/ppermute | solution.py:395
  258.3 38.0 %collective-permute-start.21 = (bf16[4,80,1280]{2,1,0:T(8,128)(2,1)}, bf16[4,80,1280]{2,1,0:T(8,128)(2,1)}, u32[]{:S(2)}, u32[]{:S(2)}) collective-permute-start(bf16[4,80,1280]{2,1,0:T(8,128)(2,1)} %slice.198), channel_id=1, source_target_pairs={{0,4},{2,6},{4,0},{6,2},{8,12},{10,14},{12,8},{14,10},{16,20},{18,... | collective-permute-start | bytes 2457608 | tf_op jit(solution)/shard_map/ppermute | solution.py:395
  325.5 38.0 %collective-permute-start.28 = (bf16[4,80,2560]{2,1,0:T(8,128)(2,1)}, bf16[4,80,2560]{2,1,0:T(8,128)(2,1)}, u32[]{:S(2)}, u32[]{:S(2)}) collective-permute-start(bf16[4,80,2560]{2,1,0:T(8,128)(2,1)} %pad_maximum_fusion.3), channel_id=1, source_target_pairs={{0,4},{2,6},{4,0},{6,2},{8,12},{10,14},{12,8},{14,10},{16,20},{18,... | collective-permute-start | bytes 4915208 | tf_op jit(solution)/shard_map/ppermute | solution.py:395
  329.8 35.6 %collective-permute-start.27 = (bf16[4,80,2560]{2,1,0:T(8,128)(2,1)}, bf16[4,80,2560]{2,1,0:T(8,128)(2,1)}, u32[]{:S(2)}, u32[]{:S(2)}) collective-permute-start(bf16[4,80,2560]{2,1,0:T(8,128)(2,1)} %pad_maximum_fusion.2), channel_id=1, source_target_pairs={{0,2},{2,0},{4,6},{6,4},{8,10},{10,8},{12,14},{14,12},{16,18},{18,... | collective-permute-start | bytes 4915208 | tf_op jit(solution)/shard_map/ppermute | solution.py:395
  404.0 38.6 %collective-permute-start.34 = (bf16[80,2560]{1,0:T(8,128)(2,1)}, bf16[80,2560]{1,0:T(8,128)(2,1)}, u32[]{:S(2)}, u32[]{:S(2)}) collective-permute-start(bf16[80,2560]{1,0:T(8,128)(2,1)} %get-tuple-element.272), channel_id=1, source_target_pairs={{0,8},{2,10},{4,12},{6,14},{8,16},{10,18},{12,20},{14,22},{16,24},... | collective-permute-start | bytes 1228808 | tf_op jit(solution)/shard_map/ppermute | solution.py:395
  404.0 38.6 %collective-permute-start.35 = (bf16[80,2560]{1,0:T(8,128)(2,1)}, bf16[80,2560]{1,0:T(8,128)(2,1)}, u32[]{:S(2)}, u32[]{:S(2)}) collective-permute-start(bf16[80,2560]{1,0:T(8,128)(2,1)} %get-tuple-element.271), channel_id=1, source_target_pairs={{0,16},{2,18},{4,20},{6,22},{8,24},{10,26},{12,28},{14,30},{16,0},... | collective-permute-start | bytes 1228808 | tf_op jit(solution)/shard_map/ppermute | solution.py:395
  405.8 36.8 %collective-permute-start.36 = (bf16[80,2560]{1,0:T(8,128)(2,1)}, bf16[80,2560]{1,0:T(8,128)(2,1)}, u32[]{:S(2)}, u32[]{:S(2)}) collective-permute-start(bf16[80,2560]{1,0:T(8,128)(2,1)} %get-tuple-element.270), channel_id=1, source_target_pairs={{0,24},{2,26},{4,28},{6,30},{8,0},{10,2},{12,4},{14,6},{16,8},{18,... | collective-permute-start | bytes 1228808 | tf_op jit(solution)/shard_map/ppermute | solution.py:395
  409.5 37.6 %collective-permute-start.33 = (bf16[4,80,2560]{2,1,0:T(8,128)(2,1)}, bf16[4,80,2560]{2,1,0:T(8,128)(2,1)}, u32[]{:S(2)}, u32[]{:S(2)}) collective-permute-start(bf16[4,80,2560]{2,1,0:T(8,128)(2,1)} %pad_maximum_fusion.5), channel_id=1, source_target_pairs={{0,4},{2,6},{4,0},{6,2},{8,12},{10,14},{12,8},{14,10},{16,20},{18,... | collective-permute-start | bytes 4915208 | tf_op jit(solution)/shard_map/ppermute | solution.py:395
  411.5 37.3 %collective-permute-start.32 = (bf16[4,80,2560]{2,1,0:T(8,128)(2,1)}, bf16[4,80,2560]{2,1,0:T(8,128)(2,1)}, u32[]{:S(2)}, u32[]{:S(2)}) collective-permute-start(bf16[4,80,2560]{2,1,0:T(8,128)(2,1)} %pad_maximum_fusion.4), channel_id=1, source_target_pairs={{0,2},{2,0},{4,6},{6,4},{8,10},{10,8},{12,14},{14,12},{16,18},{18,... | collective-permute-start | bytes 4915208 | tf_op jit(solution)/shard_map/ppermute | solution.py:395
  454.9 99.0 %collective-permute-start.38 = (bf16[80,2560]{1,0:T(8,128)(2,1)}, bf16[80,2560]{1,0:T(8,128)(2,1)S(1)}, u32[]{:S(2)}, u32[]{:S(2)}) collective-permute-start(bf16[80,2560]{1,0:T(8,128)(2,1)} %get-tuple-element.269), channel_id=1, source_target_pairs={{0,8},{2,10},{4,12},{6,14},{8,16},{10,18},{12,20},{14,22},{16,24},... | collective-permute-start | bytes 1228808 | tf_op jit(solution)/shard_map/ppermute | solution.py:395
  455.2 98.7 %collective-permute-start.39 = (bf16[80,2560]{1,0:T(8,128)(2,1)}, bf16[80,2560]{1,0:T(8,128)(2,1)S(1)}, u32[]{:S(2)}, u32[]{:S(2)}) collective-permute-start(bf16[80,2560]{1,0:T(8,128)(2,1)} %get-tuple-element.268), channel_id=1, source_target_pairs={{0,16},{2,18},{4,20},{6,22},{8,24},{10,26},{12,28},{14,30},{16,0},... | collective-permute-start | bytes 1228808 | tf_op jit(solution)/shard_map/ppermute | solution.py:395
  458.1 95.8 %collective-permute-start.40 = (bf16[80,2560]{1,0:T(8,128)(2,1)}, bf16[80,2560]{1,0:T(8,128)(2,1)}, u32[]{:S(2)}, u32[]{:S(2)}) collective-permute-start(bf16[80,2560]{1,0:T(8,128)(2,1)} %get-tuple-element.267), channel_id=1, source_target_pairs={{0,24},{2,26},{4,28},{6,30},{8,0},{10,2},{12,4},{14,6},{16,8},{18,... | collective-permute-start | bytes 1228808 | tf_op jit(solution)/shard_map/ppermute | solution.py:395
  630.9 40.2 %collective-permute-start.46 = (bf16[1024,1280]{1,0:T(8,128)(2,1)}, bf16[1024,1280]{1,0:T(8,128)(2,1)}, u32[]{:S(2)}, u32[]{:S(2)}) collective-permute-start(bf16[1024,1280]{1,0:T(8,128)(2,1)} %convolution_convert_fusion.1), channel_id=1, source_target_pairs={{0,1},{1,0},{2,3},{3,2},{4,5},{5,4},{6,7},{7,6},{8,9},{9,8},{10,11... | collective-permute-start | bytes 7864328 | tf_op jit(solution)/shard_map/ppermute | solution.py:395
  (93 other events, 1262.5 us)
Sparse Core Ops, SparseCore 0:
  458.3 77.4 reduce-scatter.1

commit v2 on v1

--- a/solution.py
+++ b/solution.py
@@ -19,10 +19,7 @@
 TN = (((0,), (0,)), ((), ()))
 
 
-def lasts(micros):
-    return pl.CostEstimate(flops=int(micros * 1.1e9), bytes_accessed=1, transcendentals=0)
-
-
+INSTANT = pl.CostEstimate(flops=1, bytes_accessed=1, transcendentals=0)
 ROOMY = pltpu.CompilerParams(vmem_limit_bytes=62 * 2**20)
 
 
@@ -172,7 +169,7 @@
             jax.ShapeDtypeStruct((count, 8, length), f32),
         ],
         compiler_params=ROOMY,
-        cost_estimate=lasts(10),
+        cost_estimate=INSTANT,
         name="attend",
     )(mq, mk, q, k, v, *before)
 
@@ -269,14 +266,15 @@
         + [pltpu.VMEM((length, 256), f32), pltpu.VMEM((8, length), f32)],
         out_shape=jax.ShapeDtypeStruct((length, 3 * width), bf16),
         compiler_params=pltpu.CompilerParams(vmem_limit_bytes=63 * 2**20),
-        cost_estimate=lasts(47),
+        cost_estimate=INSTANT,
         name="attend_back",
     )(mq, mk, q, k, v, o, g, lse, *tables)
 
 
-def qkv_kernel(a, w, b, cos, down, up, q, k, v):
+def qkv_kernel(where, own, other, w, b, cos, down, up, q, k, v):
     width = q.shape[1]
-    x = mm(a[...], w[...], NN) + b[...]
+    mine = pl.program_id(0) // (pl.num_programs(0) // 2) == where[0]
+    x = mm(jnp.where(mine, own[...], other[...]), w[...], NN) + b[...]
 
     def rotate(part):
         return (
@@ -290,20 +288,26 @@
     v[...] = x[:, 2 * width :].astype(bf16)
 
 
-def qkv_rotate(a, w, b, tables, block=512):
-    length, depth = a.shape
+def qkv_rotate(where, own, other, w, b, tables, block=512):
+    half, depth = own.shape
     width = w.shape[1] // 3
-    rows = lambda n: pl.BlockSpec((block, n), lambda i: (i, 0))
+    steps = half // block
+    rows = lambda n: pl.BlockSpec((block, n), lambda i, w: (i, 0))
+    part = pl.BlockSpec((block, depth), lambda i, w: (i % steps, 0))
+    fixed = lambda shape: pl.BlockSpec(shape, lambda i, w: (0, 0))
     return pl.pallas_call(
         qkv_kernel,
-        grid=(length // block,),
-        in_specs=[rows(depth), whole(w.shape), whole(b.shape)] + [rows(width)] * 3,
-        out_specs=[rows(width)] * 3,
-        out_shape=[jax.ShapeDtypeStruct((length, width), bf16)] * 3,
+        grid_spec=pltpu.PrefetchScalarGridSpec(
+            num_scalar_prefetch=1,
+            grid=(2 * steps,),
+            in_specs=[part, part, fixed(w.shape), fixed(b.shape)] + [rows(width)] * 3,
+            out_specs=[rows(width)] * 3,
+        ),
+        out_shape=[jax.ShapeDtypeStruct((2 * half, width), bf16)] * 3,
         compiler_params=ROOMY,
-        cost_estimate=lasts(9),
+        cost_estimate=INSTANT,
         name="qkv_rotate",
-    )(a, w, b, *tables)
+    )(where, own, other, w, b, *tables)
 
 
 def hidden_kernel(c, w, b, hidden, slope):
@@ -325,7 +329,7 @@
         out_specs=[rows(units)] * 2,
         out_shape=[jax.ShapeDtypeStruct((length, units), bf16)] * 2,
         compiler_params=ROOMY,
-        cost_estimate=lasts(7),
+        cost_estimate=INSTANT,
         name="hidden_slope",
     )(c, w, b)
 
@@ -355,36 +359,207 @@
             jax.ShapeDtypeStruct((8, units), f32),
         ],
         compiler_params=ROOMY,
-        cost_estimate=lasts(6),
+        cost_estimate=INSTANT,
         name="pre_grad",
     )(g, w, slope)
 
 
-def weight_grad_kernel(*refs, count):
+def weight_grad_kernel(*refs, count, size):
+    where = refs[0]
+    lefts, rights = refs[1 : 1 + count], refs[1 + count : 1 + 2 * count]
+    outs = refs[1 + 2 * count :]
     total = None
-    for left, right in zip(refs[:count], refs[count : 2 * count]):
+    for left, right in zip(lefts, rights):
         part = mm(left[...], right[...], TN)
         total = part if total is None else total + part
-    refs[2 * count][...] = total.astype(bf16)
-
-
-def weight_grad(lefts, rights, block=512):
-    count = len(lefts)
+    if not size:
+        outs[0][...] = total.astype(bf16)
+        return
+    result = outs[-1]
+    result[...] = total.astype(bf16)
+    index = where[1]
+    high, low = index // 4, index % 4
+    ring, rows = size // 4, outs[0].shape[1]
+    for out, order in zip(outs, scatter_order(ring)):
+        for slot, (bits, step) in enumerate(order):
+            block = lax.rem(high + step, ring) * 4 + (low ^ bits)
+            out[slot] = result[pl.ds(pl.multiple_of(block * rows, rows), rows), :]
+
+
+def weight_grad(where, lefts, rights, size=0, block=512):
     length, high = lefts[0].shape
     wide = rights[0].shape[1]
-    if wide % block:
-        block = 384 if wide % 384 == 0 else 128
+    if len(rights) == 1:
+        rights = rights * 2
+        specs = [
+            pl.BlockSpec((length, block), lambda i, w: (w[0], i)),
+            pl.BlockSpec((length, block), lambda i, w: (1 - w[0], i)),
+        ]
+    else:
+        specs = [pl.BlockSpec((length, block), lambda i, w: (0, i))] * 2
+    if size:
+        stacks = [(len(order), high // size) for order in scatter_order(size // 4)]
+        out_specs = [pl.BlockSpec(stack + (block,), lambda i, w: (0, 0, i)) for stack in stacks]
+        out_shape = [jax.ShapeDtypeStruct(stack + (wide,), bf16) for stack in stacks]
+        scratch = [pltpu.VMEM((high, block), bf16)]
+    else:
+        out_specs = pl.BlockSpec((high, block), lambda i, w: (0, i))
+        out_shape = jax.ShapeDtypeStruct((high, wide), bf16)
+        scratch = []
     return pl.pallas_call(
-        functools.partial(weight_grad_kernel, count=count),
-        grid=(wide // block,),
-        in_specs=[whole((length, high))] * count
-        + [pl.BlockSpec((length, block), lambda i: (0, i))] * count,
-        out_specs=pl.BlockSpec((high, block), lambda i: (0, i)),
-        out_shape=jax.ShapeDtypeStruct((high, wide), bf16),
+        functools.partial(weight_grad_kernel, count=2, size=size),
+        grid_spec=pltpu.PrefetchScalarGridSpec(
+            num_scalar_prefetch=1,
+            grid=(pl.cdiv(wide, block),),
+            in_specs=[pl.BlockSpec((length, high), lambda i, w: (0, 0))] * 2 + specs,
+            out_specs=out_specs,
+            scratch_shapes=scratch,
+        ),
+        out_shape=out_shape,
         compiler_params=ROOMY,
-        cost_estimate=lasts(9),
+        cost_estimate=INSTANT,
         name="weight_grad",
-    )(*lefts, *rights)
+    )(where, *lefts, *rights)
+
+
+def mixed_grad_kernel(where, own, other, w, out):
+    value = jnp.where(pl.program_id(0) < pl.num_programs(0) // 2, own[...], other[...])
+    out[...] = mm(value, w[...], NN).astype(bf16)
+
+
+def mixed_grad_rows(where, own, other, w, block=512):
+    half, depth = own.shape
+    wide = w.shape[1]
+    steps = half // block
+    return pl.pallas_call(
+        mixed_grad_kernel,
+        grid_spec=pltpu.PrefetchScalarGridSpec(
+            num_scalar_prefetch=1,
+            grid=(2 * steps,),
+            in_specs=[
+                pl.BlockSpec((block, depth), lambda i, w: (jnp.minimum(i, steps - 1), 0)),
+                pl.BlockSpec((block, depth), lambda i, w: (jnp.maximum(i - steps, 0), 0)),
+                pl.BlockSpec((depth, wide), lambda i, w: (0, 0)),
+            ],
+            out_specs=pl.BlockSpec(
+                (block, wide), lambda i, w: ((w[0] * steps + i) % (2 * steps), 0)
+            ),
+        ),
+        out_shape=jax.ShapeDtypeStruct((2 * half, wide), bf16),
+        compiler_params=ROOMY,
+        cost_estimate=INSTANT,
+        name="mixed_grad",
+    )(where, own, other, w)
+
+
+def closing_kernel(*refs, finish, extras, outs):
+    x, w = refs[1:3]
+    given = [ref[...] for ref in refs[3 : 3 + extras]]
+    results, sums = finish(mm(x[...], w[...], NT), *given)
+    for ref, value in zip(refs[3 + extras : 3 + extras + outs], results):
+        ref[...] = value.astype(ref.dtype)
+    totals = refs[3 + extras + outs :]
+
+    @pl.when(pl.program_id(0) == 0)
+    def _():
+        for ref in totals:
+            ref[...] = jnp.zeros(ref.shape, f32)
+
+    for ref, value in zip(totals, sums):
+        ref[...] += jnp.sum(value.reshape(-1, 8, value.shape[1]), axis=0)
+
+
+def closing(where, x, w, rows, vectors, finish, kinds, sums, name, block=256):
+    half, model = rows[0].shape
+    depth = x.shape[1]
+    steps = half // block
+    skip = x.shape[0] > half
+    part = pl.BlockSpec((block, model), lambda i, w: (i, 0))
+    fixed = lambda shape: pl.BlockSpec(shape, lambda i, w: (0, 0))
+    results = pl.pallas_call(
+        functools.partial(
+            closing_kernel, finish=finish, extras=len(rows) + len(vectors), outs=len(kinds)
+        ),
+        grid_spec=pltpu.PrefetchScalarGridSpec(
+            num_scalar_prefetch=1,
+            grid=(steps,),
+            in_specs=[
+                pl.BlockSpec((block, depth), lambda i, w: (w[0] * steps * skip + i, 0)),
+                fixed(w.shape),
+            ]
+            + [part] * len(rows)
+            + [fixed((1, model))] * len(vectors),
+            out_specs=[part] * len(kinds) + [fixed((8, model))] * sums,
+        ),
+        out_shape=[jax.ShapeDtypeStruct((half, model), kind) for kind in kinds]
+        + [jax.ShapeDtypeStruct((8, model), f32)] * sums,
+        compiler_params=ROOMY,
+        cost_estimate=INSTANT,
+        name=name,
+    )(where, x, w, *rows, *[vector.reshape(1, model) for vector in vectors])
+    return list(results[: len(kinds)]) + [jnp.sum(value, axis=0) for value in results[len(kinds) :]]
+
+
+def product_kernel(where, x, w, out):
+    out[...] = mm(x[...], w[...], NT).astype(bf16)
+
+
+def product_for_other(where, x, w, half, block=256):
+    depth, model = x.shape[1], w.shape[0]
+    steps = half // block
+    skip = x.shape[0] > half
+    return pl.pallas_call(
+        product_kernel,
+        grid_spec=pltpu.PrefetchScalarGridSpec(
+            num_scalar_prefetch=1,
+            grid=(steps,),
+            in_specs=[
+                pl.BlockSpec((block, depth), lambda i, w: ((1 - w[0]) * steps * skip + i, 0)),
+                pl.BlockSpec(w.shape, lambda i, w: (0, 0)),
+            ],
+            out_specs=pl.BlockSpec((block, model), lambda i, w: (i, 0)),
+        ),
+        out_shape=jax.ShapeDtypeStruct((half, model), bf16),
+        compiler_params=ROOMY,
+        cost_estimate=INSTANT,
+        name="product_for_other",
+    )(where, x, w)
+
+
+def finish_attention(value, away, tokens, bias, gain, shift):
+    middle = tokens.astype(f32) + (value + away.astype(f32) + bias)
+    unit, _ = norm_parts(middle)
+    return (middle, unit * gain + shift), ()
+
+
+def finish_output(value, away, middle, bias):
+    return (middle + (value + away.astype(f32)) + bias,), ()
+
+
+def norm_back(grad_out, values, gain):
+    unit, inverse = norm_parts(values)
+    scaled = grad_out * gain
+    grad_in = inverse * (
+        scaled
+        - jnp.mean(scaled, axis=-1, keepdims=True)
+        - unit * jnp.mean(scaled * unit, axis=-1, keepdims=True)
+    )
+    return grad_in, grad_out * unit
+
+
+def finish_middle(value, away, middle, cotangent, gain):
+    grad = value + away.astype(f32)
+    back, by_gain = norm_back(grad, middle, gain)
+    out_grad = cotangent.astype(f32)
+    total = out_grad + back
+    low = total.astype(bf16)
+    return (total, low), (by_gain, grad, low.astype(f32), out_grad)
+
+
+def finish_input(value, away, tokens, middle_grad, gain):
+    grad = value + away.astype(f32)
+    back, by_gain = norm_back(grad, tokens.astype(f32), gain)
+    return (middle_grad + back,), (by_gain, grad)
 
 
 def flip(size, bit):
@@ -412,80 +587,47 @@
     return send(own, flip(size, 1)), send(own, flip(size, 2))
 
 
-def gather_far(near, size, cut):
-    return send(near[0][:, :, :cut], flip(size, 2)), send(near[1][:, :, cut:], flip(size, 1))
-
-
-def place_kernel(index_ref, own, fast, second, left, right, out, sem, *, size, cut):
-    index = index_ref[0]
+def gather_far(near, size):
+    half = size // 8
+    return send(near[0][:half], flip(size, 2)), send(near[1][half:], flip(size, 1))
+
+
+def place_kernel(*refs, size, widths):
+    index, pieces, outs, sem = refs[0][0], refs[1:6], refs[6:-1], refs[-1]
     high, low = index // 4, index % 4
-    ring, rows = size // 4, own.shape[1]
-    wide = out.shape[1]
+    ring, rows = size // 4, pieces[0].shape[1]
     copies = []
-    for piece, bits, start, stop in (
-        (own, 0, 0, wide), (fast, 1, 0, wide), (second, 2, 0, wide),
-        (left, 3, 0, cut), (right, 3, cut, wide),
-    ):
-        for step in range(ring):
-            block = lax.rem(high - step + ring, ring) * 4 + (low ^ bits)
-            to = out.at[pl.ds(pl.multiple_of(block * rows, rows), rows), pl.ds(start, stop - start)]
-            copies.append(pltpu.make_async_copy(piece.at[step], to, sem.at[len(copies)]))
+    for piece, bits, first in zip(pieces, (0, 1, 2, 3, 3), (0, 0, 0, 0, ring // 2)):
+        for step in range(piece.shape[0]):
+            block = lax.rem(high - first - step + ring, ring) * 4 + (low ^ bits)
+            to = pl.ds(pl.multiple_of(block * rows, rows), rows)
+            start = 0
+            for out, wide in zip(outs, widths):
+                copies.append(
+                    pltpu.make_async_copy(
+                        piece.at[step, :, pl.ds(start, wide)], out.at[to, :], sem.at[len(copies)]
+                    )
+                )
+                start += wide
     for copy in copies:
         copy.start()
     for copy in copies:
         copy.wait()
 
 
-def place(own, near, far, size):
-    _, rows, wide = own.shape
+def place(own, near, far, size, widths):
+    rows = own.shape[1]
     anywhere = pl.BlockSpec(memory_space=pl.ANY)
     return pl.pallas_call(
-        functools.partial(place_kernel, size=size, cut=far[0].shape[2]),
+        functools.partial(place_kernel, size=size, widths=widths),
         in_specs=[pl.BlockSpec(memory_space=pltpu.SMEM)] + [anywhere] * 5,
-        out_specs=pl.BlockSpec(memory_space=pltpu.VMEM),
-        scratch_shapes=[pltpu.SemaphoreType.DMA((5 * size // 4,))],
-        out_shape=jax.ShapeDtypeStruct((rows * size, wide), bf16),
+        out_specs=[pl.BlockSpec(memory_space=pltpu.VMEM)] * len(widths),
+        scratch_shapes=[pltpu.SemaphoreType.DMA((size * len(widths),))],
+        out_shape=[jax.ShapeDtypeStruct((rows * size, wide), bf16) for wide in widths],
         compiler_params=pltpu.CompilerParams(vmem_limit_bytes=24 * 2**20),
-        cost_estimate=lasts(1),
+        cost_estimate=INSTANT,
         name="place",
     )(lax.axis_index("dp").reshape(1), own, *near, *far)
-
-
-def split_grad_kernel(*refs, count, size):
-    index = refs[0][0]
-    lefts, rights = refs[1 : 1 + count], refs[1 + count : 1 + 2 * count]
-    outs, result = refs[1 + 2 * count : 5 + 2 * count], refs[5 + 2 * count]
-    total = None
-    for left, right in zip(lefts, rights):
-        part = mm(left[...], right[...], TN)
-        total = part if total is None else total + part
-    result[...] = total.astype(bf16)
-    high, low = index // 4, index % 4
-    ring, rows = size // 4, outs[0].shape[1]
-    for bits in range(4):
-        for step in range(ring):
-            block = lax.rem(high + step, ring) * 4 + (low ^ bits)
-            outs[bits][step] = result[pl.ds(pl.multiple_of(block * rows, rows), rows), :]
-
-
-def split_grad(lefts, rights, size, block=512):
-    count = len(lefts)
-    length, high = lefts[0].shape
-    wide = rights[0].shape[1]
-    ring, rows = size // 4, high // size
-    return pl.pallas_call(
-        functools.partial(split_grad_kernel, count=count, size=size),
-        grid=(pl.cdiv(wide, block),),
-        in_specs=[pl.BlockSpec(memory_space=pltpu.SMEM)]
-        + [whole((length, high))] * count
-        + [pl.BlockSpec((length, block), lambda i: (0, i))] * count,
-        out_specs=[pl.BlockSpec((ring, rows, block), lambda i: (0, 0, i))] * 4,
-        out_shape=[jax.ShapeDtypeStruct((ring, rows, wide), bf16)] * 4,
-        scratch_shapes=[pltpu.VMEM((high, block), bf16)],
-        compiler_params=ROOMY,
-        cost_estimate=lasts(9),
-        name="split_grad",
-    )(lax.axis_index("dp").reshape(1), *lefts, *rights)
 
 
 def add_low(*parts):
@@ -495,24 +637,42 @@
     return total.astype(bf16)
 
 
-def scatter_far(stacks, size, cut):
-    far = stacks[3]
-    return send(far[:, :, :cut], flip(size, 2)), send(far[:, :, cut:], flip(size, 1))
+def scatter_order(ring):
+    low, high = list(range(ring // 2)), list(range(ring // 2, ring))
+    pick = lambda bits, steps: [(bits, step) for step in steps]
+    return [
+        pick(0, low + high),
+        pick(1, high) + pick(3, high),
+        pick(2, low) + pick(3, low),
+        pick(1, low),
+        pick(2, high),
+    ]
+
+
+def scatter_far(stacks, size):
+    return send(stacks[1], flip(size, 1)), send(stacks[2], flip(size, 2))
 
 
 def scatter_near(stacks, got, size):
-    left, right = got
-    cut = left.shape[2]
-    fast = jnp.concatenate([add_low(stacks[1][:, :, :cut], left), stacks[1][:, :, cut:]], axis=2)
-    second = jnp.concatenate([stacks[2][:, :, :cut], add_low(stacks[2][:, :, cut:], right)], axis=2)
-    return send(fast, flip(size, 1)), send(second, flip(size, 2))
-
-
-def scatter_slow(stacks, got, size):
-    total = add_low(stacks[0], *got)
-    return total[0], [
-        send(total[step], [(i, (i + 4 * step) % size) for i in range(size)])
-        for step in range(1, size // 4)
+    half = size // 8
+    return (
+        send(add_low(stacks[3], got[1][half:]), flip(size, 1)),
+        send(add_low(stacks[4], got[0][half:]), flip(size, 2)),
+    )
+
+
+def scatter_slow(groups, size):
+    ring = size // 4
+    half = ring // 2
+    low, high = [], []
+    for stacks, got, more in groups:
+        low.append(add_low(stacks[0][:half], more[0], got[1][:half]))
+        high.append(add_low(stacks[0][half:], more[1], got[0][:half]))
+    low, high = jnp.concatenate(low, axis=2), jnp.concatenate(high, axis=2)
+    blocks = [low[step] for step in range(half)] + [high[step] for step in range(half)]
+    return blocks[0], [
+        send(blocks[step], [(i, (i + 4 * step) % size) for i in range(size)])
+        for step in range(1, ring)
     ]
 
 
@@ -554,121 +714,106 @@
     units = fc1_weight.shape[1]
     swap = [(0, 1), (1, 0)]
     cross = lambda value: send(value, swap, "tensor")
-    mine = lambda value: lax.dynamic_slice_in_dim(value, me * half, half, 0)
-    theirs = lambda value: lax.dynamic_slice_in_dim(value, (1 - me) * half, half, 0)
-
-    def in_order(own, other):
-        return jnp.where(
-            me == 0, jnp.concatenate([own, other], 0), jnp.concatenate([other, own], 0)
-        )
 
     gain_one, shift_one = norm1_gain.astype(f32), norm1_bias.astype(f32)
     gain_two, shift_two = norm2_gain.astype(f32), norm2_bias.astype(f32)
     qkv_shift = lax.dynamic_slice_in_dim(qkv_bias.astype(f32), me * width, width, 1).reshape(1, -1)
     fc1_shift = lax.dynamic_slice_in_dim(fc1_bias.astype(f32), me * units, units, 0).reshape(1, -1)
 
-    qkv_cut, cut, fc1_cut, fc2_cut = 1024, 1664, 1280, 1280
+    where = jnp.stack([me, lax.axis_index("dp")]).astype(jnp.int32)
     inputs = tokens.astype(f32)
     unit_one, inverse_one = norm_parts(inputs)
-    normed_own = (unit_one * gain_one + shift_one).astype(bf16)
-    attn_in = in_order(normed_own, cross(normed_own))
+    a_own = (unit_one * gain_one + shift_one).astype(bf16)
+    a_other = cross(a_own)
     tables = rope_tables(positions, width)
     mq, mk = mask_lanes(picture_ids, valid, width // 128 - 1)
 
     qkv_own = gather_slow(qkv_weight.reshape(rows, 3 * width), size)
     joined = jnp.concatenate([proj_weight.T, fc1_weight], axis=1)
-    qkv_own, joined = tie(qkv_own, joined)
+    cosine, down, up = tables
+    qkv_own, joined, a_other, cosine, down = tie(qkv_own, joined, a_other, cosine, down)
     qkv_near = gather_near(qkv_own, size)
     own = gather_slow(joined, size)
-    qkv_near, attn_in = tie(qkv_near, attn_in)
-    qkv_far = gather_far(qkv_near, size, qkv_cut)
-    qkv_far, own, tables = tie(qkv_far, own, tables)
+    qkv_near, up, mq, mk = tie(qkv_near, up, mq, mk)
+    qkv_far = gather_far(qkv_near, size)
+    qkv_far, own = tie(qkv_far, own)
+    tables = (cosine, down, up)
     near = gather_near(own, size)
-    qkv_full = place(qkv_own, qkv_near, qkv_far, size)
-    q, k, v = qkv_rotate(attn_in, qkv_full, qkv_shift, tables)
+    (qkv_full,) = place(qkv_own, qkv_near, qkv_far, size, [3 * width])
+    q, k, v = qkv_rotate(where, a_own, a_other, qkv_full, qkv_shift, tables)
     pairs = mq.shape[0]
-    fc2_shard, q, mq = tie(fc2_weight.T, q, mq)
-    fc2_own = gather_slow(fc2_shard, size)
     mixed, lse_low = attend(mq, mk, q, k, v, 0, pairs // 2)
-    near, mixed = tie(near, mixed)
-    far = gather_far(near, size, cut)
+    near, mixed, fc2_shard = tie(near, mixed, fc2_weight.T)
+    far = gather_far(near, size)
+    fc2_turned = lax.all_gather(fc2_shard, "dp", axis=0, tiled=True)
     mixed, lse_high = attend(mq, mk, q, k, v, pairs // 2, pairs - pairs // 2, (mixed,))
-    far, fc2_own, mixed = tie(far, fc2_own, mixed)
-    fc2_near = gather_near(fc2_own, size)
-    joined = place(own, near, far, size)
-    proj_turned, fc1_full = joined[:, :width], joined[:, width:]
-
-    away = cross(mm(theirs(mixed), proj_turned, NT).astype(bf16))
-    attn_out = mm(mine(mixed), proj_turned, NT) + away.astype(f32)
-    middle = inputs + (attn_out + proj_bias.astype(f32))
-    unit_two, inverse_two = norm_parts(middle)
-    c_own = (unit_two * gain_two + shift_two).astype(bf16)
+    far, mixed = tie(far, mixed)
+    proj_turned, fc1_full = place(own, near, far, size, [width, units])
+
+    away = cross(product_for_other(where, mixed, proj_turned, half))
+    middle, c_own = closing(
+        where, mixed, proj_turned, [away, tokens], [proj_bias.astype(f32), gain_two, shift_two],
+        finish_attention, [f32, bf16], 0, "middle",
+    )
     grad_other = cross(cotangent)
     c_other = cross(c_own)
     hidden_own, slope_own = hidden_slope(c_own, fc1_full, fc1_shift)
-    fc2_near, hidden_own = tie(fc2_near, hidden_own)
-    fc2_far = gather_far(fc2_near, size, fc2_cut)
     hidden_other, slope_other = hidden_slope(c_other, fc1_full, fc1_shift)
 
-    fc2_stacks = split_grad([cotangent, grad_other], [hidden_own, hidden_other], size)
-    fc2_far, fc2_stacks = tie(fc2_far, fc2_stacks)
-    fc2_got = scatter_far(fc2_stacks, size, fc2_cut)
-    fc2_turned = place(fc2_own, fc2_near, fc2_far, size)
+    fc2_stacks = weight_grad(where, [cotangent, grad_other], [hidden_own, hidden_other], size)
+    fc2_turned, fc2_stacks = tie(fc2_turned, fc2_stacks)
+    fc2_got = scatter_far(fc2_stacks, size)
     pre_other, bias_other = pre_grad(grad_other, fc2_turned, slope_other)
-    fc2_got, pre_other = tie(fc2_got, pre_other)
-    fc2_got = scatter_near(fc2_stacks, fc2_got, size)
+    part = product_for_other(where, pre_other, fc1_full, half)
     pre_own, bias_own = pre_grad(cotangent, fc2_turned, slope_own)
-    fc1_stacks = split_grad([c_own, c_other], [pre_own, pre_other], size)
-    fc2_got, fc1_stacks, pre_other, pre_own = tie(fc2_got, fc1_stacks, pre_other, pre_own)
-    fc2_kept, fc2_got = scatter_slow(fc2_stacks, fc2_got, size)
-    fc1_got = scatter_far(fc1_stacks, size, fc1_cut)
-    away = cross(mm(pre_other, fc1_full, NT).astype(bf16))
-    normed_two_grad = mm(pre_own, fc1_full, NT) + away.astype(f32)
-
-    out_grad = cotangent.astype(f32)
-    fc2_shift_grad = jnp.sum(out_grad, axis=0)
-    middle_part, gain_two_grad, shift_two_grad = norm_backward(
-        normed_two_grad, unit_two, inverse_two, gain_two
-    )
-    middle_grad = out_grad + middle_part
-    attn_grad_own = middle_grad.astype(bf16)
-    proj_shift_grad = jnp.sum(attn_grad_own.astype(f32), axis=0)
-    fc1_got, attn_grad_own = tie(fc1_got, attn_grad_own)
-    attn_grad_other = cross(attn_grad_own)
-    fc1_got = scatter_near(fc1_stacks, fc1_got, size)
-    attn_grad = in_order(attn_grad_own, attn_grad_other)
-    mixed_grad = mm(attn_grad, proj_turned, NN).astype(bf16)
-    proj_grad = weight_grad([attn_grad], [mixed])
-    fc1_got, fc2_got, mixed_grad, proj_grad = tie(fc1_got, fc2_got, mixed_grad, proj_grad)
-    fc2_shard = scatter_last(fc2_kept, fc2_got)
-    fc1_kept, fc1_got = scatter_slow(fc1_stacks, fc1_got, size)
-    proj_shard = lax.psum_scatter(proj_grad, "dp", scatter_dimension=0, tiled=True).astype(f32)
+    fc2_got, pre_own, pre_other, part = tie(fc2_got, pre_own, pre_other, part)
+    fc2_more = scatter_near(fc2_stacks, fc2_got, size)
+    away = cross(part)
+    fc1_stacks = weight_grad(where, [c_own, c_other], [pre_own, pre_other], size)
+    fc2_more, fc1_stacks, pre_own, away, hidden_other = tie(
+        fc2_more, fc1_stacks, pre_own, away, hidden_other
+    )
+    fc1_got = scatter_far(fc1_stacks, size)
+    out_part = product_for_other(where, hidden_other, fc2_turned, half)
+    (middle_grad, g_own, gain_two_grad, shift_two_grad, proj_shift_grad, fc2_shift_grad) = closing(
+        where, pre_own, fc1_full, [away, middle, cotangent], [gain_two],
+        finish_middle, [f32, bf16], 4, "middle_grad",
+    )
+    (output,) = closing(
+        where, hidden_own, fc2_turned, [cross(out_part), middle], [fc2_bias.astype(f32)],
+        finish_output, [f32], 0, "output",
+    )
+    fc1_got, g_own, output = tie(fc1_got, g_own, output)
+    fc1_more = scatter_near(fc1_stacks, fc1_got, size)
+    g_other = cross(g_own)
+    mixed_grad = mixed_grad_rows(where, g_own, g_other, proj_turned)
+    proj_grad = weight_grad(where, [g_own, g_other], [mixed])
     lse = jnp.concatenate([lse_low, lse_high], axis=0)
-    mixed_grad, fc2_shard, fc1_kept = tie(mixed_grad, fc2_shard, fc1_kept)
+    fc1_more, mixed_grad, proj_grad = tie(fc1_more, mixed_grad, proj_grad)
+    groups = [(fc2_stacks, fc2_got, fc2_more), (fc1_stacks, fc1_got, fc1_more)]
+    kept, got = scatter_slow(groups, size)
+    proj_shard = lax.psum_scatter(proj_grad, "dp", scatter_dimension=0, tiled=True)
+    kept, mixed_grad = tie(kept, mixed_grad)
     qkv_grad = attend_back(mq, mk, q, k, v, mixed, mixed_grad, lse, tables)
-    fc1_got, proj_shard, qkv_grad = tie(fc1_got, proj_shard, qkv_grad)
-    fc1_shard = scatter_last(fc1_kept, fc1_got)
-    qkv_stacks = split_grad([attn_in], [qkv_grad], size)
+    got, proj_shard, qkv_grad = tie(got, proj_shard, qkv_grad)
+    qkv_stacks = weight_grad(where, [a_own, a_other], [qkv_grad], size)
     qkv_stacks, qkv_grad = tie(qkv_stacks, qkv_grad)
-    qkv_got = scatter_far(qkv_stacks, size, qkv_cut)
-    part = mm(theirs(qkv_grad), qkv_full, NT).astype(bf16)
-    qkv_got, part = tie(qkv_got, part)
-    qkv_got = scatter_near(qkv_stacks, qkv_got, size)
-    normed_one_grad = mm(mine(qkv_grad), qkv_full, NT) + cross(part).astype(f32)
+    qkv_got = scatter_far(qkv_stacks, size)
+    part = product_for_other(where, qkv_grad, qkv_full, half)
     qkv_shift_grad = jnp.sum(qkv_grad.astype(f32), axis=0)
-    input_part, gain_one_grad, shift_one_grad = norm_backward(
-        normed_one_grad, unit_one, inverse_one, gain_one
-    )
-    input_grad = middle_grad + input_part
-
-    input_grad, hidden_other = tie(input_grad, hidden_other)
-    part = mm(hidden_other, fc2_turned, NT).astype(bf16)
-    qkv_got, part = tie(qkv_got, part)
-    qkv_kept, qkv_got = scatter_slow(qkv_stacks, qkv_got, size)
-    output = (
-        middle + (mm(hidden_own, fc2_turned, NT) + cross(part).astype(f32)) + fc2_bias.astype(f32)
-    )
-    qkv_shard = scatter_last(qkv_kept, qkv_got)
+    input_grad, gain_one_grad, shift_one_grad = closing(
+        where, qkv_grad, qkv_full, [cross(part), tokens, middle_grad], [gain_one],
+        finish_input, [f32], 2, "input_grad",
+    )
+    qkv_got, input_grad, qkv_shift_grad, gain_one_grad = tie(
+        qkv_got, input_grad, qkv_shift_grad, gain_one_grad
+    )
+    more = scatter_near(qkv_stacks, qkv_got, size)
+    both_shards = scatter_last(kept, got)
+    fc2_shard, fc1_shard = both_shards[:, :units], both_shards[:, units:]
+    more, fc2_shard, fc1_shard = tie(more, fc2_shard, fc1_shard)
+    kept, got = scatter_slow([(qkv_stacks, qkv_got, more)], size)
+    qkv_shard = scatter_last(kept, got)
 
     fc1_shift_grad = jnp.sum(bias_own, axis=0) + jnp.sum(bias_other, axis=0)
     fc1_place = lax.dynamic_update_slice_in_dim(
@@ -693,13 +838,13 @@
         small[1],
         qkv_shard.reshape(rows, 3, width),
         small[2].reshape(3, 2 * width),
-        proj_shard.T,
+        proj_shard.astype(f32).T,
         small[3],
         small[4],
         small[5],
         fc1_shard,
         small[6],
-        fc2_shard.T,
+        fc2_shard.astype(f32).T,
         small[7],
     )
 

time: 706 us -> 631 us (0.89)
  Pallas kernels: 285 us -> 390 us
  matrix products: 109 us -> 20.7 us
  other arithmetic: 78.6 us -> 45.6 us
  waiting for transfers between devices: 105 us -> 76.4 us
  local copies, waits for them, and re-layouts: 43.2 us -> 24.1 us
    pallas_call x8 -> x16, Pallas kernels: 93.6 us -> 197 us  [the longest x4 67.7 us: weight_grad(): pl.pallas_call(functools.partial(weight_grad_kernel, count=2, size=size),...]
    dot_general x9 -> x0, matrix products: 87.9 us -> none  [mm(): return lax.dot_general(left, right, dims, preferred_element_type=f32)]
    ppermute x55 -> x45, waiting for transfers between devices: 105 us -> 76.3 us  [send(): return lax.ppermute(value, axis, pairs)]
    slice x17 -> x5, local copies, waits for them, and re-layouts: 27 us -> 5.88 us  [the longest x2 2.31 us: gather_far(): near[1][half:]]
    select_n x2 -> x0, other arithmetic: 16.3 us -> none  [in_order(): jnp.where(me == 0, jnp.concatenate([own, other], 0), jnp.concatenate([oth...]
    ppermute x55 -> x45, starting transfers between devices: 56.4 us -> 51.4 us  [send(): return lax.ppermute(value, axis, pairs)]
  transfers between devices with their start and end apart: 56 -> 47, of which waited for: 24 -> 21; matrix products, arithmetic and copies ran while one was open for 24% -> 12% of each run, Pallas kernels for 38% -> 56%
where the time goes in v2:
time: 631 us; the launch traced here: 623 us
  Pallas kernels  390 us (62%)
  waiting for transfers between devices  76.4 us (12%)
  starting transfers between devices  51.5 us (8%)
  other arithmetic  45.6 us (7%)
  local copies, waits for them, and re-layouts  24.1 us (4%)
  matrix products  20.7 us (3%)
  between operations  15.2 us (2%)
    pallas_call x1, Pallas kernels, attend_back(): pl.pallas_call(functools.partial(attend_back_kernel, block=block, step=st...  94.1 us
    ppermute x45, waiting for transfers between devices, send(): return lax.ppermute(value, axis, pairs)  76.3 us
    pallas_call x4, Pallas kernels, weight_grad(): pl.pallas_call(functools.partial(weight_grad_kernel, count=2, size=size),...  67.7 us
    pallas_call x4, Pallas kernels, closing(): pl.pallas_call(functools.partial(closing_kernel, finish=finish, extras=le...  54.7 us
    ppermute x45, starting transfers between devices, send(): return lax.ppermute(value, axis, pairs)  51.4 us
    pallas_call x2, Pallas kernels, attend(): pl.pallas_call(functools.partial(attend_kernel, block=block, begin=begin)...  45.3 us
    pallas_call x4, Pallas kernels, product_for_other(): pl.pallas_call(product_kernel, grid_spec=pltpu.PrefetchScalarGridSpec(num...  42.2 us
    pallas_call x2, Pallas kernels, hidden_slope(): pl.pallas_call(hidden_kernel, grid=(length // block,), in_specs=[rows(dep...  27.3 us
  transfers between devices with their start and end apart: 47, of which 21 were waited for; matrix products, arithmetic and copies ran while one was open for 12% of the time, Pallas kernels for 56%

profile of v2, /device:TPU:8, one launch (start us, length us, event | category | flops | bytes accessed | tf_op | source)
XLA Modules:
  0.0 622.9 jit_solution(5167983502865625891)
XLA Ops:
  57.4 9.5 %collective-permute-done.5.refs_3_ = bf16[4,80,1920]{2,1,0:T(8,128)(2,1)S(1)} collective-permute-done((bf16[4,80,1920]{2,1,0:T(8,128)(2,1)S(1)}, bf16[4,80,1920]{2,1,0:T(8,128)(2,1)S(1)}, u32[]{:S(2)}, u32[]{:S(2)}) %collective-permute-start.5) | collective-permute-done | bytes 1228832 | tf_op jit(solution)/shard_map/ppermute | solution.py:570
  70.3 8.7 %collective-permute-done.10 = bf16[80,3200]{1,0:T(8,128)(2,1)S(1)} collective-permute-done((bf16[80,3200]{1,0:T(8,128)(2,1)S(1)}, bf16[80,3200]{1,0:T(8,128)(2,1)S(1)}, u32[]{:S(2)}, u32[]{:S(2)}) %collective-permute-start.10) | collective-permute-done | bytes 512032 | tf_op jit(solution)/shard_map/ppermute | solution.py:570
  96.1 19.1 %qkv_rotate.1 = (bf16[2048,640]{1,0:T(8,128)(2,1)}, bf16[2048,640]{1,0:T(8,128)(2,1)}, bf16[2048,640]{1,0:T(8,128)(2,1)}) custom-call(s32[2]{0:T(128)} %pad_add_fusion.where.refs_0_, bf16[1024,1280]{1,0:T(8,128)(2,1)} %fusion.9.own.refs_1_, bf16[1024,1280]{1,0:T(8,128)(2,1)} %collective-permute-done.3.other.refs_2_, bf16[1280,1920]{1,0:T(8,128)(2,1)} %copy-done.1, ...), custom_call_target="tpu_custom_call" | custom-call | flops 1 | bytes 1 | tf_op jit(solution)/shard_map/qkv_rotate/pallas_call | solution.py:298
  115.2 21.9 %attend.2 = (bf16[2048,640]{1,0:T(8,128)(2,1)}, f32[2,8,2048]{2,1,0:T(8,128)}) custom-call(bf16[4,2048,256]{2,1,0:T(8,128)(2,1)} %get-tuple-element.133.refs_0_.mq_ref, bf16[4,2048,256]{2,1,0:T(8,128)(2,1)} %get-tuple-element.134.refs_1_.mk_ref, bf16[2048,640]{1,0:T(8,128)(2,1)} %get-tuple-element.141.refs_2_.q_ref, ...), custom_call_target="tpu_custom_call" | custom-call | flops 1 | bytes 1 | tf_op jit(solution)/shard_map/attend/pallas_call | solution.py:159
  144.8 23.4 %attend.3 = (bf16[2048,640]{1,0:T(8,128)(2,1)}, f32[2,8,2048]{2,1,0:T(8,128)}) custom-call(bf16[4,2048,256]{2,1,0:T(8,128)(2,1)} %get-tuple-element.133.refs_0_.mq_ref, bf16[4,2048,256]{2,1,0:T(8,128)(2,1)} %get-tuple-element.134.refs_1_.mk_ref, bf16[2048,640]{1,0:T(8,128)(2,1)} %get-tuple-element.141.refs_2_.q_ref, ...), custom_call_target="tpu_custom_call" | custom-call | flops 1 | bytes 1 | tf_op jit(solution)/shard_map/attend/pallas_call | solution.py:159
  189.4 9.0 %middle.1 = (f32[1024,1280]{1,0:T(8,128)}, bf16[1024,1280]{1,0:T(8,128)(2,1)}) custom-call(s32[2]{0:T(128)} %pad_add_fusion.where.refs_0_, bf16[2048,640]{1,0:T(8,128)(2,1)} %get-tuple-element.150.x.refs_1_.refs_3_.refs_4_.o_ref, bf16[1280,640]{1,0:T(8,128)(2,1)} %copy-done.2, bf16[1024,1280]{1,0:T(8,128)(2,1)} %collective-permute-done.16.refs_3_, ...), custom_call_target="tpu_custom_call" | custom-call | flops 1 | bytes 1 | tf_op jit(solution)/shard_map/middle/pallas_call | solution.py:479
  199.6 13.5 %hidden_slope.2 = (bf16[1024,2560]{1,0:T(8,128)(2,1)}, bf16[1024,2560]{1,0:T(8,128)(2,1)}) custom-call(bf16[1024,1280]{1,0:T(8,128)(2,1)} %get-tuple-element.154.c.refs_1_, bf16[1280,2560]{1,0:T(8,128)(2,1)} %copy-done, f32[1,2560]{1,0:T(1,128)} %reshape.255.b), custom_call_target="tpu_custom_call" | custom-call | flops 1 | bytes 1 | tf_op jit(solution)/shard_map/hidden_slope/pallas_call | solution.py:325
  213.1 13.8 %hidden_slope.3 = (bf16[1024,2560]{1,0:T(8,128)(2,1)}, bf16[1024,2560]{1,0:T(8,128)(2,1)}) custom-call(bf16[1024,1280]{1,0:T(8,128)(2,1)} %collective-permute-done.17.c.refs_2_, bf16[1280,2560]{1,0:T(8,128)(2,1)} %copy-done, f32[1,2560]{1,0:T(1,128)} %reshape.255.b), custom_call_target="tpu_custom_call" | custom-call | flops 1 | bytes 1 | tf_op jit(solution)/shard_map/hidden_slope/pallas_call | solution.py:325
  227.0 20.1 %weight_grad.4 = (bf16[4,80,2560]{2,1,0:T(8,128)(2,1)}, bf16[4,80,2560]{2,1,0:T(8,128)(2,1)}, bf16[4,80,2560]{2,1,0:T(8,128)(2,1)}, bf16[2,80,2560]{2,1,0:T(8,128)(2,1)}, bf16[2,80,2560]{2,1,0:T(8,128)(2,1)}) custom-call(s32[2]{0:T(128)} %pad_add_fusion.where.refs_0_, bf16[1024,1280]{1,0:T(8,128)(2,1)} %refs_5_.1, ...), custom_call_target="tpu_custom_call" | custom-call | flops 1 | bytes 1 | tf_op jit(solution)/shard_map/weight_grad/pallas_call | solution.py:409
  249.4 12.7 %pre_grad.2 = (bf16[1024,2560]{1,0:T(8,128)(2,1)}, f32[8,2560]{1,0:T(8,128)}) custom-call(bf16[1024,1280]{1,0:T(8,128)(2,1)} %refs_5_.1, bf16[1280,2560]{1,0:T(8,128)(2,1)} %all-gather.2.cloned.1.call-done.w.refs_2_, bf16[1024,2560]{1,0:T(8,128)(2,1)} %get-tuple-element.167.slope), custom_call_target="tpu_custom_call" | custom-call | flops 1 | bytes 1 | tf_op jit(solution)/shard_map/pre_grad/pallas_call | solution.py:352
  262.1 12.6 %pre_grad.3 = (bf16[1024,2560]{1,0:T(8,128)(2,1)}, f32[8,2560]{1,0:T(8,128)}) custom-call(bf16[1024,1280]{1,0:T(8,128)(2,1)} %collective-permute-done.13.refs_2_.g, bf16[1280,2560]{1,0:T(8,128)(2,1)} %all-gather.2.cloned.1.call-done.w.refs_2_, bf16[1024,2560]{1,0:T(8,128)(2,1)} %get-tuple-element.169.slope), custom_call_target="tpu_custom_call" | custom-call | flops 1 | bytes 1 | tf_op jit(solution)/shard_map/pre_grad/pallas_call | solution.py:352
  274.7 12.4 %product_for_other.5 = bf16[1024,1280]{1,0:T(8,128)(2,1)} custom-call(s32[2]{0:T(128)} %pad_add_fusion.where.refs_0_, bf16[1024,2560]{1,0:T(8,128)(2,1)} %get-tuple-element.175.x.refs_4_, bf16[1280,2560]{1,0:T(8,128)(2,1)} %copy-done), custom_call_target="tpu_custom_call" | custom-call | flops 1 | bytes 1 | tf_op jit(solution)/shard_map/product_for_other/pallas_call | solution.py:511
  293.5 20.0 %weight_grad.5 = (bf16[4,80,2560]{2,1,0:T(8,128)(2,1)}, bf16[4,80,2560]{2,1,0:T(8,128)(2,1)}, bf16[4,80,2560]{2,1,0:T(8,128)(2,1)}, bf16[2,80,2560]{2,1,0:T(8,128)(2,1)}, bf16[2,80,2560]{2,1,0:T(8,128)(2,1)}) custom-call(s32[2]{0:T(128)} %pad_add_fusion.where.refs_0_, bf16[1024,1280]{1,0:T(8,128)(2,1)} %get-tuple-element.154.c.refs_1_, ...), custom_call_target="tpu_custom_call" | custom-call | flops 1 | bytes 1 | tf_op jit(solution)/shard_map/weight_grad/pallas_call | solution.py:409
  313.6 12.5 %product_for_other.6 = bf16[1024,1280]{1,0:T(8,128)(2,1)} custom-call(s32[2]{0:T(128)} %pad_add_fusion.where.refs_0_, bf16[1024,2560]{1,0:T(8,128)(2,1)} %get-tuple-element.188.refs_4_.x, bf16[1280,2560]{1,0:T(8,128)(2,1)} %all-gather.2.cloned.1.call-done.w.refs_2_), custom_call_target="tpu_custom_call" | custom-call | flops 1 | bytes 1 | tf_op jit(solution)/shard_map/product_for_other/pallas_call | solution.py:511
  329.0 17.4 %middle_grad.1 = (f32[1024,1280]{1,0:T(8,128)}, bf16[1024,1280]{1,0:T(8,128)(2,1)}, f32[8,1280]{1,0:T(8,128)}, f32[8,1280]{1,0:T(8,128)}, f32[8,1280]{1,0:T(8,128)}, /*index=5*/f32[8,1280]{1,0:T(8,128)}) custom-call(s32[2]{0:T(128)} %pad_add_fusion.where.refs_0_, bf16[1024,2560]{1,0:T(8,128)(2,1)} %get-tuple-element.184.refs_3_.refs_1_, ...), custom_call_target="tpu_custom_call" | custom-call | flops 1 | bytes 1 | tf_op jit(solution)/shard_map/middle_grad/pallas_call | solution.py:479
  346.4 14.0 %output.1 = f32[1024,1280]{1,0:T(8,128)} custom-call(s32[2]{0:T(128)} %pad_add_fusion.where.refs_0_, bf16[1024,2560]{1,0:T(8,128)(2,1)} %get-tuple-element.156.refs_3_.refs_1_, bf16[1280,2560]{1,0:T(8,128)(2,1)} %all-gather.2.cloned.1.call-done.w.refs_2_, bf16[1024,1280]{1,0:T(8,128)(2,1)} %collective-permute-done.25.refs_3_, ...), custom_call_target="tpu_custom_call" | custom-call | flops 1 | bytes 1 | tf_op jit(solution)/shard_map/output/pallas_call | solution.py:479
  372.6 8.9 %mixed_grad.1.g_ref = bf16[2048,640]{1,0:T(8,128)(2,1)} custom-call(s32[2]{0:T(128)} %pad_add_fusion.where.refs_0_, bf16[1024,1280]{1,0:T(8,128)(2,1)} %get-tuple-element.197.own.refs_1_, bf16[1024,1280]{1,0:T(8,128)(2,1)} %collective-permute-done.28.other.refs_2_, bf16[1280,640]{1,0:T(8,128)(2,1)} %copy-done.2), custom_call_target="tpu_custom_call" | custom-call | flops 1 | bytes 1 | tf_op jit(solution)/shard_map/mixed_grad/pallas_call | solution.py:434
  381.5 10.5 %weight_grad.6 = bf16[1280,640]{1,0:T(8,128)(2,1)} custom-call(s32[2]{0:T(128)} %pad_add_fusion.where.refs_0_, bf16[1024,1280]{1,0:T(8,128)(2,1)} %get-tuple-element.197.own.refs_1_, bf16[1024,1280]{1,0:T(8,128)(2,1)} %collective-permute-done.28.other.refs_2_, bf16[2048,640]{1,0:T(8,128)(2,1)} %get-tuple-element.150.x.refs_1_.refs_3_.refs_4_.o_ref, ...), custom_call_target="tpu_custom_call" | custom-call | flops 1 | bytes 1 | tf_op jit(solution)/shard_map/weight_grad/pallas_call | solution.py:409
  408.2 94.1 %attend_back.1.refs_3_.refs_4_.x.refs_1_ = bf16[2048,1920]{1,0:T(8,128)(2,1)} custom-call(bf16[4,2048,256]{2,1,0:T(8,128)(2,1)} %get-tuple-element.133.refs_0_.mq_ref, bf16[4,2048,256]{2,1,0:T(8,128)(2,1)} %get-tuple-element.134.refs_1_.mk_ref, bf16[2048,640]{1,0:T(8,128)(2,1)} %get-tuple-element.141.refs_2_.q_ref, ...), custom_call_target="tpu_custom_call" | custom-call | flops 1 | bytes 1 | tf_op jit(solution)/shard_map/attend_back/pallas_call | solution.py:257
  502.4 17.1 %weight_grad.7 = (bf16[4,80,1920]{2,1,0:T(8,128)(2,1)}, bf16[4,80,1920]{2,1,0:T(8,128)(2,1)}, bf16[4,80,1920]{2,1,0:T(8,128)(2,1)}, bf16[2,80,1920]{2,1,0:T(8,128)(2,1)}, bf16[2,80,1920]{2,1,0:T(8,128)(2,1)}) custom-call(s32[2]{0:T(128)} %pad_add_fusion.where.refs_0_, bf16[1024,1280]{1,0:T(8,128)(2,1)} %fusion.9.own.refs_1_, ...), custom_call_target="tpu_custom_call" | custom-call | flops 1 | bytes 1 | tf_op jit(solution)/shard_map/weight_grad/pallas_call | solution.py:409
  519.5 10.6 %product_for_other.7 = bf16[1024,1280]{1,0:T(8,128)(2,1)} custom-call(s32[2]{0:T(128)} %pad_add_fusion.where.refs_0_, bf16[2048,1920]{1,0:T(8,128)(2,1)} %attend_back.1.refs_3_.refs_4_.x.refs_1_, bf16[1280,1920]{1,0:T(8,128)(2,1)} %copy-done.1), custom_call_target="tpu_custom_call" | custom-call | flops 1 | bytes 1 | tf_op jit(solution)/shard_map/product_for_other/pallas_call | solution.py:511
  537.1 14.2 %input_grad.1 = (f32[1024,1280]{1,0:T(8,128)}, f32[8,1280]{1,0:T(8,128)}, f32[8,1280]{1,0:T(8,128)}) custom-call(s32[2]{0:T(128)} %pad_add_fusion.where.refs_0_, bf16[2048,1920]{1,0:T(8,128)(2,1)} %attend_back.1.refs_3_.refs_4_.x.refs_1_, bf16[1280,1920]{1,0:T(8,128)(2,1)} %copy-done.1, bf16[1024,1280]{1,0:T(8,128)(2,1)} %collective-permute-done.34.refs_3_, ...), custom_call_target="tpu_custom_call" | custom-call | flops 1 | bytes 1 | tf_op jit(solution)/shard_map/input_grad/pallas_call | solution.py:479
  552.9 7.0 %collective-permute-done.32 = bf16[4,80,1920]{2,1,0:T(8,128)(2,1)} collective-permute-done((bf16[4,80,1920]{2,1,0:T(8,128)(2,1)}, bf16[4,80,1920]{2,1,0:T(8,128)(2,1)}, u32[]{:S(2)}, u32[]{:S(2)}) %collective-permute-start.32) | collective-permute-done | bytes 1228832 | tf_op jit(solution)/shard_map/ppermute | solution.py:570
  594.0 15.3 %collective-permute-done.42 = bf16[80,1920]{1,0:T(8,128)(2,1)S(1)} collective-permute-done((bf16[80,1920]{1,0:T(8,128)(2,1)S(1)}, bf16[80,1920]{1,0:T(8,128)(2,1)S(1)}, u32[]{:S(2)}, u32[]{:S(2)}) %collective-permute-start.42) | collective-permute-done | bytes 307232 | tf_op jit(solution)/shard_map/ppermute | solution.py:570
  (260 shorter events, 189.2 us)
Async XLA Ops:
  7.2 239.9 %all-gather.2.cloned.1.call-start = ((), (), s32[]{:S(2)}) async-start(), calls=%async_computation.1 | async-start | bytes 6963200 | tf_op jit(solution)/shard_map/all_gather | solution.py:748
  8.4 26.6 %collective-permute-start.2 = (bf16[80,1920]{1,0:T(8,128)(2,1)S(1)}, bf16[80,1920]{1,0:T(8,128)(2,1)S(1)}, u32[]{:S(2)}, u32[]{:S(2)}) collective-permute-start(bf16[80,1920]{1,0:T(8,128)(2,1)S(1)} %bitcast.73), channel_id=1, source_target_pairs={{0,24},{2,26},{4,28},{6,30},{8,0},{10,2},{12,4},{14,6},{16,8},{18,... | collective-permute-start | bytes 921608 | tf_op jit(solution)/shard_map/ppermute | solution.py:570
  8.4 26.5 %collective-permute-start.1 = (bf16[80,1920]{1,0:T(8,128)(2,1)S(1)}, bf16[80,1920]{1,0:T(8,128)(2,1)S(1)}, u32[]{:S(2)}, u32[]{:S(2)}) collective-permute-start(bf16[80,1920]{1,0:T(8,128)(2,1)S(1)} %bitcast.74), channel_id=1, source_target_pairs={{0,16},{2,18},{4,20},{6,22},{8,24},{10,26},{12,28},{14,30},{16,0},... | collective-permute-start | bytes 921608 | tf_op jit(solution)/shard_map/ppermute | solution.py:570
  38.7 28.2 %collective-permute-start.5 = (bf16[4,80,1920]{2,1,0:T(8,128)(2,1)S(1)}, bf16[4,80,1920]{2,1,0:T(8,128)(2,1)S(1)}, u32[]{:S(2)}, u32[]{:S(2)}) collective-permute-start(bf16[4,80,1920]{2,1,0:T(8,128)(2,1)S(1)} %pad_maximum_fusion.1.refs_1_), channel_id=1, source_target_pairs={{0,4},{2,6},{4,0},{6,2},{8,12},{10,14},{12,8},{14,10},{16,20},{18,... | collective-permute-start | bytes 3686408 | tf_op jit(solution)/shard_map/ppermute | solution.py:570
  40.3 27.9 %collective-permute-start.4 = (bf16[4,80,1920]{2,1,0:T(8,128)(2,1)S(1)}, bf16[4,80,1920]{2,1,0:T(8,128)(2,1)S(1)}, u32[]{:S(2)}, u32[]{:S(2)}) collective-permute-start(bf16[4,80,1920]{2,1,0:T(8,128)(2,1)S(1)} %pad_maximum_fusion.1.refs_1_), channel_id=1, source_target_pairs={{0,2},{2,0},{4,6},{6,4},{8,10},{10,8},{12,14},{14,12},{16,18},{18,... | collective-permute-start | bytes 3686408 | tf_op jit(solution)/shard_map/ppermute | solution.py:570
  41.8 37.2 %collective-permute-start.10 = (bf16[80,3200]{1,0:T(8,128)(2,1)S(1)}, bf16[80,3200]{1,0:T(8,128)(2,1)S(1)}, u32[]{:S(2)}, u32[]{:S(2)}) collective-permute-start(bf16[80,3200]{1,0:T(8,128)(2,1)S(1)} %pad_maximum_fusion.4), channel_id=1, source_target_pairs={{0,24},{2,26},{4,28},{6,30},{8,0},{10,2},{12,4},{14,6},{16,8},{18,... | collective-permute-start | bytes 1536008 | tf_op jit(solution)/shard_map/ppermute | solution.py:570
  43.0 36.0 %collective-permute-start.9 = (bf16[80,3200]{1,0:T(8,128)(2,1)S(1)}, bf16[80,3200]{1,0:T(8,128)(2,1)S(1)}, u32[]{:S(2)}, u32[]{:S(2)}) collective-permute-start(bf16[80,3200]{1,0:T(8,128)(2,1)S(1)} %pad_maximum_fusion.4), channel_id=1, source_target_pairs={{0,16},{2,18},{4,20},{6,22},{8,24},{10,26},{12,28},{14,30},{16,0},... | collective-permute-start | bytes 1536008 | tf_op jit(solution)/shard_map/ppermute | solution.py:570
  45.9 39.3 %collective-permute-start.8 = (bf16[80,3200]{1,0:T(8,128)(2,1)S(1)}, bf16[80,3200]{1,0:T(8,128)(2,1)S(1)}, u32[]{:S(2)}, u32[]{:S(2)}) collective-permute-start(bf16[80,3200]{1,0:T(8,128)(2,1)S(1)} %pad_maximum_fusion.4), channel_id=1, source_target_pairs={{0,8},{2,10},{4,12},{6,14},{8,16},{10,18},{12,20},{14,22},{16,24},... | collective-permute-start | bytes 1536008 | tf_op jit(solution)/shard_map/ppermute | solution.py:570
  87.7 49.4 %collective-permute-start.12 = (bf16[4,80,3200]{2,1,0:T(8,128)(2,1)}, bf16[4,80,3200]{2,1,0:T(8,128)(2,1)}, u32[]{:S(2)}, u32[]{:S(2)}) collective-permute-start(bf16[4,80,3200]{2,1,0:T(8,128)(2,1)} %pad_maximum_fusion.refs_1_), channel_id=1, source_target_pairs={{0,4},{2,6},{4,0},{6,2},{8,12},{10,14},{12,8},{14,10},{16,20},{18,... | collective-permute-start | bytes 6144008 | tf_op jit(solution)/shard_map/ppermute | solution.py:570
  88.3 48.9 %collective-permute-start.11 = (bf16[4,80,3200]{2,1,0:T(8,128)(2,1)}, bf16[4,80,3200]{2,1,0:T(8,128)(2,1)}, u32[]{:S(2)}, u32[]{:S(2)}) collective-permute-start(bf16[4,80,3200]{2,1,0:T(8,128)(2,1)} %pad_maximum_fusion.refs_1_), channel_id=1, source_target_pairs={{0,2},{2,0},{4,6},{6,4},{8,10},{10,8},{12,14},{14,12},{16,18},{18,... | collective-permute-start | bytes 6144008 | tf_op jit(solution)/shard_map/ppermute | solution.py:570
  137.2 365.2 %reduce-scatter.2.cloned.1.call-start = ((), (), s32[]{:S(2)}) async-start(), calls=%async_computation.2 | async-start | bytes 1740800 | tf_op jit(solution)/shard_map/reduce_scatter | solution.py:795
  141.8 27.1 %collective-permute-start.15 = (bf16[2,80,3200]{2,1,0:T(8,128)(2,1)}, bf16[2,80,3200]{2,1,0:T(8,128)(2,1)S(1)}, u32[]{:S(2)}, u32[]{:S(2)}) collective-permute-start(bf16[2,80,3200]{2,1,0:T(8,128)(2,1)} %slice.177), channel_id=1, source_target_pairs={{0,2},{2,0},{4,6},{6,4},{8,10},{10,8},{12,14},{14,12},{16,18},{18,... | collective-permute-start | bytes 3072008 | tf_op jit(solution)/shard_map/ppermute | solution.py:570
  143.2 26.9 %collective-permute-start.14 = (bf16[2,80,3200]{2,1,0:T(8,128)(2,1)}, bf16[2,80,3200]{2,1,0:T(8,128)(2,1)}, u32[]{:S(2)}, u32[]{:S(2)}) collective-permute-start(bf16[2,80,3200]{2,1,0:T(8,128)(2,1)} %slice.176), channel_id=1, source_target_pairs={{0,4},{2,6},{4,0},{6,2},{8,12},{10,14},{12,8},{14,10},{16,20},{18,... | collective-permute-start | bytes 3072008 | tf_op jit(solution)/shard_map/ppermute | solution.py:570
  198.6 28.4 %collective-permute-start.13 = (bf16[1024,1280]{1,0:T(8,128)(2,1)}, bf16[1024,1280]{1,0:T(8,128)(2,1)}, u32[]{:S(2)}, u32[]{:S(2)}) collective-permute-start(bf16[1024,1280]{1,0:T(8,128)(2,1)} %refs_5_.1), channel_id=1, source_target_pairs={{0,1},{1,0},{2,3},{3,2},{4,5},{5,4},{6,7},{7,6},{8,9},{9,8},{10,11... | collective-permute-start | bytes 7864328 | tf_op jit(solution)/shard_map/ppermute | solution.py:570
  247.1 40.1 %collective-permute-start.18 = (bf16[4,80,2560]{2,1,0:T(8,128)(2,1)}, bf16[4,80,2560]{2,1,0:T(8,128)(2,1)S(1)}, u32[]{:S(2)}, u32[]{:S(2)}) collective-permute-start(bf16[4,80,2560]{2,1,0:T(8,128)(2,1)} %get-tuple-element.164), channel_id=1, source_target_pairs={{0,2},{2,0},{4,6},{6,4},{8,10},{10,8},{12,14},{14,12},{16,18},{18,... | collective-permute-start | bytes 4915208 | tf_op jit(solution)/shard_map/ppermute | solution.py:570
  247.9 39.2 %collective-permute-start.19 = (bf16[4,80,2560]{2,1,0:T(8,128)(2,1)}, bf16[4,80,2560]{2,1,0:T(8,128)(2,1)}, u32[]{:S(2)}, u32[]{:S(2)}) collective-permute-start(bf16[4,80,2560]{2,1,0:T(8,128)(2,1)} %get-tuple-element.165), channel_id=1, source_target_pairs={{0,4},{2,6},{4,0},{6,2},{8,12},{10,14},{12,8},{14,10},{16,20},{18,... | collective-permute-start | bytes 4915208 | tf_op jit(solution)/shard_map/ppermute | solution.py:570
  287.1 26.4 %collective-permute-start.22 = (bf16[1024,1280]{1,0:T(8,128)(2,1)}, bf16[1024,1280]{1,0:T(8,128)(2,1)}, u32[]{:S(2)}, u32[]{:S(2)}) collective-permute-start(bf16[1024,1280]{1,0:T(8,128)(2,1)} %product_for_other.5), channel_id=1, source_target_pairs={{0,1},{1,0},{2,3},{3,2},{4,5},{5,4},{6,7},{7,6},{8,9},{9,8},{10,11... | collective-permute-start | bytes 7864328 | tf_op jit(solution)/shard_map/ppermute | solution.py:570
  326.1 38.5 %collective-permute-start.23 = (bf16[4,80,2560]{2,1,0:T(8,128)(2,1)}, bf16[4,80,2560]{2,1,0:T(8,128)(2,1)}, u32[]{:S(2)}, u32[]{:S(2)}) collective-permute-start(bf16[4,80,2560]{2,1,0:T(8,128)(2,1)} %get-tuple-element.182), channel_id=1, source_target_pairs={{0,2},{2,0},{4,6},{6,4},{8,10},{10,8},{12,14},{14,12},{16,18},{18,... | collective-permute-start | bytes 4915208 | tf_op jit(solution)/shard_map/ppermute | solution.py:570
  326.9 38.2 %collective-permute-start.24 = (bf16[4,80,2560]{2,1,0:T(8,128)(2,1)}, bf16[4,80,2560]{2,1,0:T(8,128)(2,1)}, u32[]{:S(2)}, u32[]{:S(2)}) collective-permute-start(bf16[4,80,2560]{2,1,0:T(8,128)(2,1)} %get-tuple-element.183), channel_id=1, source_target_pairs={{0,4},{2,6},{4,0},{6,2},{8,12},{10,14},{12,8},{14,10},{16,20},{18,... | collective-permute-start | bytes 4915208 | tf_op jit(solution)/shard_map/ppermute | solution.py:570
  398.5 103.9 %collective-permute-start.29 = (bf16[80,5120]{1,0:T(8,128)(2,1)}, bf16[80,5120]{1,0:T(8,128)(2,1)}, u32[]{:S(2)}, u32[]{:S(2)}) collective-permute-start(bf16[80,5120]{1,0:T(8,128)(2,1)} %get-tuple-element.287), channel_id=1, source_target_pairs={{0,8},{2,10},{4,12},{6,14},{8,16},{10,18},{12,20},{14,22},{16,24},... | collective-permute-start | bytes 2457608 | tf_op jit(solution)/shard_map/ppermute | solution.py:570
  403.4 98.9 %collective-permute-start.31 = (bf16[80,5120]{1,0:T(8,128)(2,1)}, bf16[80,5120]{1,0:T(8,128)(2,1)}, u32[]{:S(2)}, u32[]{:S(2)}) collective-permute-start(bf16[80,5120]{1,0:T(8,128)(2,1)} %get-tuple-element.288), channel_id=1, source_target_pairs={{0,24},{2,26},{4,28},{6,30},{8,0},{10,2},{12,4},{14,6},{16,8},{18,... | collective-permute-start | bytes 2457608 | tf_op jit(solution)/shard_map/ppermute | solution.py:570
  405.1 97.2 %collective-permute-start.30 = (bf16[80,5120]{1,0:T(8,128)(2,1)}, bf16[80,5120]{1,0:T(8,128)(2,1)}, u32[]{:S(2)}, u32[]{:S(2)}) collective-permute-start(bf16[80,5120]{1,0:T(8,128)(2,1)} %get-tuple-element.289), channel_id=1, source_target_pairs={{0,16},{2,18},{4,20},{6,22},{8,24},{10,26},{12,28},{14,30},{16,0},... | collective-permute-start | bytes 2457608 | tf_op jit(solution)/shard_map/ppermute | solution.py:570
  530.2 29.7 %collective-permute-start.32 = (bf16[4,80,1920]{2,1,0:T(8,128)(2,1)}, bf16[4,80,1920]{2,1,0:T(8,128)(2,1)}, u32[]{:S(2)}, u32[]{:S(2)}) collective-permute-start(bf16[4,80,1920]{2,1,0:T(8,128)(2,1)} %get-tuple-element.212), channel_id=1, source_target_pairs={{0,2},{2,0},{4,6},{6,4},{8,10},{10,8},{12,14},{14,12},{16,18},{18,... | collective-permute-start | bytes 3686408 | tf_op jit(solution)/shard_map/ppermute | solution.py:570
  531.5 29.5 %collective-permute-start.33 = (bf16[4,80,1920]{2,1,0:T(8,128)(2,1)}, bf16[4,80,1920]{2,1,0:T(8,128)(2,1)}, u32[]{:S(2)}, u32[]{:S(2)}) collective-permute-start(bf16[4,80,1920]{2,1,0:T(8,128)(2,1)} %get-tuple-element.213), channel_id=1, source_target_pairs={{0,4},{2,6},{4,0},{6,2},{8,12},{10,14},{12,8},{14,10},{16,20},{18,... | collective-permute-start | bytes 3686408 | tf_op jit(solution)/shard_map/ppermute | solution.py:570
  (59 other events, 599.0 us)
Sparse Core Ops, SparseCore 0:
  137.3 100.1 all-gather.1
  392.2 104.3 reduce-scatter.1

commit v3 on v2

--- a/solution.py
+++ b/solution.py
@@ -21,6 +21,7 @@
 
 INSTANT = pl.CostEstimate(flops=1, bytes_accessed=1, transcendentals=0)
 ROOMY = pltpu.CompilerParams(vmem_limit_bytes=62 * 2**20)
+MODEST = pltpu.CompilerParams(vmem_limit_bytes=32 * 2**20)
 
 
 def mm(left, right, dims):
@@ -416,7 +417,7 @@
             scratch_shapes=scratch,
         ),
         out_shape=out_shape,
-        compiler_params=ROOMY,
+        compiler_params=MODEST if wide < high else ROOMY,
         cost_estimate=INSTANT,
         name="weight_grad",
     )(where, *lefts, *rights)
@@ -446,7 +447,7 @@
             ),
         ),
         out_shape=jax.ShapeDtypeStruct((2 * half, wide), bf16),
-        compiler_params=ROOMY,
+        compiler_params=MODEST,
         cost_estimate=INSTANT,
         name="mixed_grad",
     )(where, own, other, w)
@@ -493,7 +494,7 @@
         ),
         out_shape=[jax.ShapeDtypeStruct((half, model), kind) for kind in kinds]
         + [jax.ShapeDtypeStruct((8, model), f32)] * sums,
-        compiler_params=ROOMY,
+        compiler_params=MODEST if depth < model else ROOMY,
         cost_estimate=INSTANT,
         name=name,
     )(where, x, w, *rows, *[vector.reshape(1, model) for vector in vectors])
@@ -520,7 +521,7 @@
             out_specs=pl.BlockSpec((block, model), lambda i, w: (i, 0)),
         ),
         out_shape=jax.ShapeDtypeStruct((half, model), bf16),
-        compiler_params=ROOMY,
+        compiler_params=MODEST if depth < w.shape[0] else ROOMY,
         cost_estimate=INSTANT,
         name="product_for_other",
     )(where, x, w)
@@ -680,8 +681,14 @@
     return sum((part.astype(f32) for part in got), own.astype(f32))
 
 
-def sum_everywhere(value, size):
-    for bit in [1 << i for i in range(size.bit_length() - 1)]:
+def sum_slow(value, size):
+    for bit in [1 << i for i in range(size.bit_length() - 1)][2:]:
+        value = value + send(value, flip(size, bit))
+    return value
+
+
+def sum_fast(value, size):
+    for bit in (1, 2):
         value = value + send(value, flip(size, bit))
     return value + send(value, [(0, 1), (1, 0)], "tensor")
 
@@ -805,16 +812,6 @@
         where, qkv_grad, qkv_full, [cross(part), tokens, middle_grad], [gain_one],
         finish_input, [f32], 2, "input_grad",
     )
-    qkv_got, input_grad, qkv_shift_grad, gain_one_grad = tie(
-        qkv_got, input_grad, qkv_shift_grad, gain_one_grad
-    )
-    more = scatter_near(qkv_stacks, qkv_got, size)
-    both_shards = scatter_last(kept, got)
-    fc2_shard, fc1_shard = both_shards[:, :units], both_shards[:, units:]
-    more, fc2_shard, fc1_shard = tie(more, fc2_shard, fc1_shard)
-    kept, got = scatter_slow([(qkv_stacks, qkv_got, more)], size)
-    qkv_shard = scatter_last(kept, got)
-
     fc1_shift_grad = jnp.sum(bias_own, axis=0) + jnp.sum(bias_other, axis=0)
     fc1_place = lax.dynamic_update_slice_in_dim(
         jnp.zeros((2 * units,), f32), fc1_shift_grad, me * units, 0
@@ -826,7 +823,16 @@
         gain_one_grad, shift_one_grad, qkv_place.reshape(-1), proj_shift_grad,
         gain_two_grad, shift_two_grad, fc1_place, fc2_shift_grad,
     ]
-    totals = sum_everywhere(jnp.concatenate(sums).reshape(-1, 128), size).reshape(-1)
+    totals = sum_slow(jnp.concatenate(sums).reshape(-1, 128), size)
+    qkv_got, input_grad, totals = tie(qkv_got, input_grad, totals)
+    more = scatter_near(qkv_stacks, qkv_got, size)
+    more, kept, got, totals = tie(more, kept, got, totals)
+    qkv_kept, qkv_got = scatter_slow([(qkv_stacks, qkv_got, more)], size)
+    both_shards = scatter_last(kept, got)
+    fc2_shard, fc1_shard = both_shards[:, :units], both_shards[:, units:]
+    totals = sum_fast(totals, size).reshape(-1)
+    qkv_got, totals, fc2_shard, fc1_shard = tie(qkv_got, totals, fc2_shard, fc1_shard)
+    qkv_shard = scatter_last(qkv_kept, qkv_got)
     small = []
     for part in sums:
         small.append(totals[: part.shape[0]])

time: 631 us -> 638 us (1.011)
  waiting for transfers between devices: 76.4 us -> 90.1 us
  Pallas kernels: 390 us -> 377 us
  local copies, waits for them, and re-layouts: 24.1 us -> 36.3 us
  starting transfers between devices: 51.5 us -> 43.8 us
    unnamed x81 -> x111, local copies, waits for them, and re-layouts: 10.3 us -> 24.4 us
    ppermute x45, waiting for transfers between devices: 76.3 us -> 87.6 us  [send(): return lax.ppermute(value, axis, pairs)]
    ppermute x45, starting transfers between devices: 51.4 us -> 43.7 us  [send(): return lax.ppermute(value, axis, pairs)]
  transfers between devices with their start and end apart: 47 -> 47, of which waited for: 21 -> 21; matrix products, arithmetic and copies ran while one was open for 12% -> 11% of each run, Pallas kernels for 56% -> 54%
where the time goes in v3:
time: 638 us; the launch traced here: 629 us
  Pallas kernels  377 us (59%)
  waiting for transfers between devices  90.1 us (14%)
  other arithmetic  45.9 us (7%)
  starting transfers between devices  43.8 us (7%)
  local copies, waits for them, and re-layouts  36.3 us (6%)
  matrix products  20.7 us (3%)
  between operations  15.3 us (2%)
    pallas_call x1, Pallas kernels, attend_back(): pl.pallas_call(functools.partial(attend_back_kernel, block=block, step=st...  94.2 us
    ppermute x45, waiting for transfers between devices, send(): return lax.ppermute(value, axis, pairs)  87.6 us
    pallas_call x4, Pallas kernels, weight_grad(): pl.pallas_call(functools.partial(weight_grad_kernel, count=2, size=size),...  64.2 us
    pallas_call x4, Pallas kernels, closing(): pl.pallas_call(functools.partial(closing_kernel, finish=finish, extras=le...  51.7 us
    pallas_call x2, Pallas kernels, attend(): pl.pallas_call(functools.partial(attend_kernel, block=block, begin=begin)...  45.4 us
    ppermute x45, starting transfers between devices, send(): return lax.ppermute(value, axis, pairs)  43.7 us
    pallas_call x4, Pallas kernels, product_for_other(): pl.pallas_call(product_kernel, grid_spec=pltpu.PrefetchScalarGridSpec(num...  38.9 us
    pallas_call x2, Pallas kernels, hidden_slope(): pl.pallas_call(hidden_kernel, grid=(length // block,), in_specs=[rows(dep...  28.3 us
  transfers between devices with their start and end apart: 47, of which 21 were waited for; matrix products, arithmetic and copies ran while one was open for 11% of the time, Pallas kernels for 54%

profile of v3, /device:TPU:8, one launch (start us, length us, event | category | flops | bytes accessed | tf_op | source)
XLA Modules:
  0.0 629.4 jit_solution(2321991329936667671)
XLA Ops:
  20.3 6.9 %fusion.18.cos.cos_ref = f32[2048,640]{1,0:T(8,128)} fusion(f32[2048,20]{0,1:T(8,128)S(1)} %get-tuple-element.327, f32[2048,20]{0,1:T(8,128)S(1)} %get-tuple-element.326, s32[640]{0:T(1024)S(1)} %add_select_fusion.1, s32[40]{0:T(128)S(1)} %iota_add_fusion), kind=kOutput, calls=%fused_computation.48 | convolution fusion | flops 629355520 | bytes 5573280 | tf_op jit(solution)/shard_map/dot_general | solution.py:63
  27.2 6.9 %fusion.23.down.down_ref = f32[2048,640]{1,0:T(8,128)} fusion(f32[2048,20]{0,1:T(8,128)S(1)} %get-tuple-element.327, f32[2048,20]{0,1:T(8,128)S(1)} %get-tuple-element.326, s32[640]{0:T(1024)S(1)} %add_select_fusion.1), kind=kOutput, calls=%fused_computation.57 | convolution fusion | flops 629304320 | bytes 5573120 | tf_op jit(solution)/shard_map/dot_general | solution.py:63
  57.5 10.9 %collective-permute-done.4.refs_2_ = bf16[4,80,1920]{2,1,0:T(8,128)(2,1)S(1)} collective-permute-done((bf16[4,80,1920]{2,1,0:T(8,128)(2,1)S(1)}, bf16[4,80,1920]{2,1,0:T(8,128)(2,1)S(1)}, u32[]{:S(2)}, u32[]{:S(2)}) %collective-permute-start.4) | collective-permute-done | bytes 1228832 | tf_op jit(solution)/shard_map/ppermute | solution.py:571
  71.9 14.4 %collective-permute-done.9 = bf16[80,3200]{1,0:T(8,128)(2,1)S(1)} collective-permute-done((bf16[80,3200]{1,0:T(8,128)(2,1)S(1)}, bf16[80,3200]{1,0:T(8,128)(2,1)S(1)}, u32[]{:S(2)}, u32[]{:S(2)}) %collective-permute-start.9) | collective-permute-done | bytes 512032 | tf_op jit(solution)/shard_map/ppermute | solution.py:571
  98.0 19.1 %qkv_rotate.1 = (bf16[2048,640]{1,0:T(8,128)(2,1)}, bf16[2048,640]{1,0:T(8,128)(2,1)}, bf16[2048,640]{1,0:T(8,128)(2,1)}) custom-call(s32[2]{0:T(128)} %pad_add_fusion.where.refs_0_, bf16[1024,1280]{1,0:T(8,128)(2,1)} %fusion.9.own.refs_1_, bf16[1024,1280]{1,0:T(8,128)(2,1)} %collective-permute-done.3.other.refs_2_, bf16[1280,1920]{1,0:T(8,128)(2,1)} %copy-done.1, ...), custom_call_target="tpu_custom_call" | custom-call | flops 1 | bytes 1 | tf_op jit(solution)/shard_map/qkv_rotate/pallas_call | solution.py:299
  117.2 21.9 %attend.2 = (bf16[2048,640]{1,0:T(8,128)(2,1)}, f32[2,8,2048]{2,1,0:T(8,128)}) custom-call(bf16[4,2048,256]{2,1,0:T(8,128)(2,1)} %get-tuple-element.141.refs_0_.mq_ref, bf16[4,2048,256]{2,1,0:T(8,128)(2,1)} %get-tuple-element.142.refs_1_.mk_ref, bf16[2048,640]{1,0:T(8,128)(2,1)} %get-tuple-element.149.refs_2_.q_ref, ...), custom_call_target="tpu_custom_call" | custom-call | flops 1 | bytes 1 | tf_op jit(solution)/shard_map/attend/pallas_call | solution.py:160
  146.6 23.5 %attend.3 = (bf16[2048,640]{1,0:T(8,128)(2,1)}, f32[2,8,2048]{2,1,0:T(8,128)}) custom-call(bf16[4,2048,256]{2,1,0:T(8,128)(2,1)} %get-tuple-element.141.refs_0_.mq_ref, bf16[4,2048,256]{2,1,0:T(8,128)(2,1)} %get-tuple-element.142.refs_1_.mk_ref, bf16[2048,640]{1,0:T(8,128)(2,1)} %get-tuple-element.149.refs_2_.q_ref, ...), custom_call_target="tpu_custom_call" | custom-call | flops 1 | bytes 1 | tf_op jit(solution)/shard_map/attend/pallas_call | solution.py:160
  197.4 14.4 %hidden_slope.2 = (bf16[1024,2560]{1,0:T(8,128)(2,1)}, bf16[1024,2560]{1,0:T(8,128)(2,1)}) custom-call(bf16[1024,1280]{1,0:T(8,128)(2,1)} %get-tuple-element.162.c.refs_1_, bf16[1280,2560]{1,0:T(8,128)(2,1)} %copy-done, f32[1,2560]{1,0:T(1,128)} %reshape.248.b), custom_call_target="tpu_custom_call" | custom-call | flops 1 | bytes 1 | tf_op jit(solution)/shard_map/hidden_slope/pallas_call | solution.py:326
  211.9 13.9 %hidden_slope.3 = (bf16[1024,2560]{1,0:T(8,128)(2,1)}, bf16[1024,2560]{1,0:T(8,128)(2,1)}) custom-call(bf16[1024,1280]{1,0:T(8,128)(2,1)} %collective-permute-done.17.c.refs_2_, bf16[1280,2560]{1,0:T(8,128)(2,1)} %copy-done, f32[1,2560]{1,0:T(1,128)} %reshape.248.b), custom_call_target="tpu_custom_call" | custom-call | flops 1 | bytes 1 | tf_op jit(solution)/shard_map/hidden_slope/pallas_call | solution.py:326
  225.7 20.1 %weight_grad.4 = (bf16[4,80,2560]{2,1,0:T(8,128)(2,1)}, bf16[4,80,2560]{2,1,0:T(8,128)(2,1)}, bf16[4,80,2560]{2,1,0:T(8,128)(2,1)}, bf16[2,80,2560]{2,1,0:T(8,128)(2,1)}, bf16[2,80,2560]{2,1,0:T(8,128)(2,1)}) custom-call(s32[2]{0:T(128)} %pad_add_fusion.where.refs_0_, bf16[1024,1280]{1,0:T(8,128)(2,1)} %refs_5_.1, ...), custom_call_target="tpu_custom_call" | custom-call | flops 1 | bytes 1 | tf_op jit(solution)/shard_map/weight_grad/pallas_call | solution.py:410
  247.8 12.7 %pre_grad.2 = (bf16[1024,2560]{1,0:T(8,128)(2,1)}, f32[8,2560]{1,0:T(8,128)}) custom-call(bf16[1024,1280]{1,0:T(8,128)(2,1)} %refs_5_.1, bf16[1280,2560]{1,0:T(8,128)(2,1)} %all-gather.2.cloned.1.call-done.w.refs_2_, bf16[1024,2560]{1,0:T(8,128)(2,1)} %get-tuple-element.175.slope), custom_call_target="tpu_custom_call" | custom-call | flops 1 | bytes 1 | tf_op jit(solution)/shard_map/pre_grad/pallas_call | solution.py:353
  260.5 12.6 %pre_grad.3 = (bf16[1024,2560]{1,0:T(8,128)(2,1)}, f32[8,2560]{1,0:T(8,128)}) custom-call(bf16[1024,1280]{1,0:T(8,128)(2,1)} %collective-permute-done.13.refs_2_.g, bf16[1280,2560]{1,0:T(8,128)(2,1)} %all-gather.2.cloned.1.call-done.w.refs_2_, bf16[1024,2560]{1,0:T(8,128)(2,1)} %get-tuple-element.177.slope), custom_call_target="tpu_custom_call" | custom-call | flops 1 | bytes 1 | tf_op jit(solution)/shard_map/pre_grad/pallas_call | solution.py:353
  273.2 12.4 %product_for_other.5 = bf16[1024,1280]{1,0:T(8,128)(2,1)} custom-call(s32[2]{0:T(128)} %pad_add_fusion.where.refs_0_, bf16[1024,2560]{1,0:T(8,128)(2,1)} %get-tuple-element.183.x.refs_4_, bf16[1280,2560]{1,0:T(8,128)(2,1)} %copy-done), custom_call_target="tpu_custom_call" | custom-call | flops 1 | bytes 1 | tf_op jit(solution)/shard_map/product_for_other/pallas_call | solution.py:512
  292.5 20.0 %weight_grad.5 = (bf16[4,80,2560]{2,1,0:T(8,128)(2,1)}, bf16[4,80,2560]{2,1,0:T(8,128)(2,1)}, bf16[4,80,2560]{2,1,0:T(8,128)(2,1)}, bf16[2,80,2560]{2,1,0:T(8,128)(2,1)}, bf16[2,80,2560]{2,1,0:T(8,128)(2,1)}) custom-call(s32[2]{0:T(128)} %pad_add_fusion.where.refs_0_, bf16[1024,1280]{1,0:T(8,128)(2,1)} %get-tuple-element.162.c.refs_1_, ...), custom_call_target="tpu_custom_call" | custom-call | flops 1 | bytes 1 | tf_op jit(solution)/shard_map/weight_grad/pallas_call | solution.py:410
  312.7 12.5 %product_for_other.6 = bf16[1024,1280]{1,0:T(8,128)(2,1)} custom-call(s32[2]{0:T(128)} %pad_add_fusion.where.refs_0_, bf16[1024,2560]{1,0:T(8,128)(2,1)} %get-tuple-element.196.refs_4_.x, bf16[1280,2560]{1,0:T(8,128)(2,1)} %all-gather.2.cloned.1.call-done.w.refs_2_), custom_call_target="tpu_custom_call" | custom-call | flops 1 | bytes 1 | tf_op jit(solution)/shard_map/product_for_other/pallas_call | solution.py:512
  327.6 17.4 %middle_grad.1 = (f32[1024,1280]{1,0:T(8,128)}, bf16[1024,1280]{1,0:T(8,128)(2,1)}, f32[8,1280]{1,0:T(8,128)}, f32[8,1280]{1,0:T(8,128)}, f32[8,1280]{1,0:T(8,128)}, /*index=5*/f32[8,1280]{1,0:T(8,128)}) custom-call(s32[2]{0:T(128)} %pad_add_fusion.where.refs_0_, bf16[1024,2560]{1,0:T(8,128)(2,1)} %get-tuple-element.192.refs_3_.refs_1_, ...), custom_call_target="tpu_custom_call" | custom-call | flops 1 | bytes 1 | tf_op jit(solution)/shard_map/middle_grad/pallas_call | solution.py:480
  345.1 14.0 %output.1 = f32[1024,1280]{1,0:T(8,128)} custom-call(s32[2]{0:T(128)} %pad_add_fusion.where.refs_0_, bf16[1024,2560]{1,0:T(8,128)(2,1)} %get-tuple-element.164.refs_3_.refs_1_, bf16[1280,2560]{1,0:T(8,128)(2,1)} %all-gather.2.cloned.1.call-done.w.refs_2_, bf16[1024,1280]{1,0:T(8,128)(2,1)} %collective-permute-done.25.refs_3_, f32[1024,1280]{1,0:T(8,128)} %copy-done.6, ...), custom_call_target="tpu_custom_call" | custom-call | flops 1 | bytes 1 | tf_op jit(solution)/shard_map/output/pallas_call | solution.py:480
  372.5 7.0 %weight_grad.6 = bf16[1280,640]{1,0:T(8,128)(2,1)S(1)} custom-call(s32[2]{0:T(128)S(1)} %copy-done.20, bf16[1024,1280]{1,0:T(8,128)(2,1)S(1)} %copy-done.8, bf16[1024,1280]{1,0:T(8,128)(2,1)S(1)} %collective-permute-done.28.other.refs_2_, bf16[2048,640]{1,0:T(8,128)(2,1)S(1)} %copy-done.3, bf16[2048,640]{1,0:T(8,128)(2,1)S(1)} %copy-done.3), custom_call_target="tpu_custom_call" | custom-call | flops 1 | bytes 1 | tf_op jit(solution)/shard_map/weight_grad/pallas_call | solution.py:410
  405.3 94.2 %attend_back.1.refs_3_.refs_4_.x.refs_1_ = bf16[2048,1920]{1,0:T(8,128)(2,1)} custom-call(bf16[4,2048,256]{2,1,0:T(8,128)(2,1)} %get-tuple-element.141.refs_0_.mq_ref, bf16[4,2048,256]{2,1,0:T(8,128)(2,1)} %get-tuple-element.142.refs_1_.mk_ref, bf16[2048,640]{1,0:T(8,128)(2,1)} %get-tuple-element.149.refs_2_.q_ref, ...), custom_call_target="tpu_custom_call" | custom-call | flops 1 | bytes 1 | tf_op jit(solution)/shard_map/attend_back/pallas_call | solution.py:258
  501.9 17.1 %weight_grad.7 = (bf16[4,80,1920]{2,1,0:T(8,128)(2,1)}, bf16[4,80,1920]{2,1,0:T(8,128)(2,1)}, bf16[4,80,1920]{2,1,0:T(8,128)(2,1)}, bf16[2,80,1920]{2,1,0:T(8,128)(2,1)}, bf16[2,80,1920]{2,1,0:T(8,128)(2,1)}) custom-call(s32[2]{0:T(128)} %pad_add_fusion.where.refs_0_, bf16[1024,1280]{1,0:T(8,128)(2,1)} %fusion.9.own.refs_1_, ...), custom_call_target="tpu_custom_call" | custom-call | flops 1 | bytes 1 | tf_op jit(solution)/shard_map/weight_grad/pallas_call | solution.py:410
  519.1 10.6 %product_for_other.7 = bf16[1024,1280]{1,0:T(8,128)(2,1)} custom-call(s32[2]{0:T(128)} %pad_add_fusion.where.refs_0_, bf16[2048,1920]{1,0:T(8,128)(2,1)} %attend_back.1.refs_3_.refs_4_.x.refs_1_, bf16[1280,1920]{1,0:T(8,128)(2,1)} %copy-done.1), custom_call_target="tpu_custom_call" | custom-call | flops 1 | bytes 1 | tf_op jit(solution)/shard_map/product_for_other/pallas_call | solution.py:512
  536.8 14.4 %input_grad.1 = (f32[1024,1280]{1,0:T(8,128)}, f32[8,1280]{1,0:T(8,128)}, f32[8,1280]{1,0:T(8,128)}) custom-call(s32[2]{0:T(128)} %pad_add_fusion.where.refs_0_, bf16[2048,1920]{1,0:T(8,128)(2,1)} %attend_back.1.refs_3_.refs_4_.x.refs_1_, bf16[1280,1920]{1,0:T(8,128)(2,1)} %copy-done.1, bf16[1024,1280]{1,0:T(8,128)(2,1)} %collective-permute-done.34.refs_3_, ...), custom_call_target="tpu_custom_call" | custom-call | flops 1 | bytes 1 | tf_op jit(solution)/shard_map/input_grad/pallas_call | solution.py:480
  571.5 10.4 %collective-permute-done.38 = bf16[2,80,1920]{2,1,0:T(8,128)(2,1)S(1)} collective-permute-done((bf16[2,80,1920]{2,1,0:T(8,128)(2,1)S(1)}, bf16[2,80,1920]{2,1,0:T(8,128)(2,1)S(1)}, u32[]{:S(2)}, u32[]{:S(2)}) %collective-permute-start.38) | collective-permute-done | bytes 614432 | tf_op jit(solution)/shard_map/ppermute | solution.py:571
  597.9 15.2 %collective-permute-done.40 = bf16[80,1920]{1,0:T(8,128)(2,1)S(1)} collective-permute-done((bf16[80,1920]{1,0:T(8,128)(2,1)S(1)}, bf16[80,1920]{1,0:T(8,128)(2,1)S(1)}, u32[]{:S(2)}, u32[]{:S(2)}) %collective-permute-start.40) | collective-permute-done | bytes 307232 | tf_op jit(solution)/shard_map/ppermute | solution.py:571
  (290 shorter events, 191.7 us)
Async XLA Ops:
  7.2 238.6 %all-gather.2.cloned.1.call-start = ((), (), s32[]{:S(2)}) async-start(), calls=%async_computation.1 | async-start | bytes 6963200 | tf_op jit(solution)/shard_map/all_gather | solution.py:755
  10.0 26.3 %collective-permute-start.1 = (bf16[80,1920]{1,0:T(8,128)(2,1)S(1)}, bf16[80,1920]{1,0:T(8,128)(2,1)S(1)}, u32[]{:S(2)}, u32[]{:S(2)}) collective-permute-start(bf16[80,1920]{1,0:T(8,128)(2,1)S(1)} %bitcast.62), channel_id=1, source_target_pairs={{0,16},{2,18},{4,20},{6,22},{8,24},{10,26},{12,28},{14,30},{16,0},... | collective-permute-start | bytes 921608 | tf_op jit(solution)/shard_map/ppermute | solution.py:571
  11.1 27.1 %collective-permute-start.2 = (bf16[80,1920]{1,0:T(8,128)(2,1)S(1)}, bf16[80,1920]{1,0:T(8,128)(2,1)}, u32[]{:S(2)}, u32[]{:S(2)}) collective-permute-start(bf16[80,1920]{1,0:T(8,128)(2,1)S(1)} %bitcast.63), channel_id=1, source_target_pairs={{0,24},{2,26},{4,28},{6,30},{8,0},{10,2},{12,4},{14,6},{16,8},{18,... | collective-permute-start | bytes 921608 | tf_op jit(solution)/shard_map/ppermute | solution.py:571
  39.4 29.0 %collective-permute-start.4 = (bf16[4,80,1920]{2,1,0:T(8,128)(2,1)S(1)}, bf16[4,80,1920]{2,1,0:T(8,128)(2,1)S(1)}, u32[]{:S(2)}, u32[]{:S(2)}) collective-permute-start(bf16[4,80,1920]{2,1,0:T(8,128)(2,1)S(1)} %pad_maximum_fusion.1.refs_1_), channel_id=1, source_target_pairs={{0,2},{2,0},{4,6},{6,4},{8,10},{10,8},{12,14},{14,12},{16,18},{18,... | collective-permute-start | bytes 3686408 | tf_op jit(solution)/shard_map/ppermute | solution.py:571
  40.9 28.7 %collective-permute-start.5 = (bf16[4,80,1920]{2,1,0:T(8,128)(2,1)S(1)}, bf16[4,80,1920]{2,1,0:T(8,128)(2,1)S(1)}, u32[]{:S(2)}, u32[]{:S(2)}) collective-permute-start(bf16[4,80,1920]{2,1,0:T(8,128)(2,1)S(1)} %pad_maximum_fusion.1.refs_1_), channel_id=1, source_target_pairs={{0,4},{2,6},{4,0},{6,2},{8,12},{10,14},{12,8},{14,10},{16,20},{18,... | collective-permute-start | bytes 3686408 | tf_op jit(solution)/shard_map/ppermute | solution.py:571
  42.5 29.3 %collective-permute-start.8 = (bf16[80,3200]{1,0:T(8,128)(2,1)S(1)}, bf16[80,3200]{1,0:T(8,128)(2,1)S(1)}, u32[]{:S(2)}, u32[]{:S(2)}) collective-permute-start(bf16[80,3200]{1,0:T(8,128)(2,1)S(1)} %pad_maximum_fusion.4), channel_id=1, source_target_pairs={{0,8},{2,10},{4,12},{6,14},{8,16},{10,18},{12,20},{14,22},{16,24},... | collective-permute-start | bytes 1536008 | tf_op jit(solution)/shard_map/ppermute | solution.py:571
  42.5 43.7 %collective-permute-start.9 = (bf16[80,3200]{1,0:T(8,128)(2,1)S(1)}, bf16[80,3200]{1,0:T(8,128)(2,1)S(1)}, u32[]{:S(2)}, u32[]{:S(2)}) collective-permute-start(bf16[80,3200]{1,0:T(8,128)(2,1)S(1)} %pad_maximum_fusion.4), channel_id=1, source_target_pairs={{0,16},{2,18},{4,20},{6,22},{8,24},{10,26},{12,28},{14,30},{16,0},... | collective-permute-start | bytes 1536008 | tf_op jit(solution)/shard_map/ppermute | solution.py:571
  44.1 43.1 %collective-permute-start.10 = (bf16[80,3200]{1,0:T(8,128)(2,1)S(1)}, bf16[80,3200]{1,0:T(8,128)(2,1)S(1)}, u32[]{:S(2)}, u32[]{:S(2)}) collective-permute-start(bf16[80,3200]{1,0:T(8,128)(2,1)S(1)} %pad_maximum_fusion.4), channel_id=1, source_target_pairs={{0,24},{2,26},{4,28},{6,30},{8,0},{10,2},{12,4},{14,6},{16,8},{18,... | collective-permute-start | bytes 1536008 | tf_op jit(solution)/shard_map/ppermute | solution.py:571
  89.7 49.3 %collective-permute-start.11 = (bf16[4,80,3200]{2,1,0:T(8,128)(2,1)}, bf16[4,80,3200]{2,1,0:T(8,128)(2,1)}, u32[]{:S(2)}, u32[]{:S(2)}) collective-permute-start(bf16[4,80,3200]{2,1,0:T(8,128)(2,1)} %pad_maximum_fusion.refs_1_), channel_id=1, source_target_pairs={{0,2},{2,0},{4,6},{6,4},{8,10},{10,8},{12,14},{14,12},{16,18},{18,... | collective-permute-start | bytes 6144008 | tf_op jit(solution)/shard_map/ppermute | solution.py:571
  90.2 48.8 %collective-permute-start.12 = (bf16[4,80,3200]{2,1,0:T(8,128)(2,1)}, bf16[4,80,3200]{2,1,0:T(8,128)(2,1)}, u32[]{:S(2)}, u32[]{:S(2)}) collective-permute-start(bf16[4,80,3200]{2,1,0:T(8,128)(2,1)} %pad_maximum_fusion.refs_1_), channel_id=1, source_target_pairs={{0,4},{2,6},{4,0},{6,2},{8,12},{10,14},{12,8},{14,10},{16,20},{18,... | collective-permute-start | bytes 6144008 | tf_op jit(solution)/shard_map/ppermute | solution.py:571
  139.1 362.8 %reduce-scatter.2.cloned.1.call-start = ((), (), s32[]{:S(2)}) async-start(), calls=%async_computation.2 | async-start | bytes 1740800 | tf_op jit(solution)/shard_map/reduce_scatter | solution.py:802
  141.4 28.8 %collective-permute-start.14 = (bf16[2,80,3200]{2,1,0:T(8,128)(2,1)}, bf16[2,80,3200]{2,1,0:T(8,128)(2,1)S(1)}, u32[]{:S(2)}, u32[]{:S(2)}) collective-permute-start(bf16[2,80,3200]{2,1,0:T(8,128)(2,1)} %slice.158), channel_id=1, source_target_pairs={{0,4},{2,6},{4,0},{6,2},{8,12},{10,14},{12,8},{14,10},{16,20},{18,... | collective-permute-start | bytes 3072008 | tf_op jit(solution)/shard_map/ppermute | solution.py:571
  145.1 27.0 %collective-permute-start.15 = (bf16[2,80,3200]{2,1,0:T(8,128)(2,1)}, bf16[2,80,3200]{2,1,0:T(8,128)(2,1)}, u32[]{:S(2)}, u32[]{:S(2)}) collective-permute-start(bf16[2,80,3200]{2,1,0:T(8,128)(2,1)} %slice.159), channel_id=1, source_target_pairs={{0,2},{2,0},{4,6},{6,4},{8,10},{10,8},{12,14},{14,12},{16,18},{18,... | collective-permute-start | bytes 3072008 | tf_op jit(solution)/shard_map/ppermute | solution.py:571
  196.4 29.4 %collective-permute-start.13 = (bf16[1024,1280]{1,0:T(8,128)(2,1)}, bf16[1024,1280]{1,0:T(8,128)(2,1)}, u32[]{:S(2)}, u32[]{:S(2)}) collective-permute-start(bf16[1024,1280]{1,0:T(8,128)(2,1)} %refs_5_.1), channel_id=1, source_target_pairs={{0,1},{1,0},{2,3},{3,2},{4,5},{5,4},{6,7},{7,6},{8,9},{9,8},{10,11... | collective-permute-start | bytes 7864328 | tf_op jit(solution)/shard_map/ppermute | solution.py:571
  245.8 39.7 %collective-permute-start.18 = (bf16[4,80,2560]{2,1,0:T(8,128)(2,1)}, bf16[4,80,2560]{2,1,0:T(8,128)(2,1)}, u32[]{:S(2)}, u32[]{:S(2)}) collective-permute-start(bf16[4,80,2560]{2,1,0:T(8,128)(2,1)} %get-tuple-element.172), channel_id=1, source_target_pairs={{0,2},{2,0},{4,6},{6,4},{8,10},{10,8},{12,14},{14,12},{16,18},{18,... | collective-permute-start | bytes 4915208 | tf_op jit(solution)/shard_map/ppermute | solution.py:571
  247.5 38.1 %collective-permute-start.19 = (bf16[4,80,2560]{2,1,0:T(8,128)(2,1)}, bf16[4,80,2560]{2,1,0:T(8,128)(2,1)}, u32[]{:S(2)}, u32[]{:S(2)}) collective-permute-start(bf16[4,80,2560]{2,1,0:T(8,128)(2,1)} %get-tuple-element.173), channel_id=1, source_target_pairs={{0,4},{2,6},{4,0},{6,2},{8,12},{10,14},{12,8},{14,10},{16,20},{18,... | collective-permute-start | bytes 4915208 | tf_op jit(solution)/shard_map/ppermute | solution.py:571
  285.6 27.1 %collective-permute-start.22 = (bf16[1024,1280]{1,0:T(8,128)(2,1)}, bf16[1024,1280]{1,0:T(8,128)(2,1)}, u32[]{:S(2)}, u32[]{:S(2)}) collective-permute-start(bf16[1024,1280]{1,0:T(8,128)(2,1)} %product_for_other.5), channel_id=1, source_target_pairs={{0,1},{1,0},{2,3},{3,2},{4,5},{5,4},{6,7},{7,6},{8,9},{9,8},{10,11... | collective-permute-start | bytes 7864328 | tf_op jit(solution)/shard_map/ppermute | solution.py:571
  325.2 38.5 %collective-permute-start.23 = (bf16[4,80,2560]{2,1,0:T(8,128)(2,1)}, bf16[4,80,2560]{2,1,0:T(8,128)(2,1)}, u32[]{:S(2)}, u32[]{:S(2)}) collective-permute-start(bf16[4,80,2560]{2,1,0:T(8,128)(2,1)} %get-tuple-element.190), channel_id=1, source_target_pairs={{0,2},{2,0},{4,6},{6,4},{8,10},{10,8},{12,14},{14,12},{16,18},{18,... | collective-permute-start | bytes 4915208 | tf_op jit(solution)/shard_map/ppermute | solution.py:571
  326.7 38.2 %collective-permute-start.24 = (bf16[4,80,2560]{2,1,0:T(8,128)(2,1)}, bf16[4,80,2560]{2,1,0:T(8,128)(2,1)}, u32[]{:S(2)}, u32[]{:S(2)}) collective-permute-start(bf16[4,80,2560]{2,1,0:T(8,128)(2,1)} %get-tuple-element.191), channel_id=1, source_target_pairs={{0,4},{2,6},{4,0},{6,2},{8,12},{10,14},{12,8},{14,10},{16,20},{18,... | collective-permute-start | bytes 4915208 | tf_op jit(solution)/shard_map/ppermute | solution.py:571
  400.3 99.2 %collective-permute-start.30 = (bf16[80,5120]{1,0:T(8,128)(2,1)}, bf16[80,5120]{1,0:T(8,128)(2,1)}, u32[]{:S(2)}, u32[]{:S(2)}) collective-permute-start(bf16[80,5120]{1,0:T(8,128)(2,1)} %get-tuple-element.305), channel_id=1, source_target_pairs={{0,16},{2,18},{4,20},{6,22},{8,24},{10,26},{12,28},{14,30},{16,0},... | collective-permute-start | bytes 2457608 | tf_op jit(solution)/shard_map/ppermute | solution.py:571
  401.5 98.0 %collective-permute-start.31 = (bf16[80,5120]{1,0:T(8,128)(2,1)}, bf16[80,5120]{1,0:T(8,128)(2,1)}, u32[]{:S(2)}, u32[]{:S(2)}) collective-permute-start(bf16[80,5120]{1,0:T(8,128)(2,1)} %get-tuple-element.304), channel_id=1, source_target_pairs={{0,24},{2,26},{4,28},{6,30},{8,0},{10,2},{12,4},{14,6},{16,8},{18,... | collective-permute-start | bytes 2457608 | tf_op jit(solution)/shard_map/ppermute | solution.py:571
  402.6 96.9 %collective-permute-start.29 = (bf16[80,5120]{1,0:T(8,128)(2,1)}, bf16[80,5120]{1,0:T(8,128)(2,1)}, u32[]{:S(2)}, u32[]{:S(2)}) collective-permute-start(bf16[80,5120]{1,0:T(8,128)(2,1)} %get-tuple-element.303), channel_id=1, source_target_pairs={{0,8},{2,10},{4,12},{6,14},{8,16},{10,18},{12,20},{14,22},{16,24},... | collective-permute-start | bytes 2457608 | tf_op jit(solution)/shard_map/ppermute | solution.py:571
  535.1 29.8 %collective-permute-start.32 = (bf16[4,80,1920]{2,1,0:T(8,128)(2,1)}, bf16[4,80,1920]{2,1,0:T(8,128)(2,1)}, u32[]{:S(2)}, u32[]{:S(2)}) collective-permute-start(bf16[4,80,1920]{2,1,0:T(8,128)(2,1)} %get-tuple-element.220), channel_id=1, source_target_pairs={{0,2},{2,0},{4,6},{6,4},{8,10},{10,8},{12,14},{14,12},{16,18},{18,... | collective-permute-start | bytes 3686408 | tf_op jit(solution)/shard_map/ppermute | solution.py:571
  535.2 29.8 %collective-permute-start.33 = (bf16[4,80,1920]{2,1,0:T(8,128)(2,1)}, bf16[4,80,1920]{2,1,0:T(8,128)(2,1)}, u32[]{:S(2)}, u32[]{:S(2)}) collective-permute-start(bf16[4,80,1920]{2,1,0:T(8,128)(2,1)} %get-tuple-element.221), channel_id=1, source_target_pairs={{0,4},{2,6},{4,0},{6,2},{8,12},{10,14},{12,8},{14,10},{16,20},{18,... | collective-permute-start | bytes 3686408 | tf_op jit(solution)/shard_map/ppermute | solution.py:571
  (74 other events, 658.8 us)
Sparse Core Ops, SparseCore 0:
  139.2 99.3 all-gather.1
  392.6 109.2 reduce-scatter.1
